TPU v7x, 32 devices: a whole 2x2x4 slice. The times are simulated.
32 devices in a mesh: site: 8 (over z, y), branch: 4 (over x, core).
Axes of the slice: x: 2, y: 2, z: 4, core: 2. Of those that a mesh axis runs over, the one named last changes fastest.
Arguments:
- states: int32 [256, 2048], P(None, 'site'), may hold values from 0 to 63, as said below
- gap_mask: int32 [256, 2048], P(None, 'site'), may hold values 0 or 1
- weights: int32 [2048], P('site'), may hold values from 1 to 9
- leaf_order: int32 [256], replicated, may hold values from 0 to 255, each once
- exchanges: float32 [64, 64], replicated, may hold values from 0.3 to 3
- codon_freq: float32 [64], replicated, may hold values from 0.3 to 3
- omega_ratio: float32 [8], replicated, may hold values from 0.1 to 2
- lengths: float32 [508], P('branch'), may hold values from 0.05 to 1.5
- classes: int32 [508], P('branch'), may hold values from 0 to 7
Outputs:
- grad_exch: float32 [64, 64], replicated
- grad_omega: float32 [8], replicated
- grad_length: float32 [508], P('branch')
- loglik: float32 [], replicated
Inputs may be any that keep to these rules, and one draw needn't show every extreme that they name: `states`: every state is a sense codon: never 10, 11 or 14.
All inputs are finite; a program needn't handle non-finite values. No bound on the sum of `gap_mask` on one device may be relied on, other than what follows from the above.
Results may differ from a plain program's by a relative error of at most 0.0003.
Values sent between devices are 32-bit elements; how exact they have to be, the bound alone decides.
No kernel may reach another device: no remote copies, remote signals or barrier semaphores. Data moves between devices by JAX's collectives and lax.ppermute only.
A program may use at most 192 MiB of HBM per device.

v0:
```python
import functools
import jax
import jax.numpy as jnp
import numpy as np
from jax import lax
from jax.experimental import pallas as pl
from jax.experimental.pallas import tpu as pltpu
from jax.sharding import PartitionSpec as P

LEAF_DEV = 64
EDGES = 127
PAIRS = 64
CLASSES = 8
ORDER = 8
BF = jnp.bfloat16
F32 = jnp.float32

CODE_TABLE = "FFLLSSSSYYXXCCXWLLLLPPPPHHQQRRRRIIIMTTTTNNKKSSRRVVVVAAAADDEEGGGG"


def codon_tables():
    amino_acid = np.array(list(CODE_TABLE))
    codon_index = np.arange(64)
    digits = np.stack([codon_index // 16, codon_index // 4 % 4, codon_index % 4], 1)
    differ = (digits[:, None, :] != digits[None, :, :]).sum(-1)
    is_sense = amino_acid != "X"
    single = (differ == 1) & is_sense[:, None] & is_sense[None, :]
    nonsyn = single & (amino_acid[:, None] != amino_acid[None, :])
    return (is_sense.astype(np.float32), single.astype(np.float32), nonsyn.astype(np.float32))


def low_half():
    return lax.broadcasted_iota(jnp.int32, (64, 128), 1) < 64


def split(x):
    high = x.astype(BF)
    low = (x - high.astype(F32)).astype(BF)
    return high, low


def spread(x, scale=1.0):
    mask = low_half()
    low = jnp.where(mask, scale, 0.0).astype(x.dtype)
    high = jnp.where(mask, 0.0, scale).astype(x.dtype)
    return jnp.concatenate([x * low, x * high], axis=0)


def mxu(left, right):
    return jnp.dot(left, right, preferred_element_type=F32)


def mxu_nt(left, right):
    return lax.dot_general(left, right, (((1,), (1,)), ((), ())), preferred_element_type=F32)


def exact(left, right):
    return jnp.dot(left, right, preferred_element_type=F32, precision=lax.Precision.HIGHEST)


def exact_tn(left, right):
    return lax.dot_general(
        left, right, (((0,), (0,)), ((), ())), preferred_element_type=F32,
        precision=lax.Precision.HIGHEST,
    )


def pair_products(*terms):
    lefts, rights = [], []
    for left, right in terms:
        left_high, left_low = split(left)
        right_high, right_low = split(right)
        wide_high, wide_low = spread(right_high), spread(right_low)
        lefts += [left_high, left_high, left_low]
        rights += [wide_high, wide_low, wide_high]
    return mxu(jnp.concatenate(lefts, axis=1), jnp.concatenate(rights, axis=0))


def messages(matrix, high, low):
    return mxu(matrix, jnp.concatenate([high, low, high, low], axis=0))


def double(ref, p, x):
    mask = low_half()
    swapped = pltpu.roll(x, 64, 1)
    for e, both in enumerate((jnp.where(mask, x, swapped), jnp.where(mask, swapped, x))):
        high, low = split(both)
        ref[2 * p + e] = jnp.concatenate([high, low], axis=1)


def transposes(first, second):
    mask = low_half()
    turned = jnp.concatenate([first, second], axis=0).T
    top, bottom = turned[0:64], turned[64:128]
    return (
        jnp.where(mask, top, pltpu.roll(bottom, 64, 1)),
        jnp.where(mask, pltpu.roll(top, 64, 1), bottom),
    )


def frequencies(freq_ref, sense_ref):
    row = lax.broadcasted_iota(jnp.int32, (64, 128), 0)
    lane = lax.broadcasted_iota(jnp.int32, (64, 128), 1)
    twice = (row == lane % 64).astype(F32)
    sense2 = sense_ref[...]
    freq2 = exact(jnp.broadcast_to(freq_ref[...], (8, 64)), twice)[0:1] * sense2
    total = 0.5 * jnp.sum(freq2, axis=1, keepdims=True)
    pi_row = freq2 / total
    pi_col = 0.5 * jnp.sum(twice * pi_row, axis=1, keepdims=True)
    sense_col = 0.5 * jnp.sum(twice * sense2, axis=1, keepdims=True)
    root_row = jnp.sqrt(jnp.where(sense2 > 0, pi_row, 1.0))
    root_col = jnp.sqrt(jnp.where(sense_col > 0, pi_col, 1.0))
    return twice, pi_row, pi_col, root_row, root_col


def symmetric_table(ex_ref, single_ref, twice):
    ex = ex_ref[...]
    return 0.5 * (exact(ex, twice) + exact_tn(ex, twice)) * single_ref[...]


def class_pair(table, nonsyn, omega_ref, pair, twice, pi_row, pi_col):
    mask = low_half()
    omega = jnp.where(mask, omega_ref[2 * pair], omega_ref[2 * pair + 1])
    factor = 1.0 + nonsyn * (omega - 1.0)
    flux = table * factor
    off = flux * pi_row
    row0 = jnp.sum(jnp.where(mask, off, 0.0), axis=1, keepdims=True)
    row1 = jnp.sum(jnp.where(mask, 0.0, off), axis=1, keepdims=True)
    mean0 = jnp.sum(pi_col * row0, axis=0, keepdims=True)
    mean1 = jnp.sum(pi_col * row1, axis=0, keepdims=True)
    rows = jnp.where(mask, row0, row1)
    mean = jnp.where(mask, mean0, mean1)
    return factor, off, rows, mean


def neighbours():
    row = lax.broadcasted_iota(jnp.int32, (64, 128), 0)
    lane = lax.broadcasted_iota(jnp.int32, (64, 128), 1) % 64
    masks = [
        row % 16 == lane % 16,
        (row // 16 == lane // 16) & (row % 4 == lane % 4),
        row // 4 == lane // 4,
    ]
    codon = lax.broadcasted_iota(jnp.int32, (64, 16), 0)
    column = lax.broadcasted_iota(jnp.int32, (64, 16), 1)
    digits = [codon // 16, codon // 4 % 4, codon % 4]
    picks = [(column == 4 * p + digits[p]).astype(F32) for p in range(3)]
    return masks, picks


def coefficients(len_ref, cls_ref, slope):
    lane = lax.broadcasted_iota(jnp.int32, (PAIRS, EDGES), 1)
    row = lax.broadcasted_iota(jnp.int32, (PAIRS, EDGES), 0)
    lengths = len_ref[...] * 0.0625
    classes = cls_ref[...].astype(F32)
    place = lax.broadcasted_iota(jnp.int32, (PAIRS, 128), 1) % 64
    found = []
    for odd in range(2):
        here = lane == 2 * row + odd
        y = jnp.sum(jnp.where(here, lengths, 0.0), axis=1, keepdims=True)
        owner = jnp.sum(jnp.where(here, classes, 0.0), axis=1, keepdims=True)
        current = jnp.ones((PAIRS, 128), F32)
        series = jnp.zeros((PAIRS, 128), F32)
        for k in range(ORDER):
            following = current * y * (1.0 / (k + 1))
            series = jnp.where(place // CLASSES == k, current if slope else following, series)
            current = following
        found.append(jnp.where((place % CLASSES).astype(F32) == owner, series, 0.0))
    return found


def four_left(x):
    high, low = split(x)
    return jnp.concatenate([high, low], axis=1)


def four_right(x):
    high, low = split(x)
    return jnp.concatenate([high, low, high, low], axis=0)


def expand(left, dup_ref, store):
    mask = low_half()

    def some(step, carry):
        for j in range(2):
            i = step * 4 + 2 * j
            rows = jnp.concatenate(
                [dup_ref[rows_of(i, 64), :], dup_ref[rows_of(i + 1, 64), :]], axis=1
            )
            both = mxu(left, four_right(rows))
            for t in range(2):
                even, odd = both[0:64, 128 * t : 128 * t + 128], both[64:128, 128 * t : 128 * t + 128]
                store(i + t, jnp.where(mask, even, pltpu.roll(odd, 64, 1)))
                store(i + t + 32, jnp.where(mask, pltpu.roll(even, 64, 1), odd))
        return carry

    lax.fori_loop(0, 8, some, 0)


def rows_of(step, width):
    return pl.ds(pl.multiple_of(step * width, width), width)


def matrix_kernel(
    ex_ref, freq_ref, omega_ref, len_ref, cls_ref, sense_ref, single_ref, nonsyn_ref,
    chain_ref, last_ref, up_ref, power_ref, dup_ref,
    first_ref,
):
    mask = low_half()
    twice, pi_row, pi_col, root_row, root_col = frequencies(freq_ref, sense_ref)
    table = symmetric_table(ex_ref, single_ref, twice)
    nonsyn = nonsyn_ref[...]

    powers = []
    for pair in range(CLASSES // 2):
        factor, off, rows, mean = class_pair(
            table, nonsyn, omega_ref, pair, twice, pi_row, pi_col
        )
        powers.append([(table * factor * root_col * root_row - twice * rows) / mean])
    for left, right in ((0, 0), (1, 0), (1, 1), (3, 0), (3, 1), (3, 2), (3, 3)):
        for pair in range(CLASSES // 2):
            powers[pair].append(pair_products((powers[pair][left], powers[pair][right])))
    for pair in range(CLASSES // 2):
        for k in range(ORDER):
            value = powers[pair][k]
            swapped = pltpu.roll(value, 64, 1)
            at = CLASSES * k + 2 * pair
            top, half = value[0:32], low_half()[0:32]
            dup_ref[pl.ds(at, 32, stride=64), :] = jnp.where(half, top, swapped[32:64])
            dup_ref[pl.ds(at + 1, 32, stride=64), :] = jnp.where(half, swapped[0:32], value[32:64])
            if k < 4:
                power_ref[pair, k] = value

    even, odd = coefficients(len_ref, cls_ref, False)

    def store(i, value):
        first_ref[rows_of(i, 64), :] = value

    expand(four_left(jnp.concatenate([even, odd], axis=0)), dup_ref, store)

    def squarings(step, carry):
        held = [first_ref[pl.ds(step * 8 + j, 64, stride=64), :] for j in range(8)]
        for level in range(4):
            parts = []
            for j in range(8):
                high, low = split(held[j])
                chain_ref[level, 0, step * 8 + j] = high
                chain_ref[level, 1, step * 8 + j] = low
                parts.append(mxu(
                    jnp.concatenate([high, high], axis=1),
                    jnp.concatenate([spread(high, 0.5), spread(low)], axis=0),
                ))
            for j in range(0, 8, 2):
                turned = transposes(parts[j], parts[j + 1])
                for t in range(2):
                    held[j + t] = 2.0 * held[j + t] + parts[j + t] + turned[t]
        for j in range(8):
            p = step * 8 + j
            last_ref[p] = held[j]
            double(up_ref, p, inverse_root_col * (held[j] + twice) * root_row)
        return carry

    inverse_root_col = 1.0 / root_col
    lax.fori_loop(0, PAIRS // 8, squarings, 0)


def up_kernel(
    states_ref, gap_ref, order_ref, up_ref,
    top_ref, message_ref, high_ref, low_ref, leaf_ref, scale_ref, inverse_ref,
):
    subtree = lax.axis_index("branch")

    def finish(p, message):
        message_ref[p] = jnp.concatenate(message, axis=0)
        raw = message[0] * message[1]
        scaling = jnp.sum(raw, axis=0, keepdims=True)
        inverse = 1.0 / scaling
        scale_ref[pl.ds(p, 1), :] = scaling
        inverse_ref[pl.ds(p, 1), :] = inverse
        high, low = split(raw * inverse)
        high_ref[p] = high
        low_ref[p] = low

    sites = states_ref.shape[1]
    codon = lax.broadcasted_iota(jnp.int32, (64, sites), 0)

    def leaf_level(step, carry):
        for j in range(4):
            p = step * 4 + j
            both = []
            for e in range(2):
                taxon = order_ref[subtree * LEAF_DEV + 2 * p + e]
                state = jnp.where(
                    gap_ref[pl.ds(taxon, 1), :] > 0, -1, states_ref[pl.ds(taxon, 1), :]
                )
                hit = (codon == state) | (state < 0)
                both.append(jnp.where(hit, 1.0, 0.0).astype(BF))
            leaf_ref[p] = jnp.concatenate(both, axis=0)
            nothing = jnp.zeros_like(both[0])
            finish(p, [messages(up_ref[2 * p + e], both[e], nothing) for e in range(2)])
        return carry

    lax.fori_loop(0, LEAF_DEV // 8, leaf_level, 0)

    def inner(p):
        child = 2 * p - 64
        return [
            messages(up_ref[2 * p + e], high_ref[child + e], low_ref[child + e]) for e in range(2)
        ]

    def second_level(step, carry):
        for j in range(4):
            finish(32 + step * 4 + j, inner(32 + step * 4 + j))
        return carry

    lax.fori_loop(0, 4, second_level, 0)
    for p in range(48, 63):
        finish(p, inner(p))
    high_ref[63] = jnp.zeros((64, sites), BF)
    low_ref[63] = jnp.zeros((64, sites), BF)
    scale_ref[63:64, :] = jnp.ones((1, sites), F32)
    inverse_ref[63:64, :] = jnp.ones((1, sites), F32)
    top = inner(63)
    message_ref[63] = jnp.concatenate(top, axis=0)
    top_ref[...] = top[0]


def side_kernel(
    dup_ref, last_ref, len_ref, cls_ref, freq_ref, sense_ref, slope_ref, matrix_ref, turned_ref,
):
    twice, pi_row, pi_col, root_row, root_col = frequencies(freq_ref, sense_ref)
    even, odd = coefficients(len_ref, cls_ref, True)

    def store(i, value):
        slope_ref[rows_of(i, 64), :] = value

    expand(four_left(jnp.concatenate([even, odd], axis=0)), dup_ref, store)
    even, odd = coefficients(len_ref, cls_ref, False)
    turned_ref[...] = exact_tn(jnp.where(low_half(), even, odd), twice)
    inverse_root_row = 1.0 / root_row

    def matrices(step, carry):
        for j in range(8):
            r = step * 8 + j
            double(matrix_ref, r, root_col * (last_ref[32 + r] + twice) * inverse_root_row)
        return carry

    lax.fori_loop(0, 4, matrices, 0)


def down_kernel(total_sites, members, *refs):
    tops = refs[:members]
    (
        matrix_ref, message_ref, high_ref, low_ref, leaf_ref, scale_ref, inverse_ref,
        weights_ref, freq_ref, sense_ref,
        count_ref, log_ref,
        a_high_ref, a_low_ref,
    ) = refs[members:]
    subtree = lax.axis_index("branch")
    mask = low_half()
    twice, pi_row, pi_col, root_row, root_col = frequencies(freq_ref, sense_ref)
    inverse_root_row, inverse_root_col = 1.0 / root_row, 1.0 / root_col
    sites = weights_ref.shape[1]
    weight = weights_ref[...].astype(F32)

    above = jnp.broadcast_to(pi_col, (64, sites))
    for other in tops[1:]:
        above = above * other[...]
    own = tops[0][...]
    likelihood = jnp.sum(above * own, axis=0, keepdims=True)
    logs = jnp.sum(jnp.log(scale_ref[...]), axis=0, keepdims=True)
    logs = logs + jnp.where(subtree == 0, jnp.log(likelihood), 0.0)
    log_ref[...] = jnp.broadcast_to(jnp.sum(weight * logs, axis=1, keepdims=True), (8, 128))
    high, low = split(above * (weight / (likelihood * total_sites)))
    a_high_ref[31, 0:64, :] = high
    a_low_ref[31, 0:64, :] = low
    a_high_ref[31, 64:128, :] = jnp.zeros((64, sites), BF)
    a_low_ref[31, 64:128, :] = jnp.zeros((64, sites), BF)

    def store_counts(p, square):
        counts = jnp.where(mask, square[0:64], square[64:128])
        count_ref[p] = root_col * counts * inverse_root_row

    def descend(r):
        a_high, a_low = a_high_ref[r - 32], a_low_ref[r - 32]
        child = 2 * r - 64
        u_high = jnp.concatenate([high_ref[child], high_ref[child + 1]], axis=0)
        u_low = jnp.concatenate([low_ref[child], low_ref[child + 1]], axis=0)
        first = mxu_nt(u_high, jnp.concatenate([a_high, a_low], axis=0))
        second = mxu_nt(u_low, a_high)
        store_counts(r, first[:, 0:128] + first[:, 128:256] + second)
        return [
            messages(
                matrix_ref[2 * (r - 32) + e], a_high[64 * e : 64 * e + 64], a_low[64 * e : 64 * e + 64]
            )
            for e in range(2)
        ]

    def children(down, e, p):
        vector = down[e]
        inverse = inverse_ref[pl.ds(p, 1), :]
        message = message_ref[p]
        pair = jnp.concatenate(
            [vector * message[64:128] * inverse, vector * message[0:64] * inverse], axis=0
        )
        return split(pair)

    def inner(r):
        down = descend(r)
        for e in range(2):
            p = 2 * r + e - 64
            if isinstance(p, int) and p == 63:
                continue
            high, low = children(down, e, p)
            a_high_ref[p - 32] = high
            a_low_ref[p - 32] = low

    for r in range(63, 47, -1):
        inner(r)

    def leaf_level(step, carry):
        for j in range(2):
            r = 32 + step * 2 + j
            down = descend(r)
            for e in range(2):
                p = 2 * r + e - 64
                high, low = children(down, e, p)
                square = mxu_nt(leaf_ref[p], jnp.concatenate([high, low], axis=0))
                store_counts(p, square[:, 0:128] + square[:, 128:256])
        return carry

    lax.fori_loop(0, 8, leaf_level, 0)


def adjoint_kernel(
    members,
    chain_ref, turned_ref, slope_ref, power_ref, count_ref, log_ref, ex_ref, freq_ref, omega_ref,
    sense_ref, single_ref, nonsyn_ref,
    out_ref,
    back_ref, bins_ref,
):
    subtree = lax.axis_index("branch")
    mask = low_half()
    twice, pi_row, pi_col, root_row, root_col = frequencies(freq_ref, sense_ref)
    inverse_root_row = 1.0 / root_row

    def adjoint(step, carry):
        held = []
        for j in range(0, 8, 2):
            here = [count_ref[step * 8 + j + t] for t in range(2)]
            turned = transposes(*here)
            held += [0.5 * (here[t] + turned[t]) for t in range(2)]
        zero = jnp.zeros((128, 128), BF)
        for level in range(3, -1, -1):
            for j in range(0, 8, 2):
                parts, highs, lows = [], [], []
                for t in range(2):
                    high, low = split(held[j + t])
                    wide = spread(chain_ref[level, 0, step * 8 + j + t])
                    lows.append(spread(chain_ref[level, 1, step * 8 + j + t]))
                    highs.append(high)
                    parts.append(mxu(
                        jnp.concatenate([high, low], axis=1),
                        jnp.concatenate([wide, wide], axis=0),
                    ))
                rest = mxu(
                    jnp.concatenate(highs, axis=1),
                    jnp.concatenate([
                        jnp.concatenate([lows[0], zero], axis=1),
                        jnp.concatenate([zero, lows[1]], axis=1),
                    ], axis=0),
                )
                parts = [parts[t] + rest[:, 128 * t : 128 * t + 128] for t in range(2)]
                turned = transposes(*parts)
                for t in range(2):
                    held[j + t] = 2.0 * held[j + t] + parts[t] + turned[t]
        for j in range(8):
            back_ref[pl.ds(step * 8 + j, 64, stride=64), :] = held[j]
        return carry

    lax.fori_loop(0, PAIRS // 8, adjoint, 0)

    left = four_left(turned_ref[...])

    def sums(step, total):
        for j in range(4):
            ats = [rows_of(step * 8 + 2 * j + t, 64) for t in range(2)]
            values = [back_ref[at, :] for at in ats]
            both = mxu(left, four_right(jnp.concatenate(values, axis=1)))
            for t in range(2):
                total = total + values[t] * slope_ref[ats[t], :]
                here = both[:, 128 * t : 128 * t + 128]
                bins_ref[ats[t], :] = jnp.where(mask, here[0:64], here[64:128])
        return total

    slopes = lax.fori_loop(0, 8, sums, jnp.zeros((64, 128), F32)) * 0.0625

    table = symmetric_table(ex_ref, single_ref, twice)
    nonsyn = nonsyn_ref[...]
    row = lax.broadcasted_iota(jnp.int32, (64, 128), 0)
    lane = lax.broadcasted_iota(jnp.int32, (64, 128), 1)
    table_grad = jnp.zeros((64, 128), F32)
    omega_row = jnp.zeros((1, 128), F32)
    lane_row = lax.broadcasted_iota(jnp.int32, (1, 128), 1)
    for pair in range(CLASSES // 2):
        grads = []
        for k in range(ORDER):
            at = CLASSES * k + 2 * pair
            first = bins_ref[pl.ds(at, 64, stride=64), :]
            second = bins_ref[pl.ds(at + 1, 64, stride=64), :]
            first = first + pltpu.roll(first, 64, 1)
            second = second + pltpu.roll(second, 64, 1)
            grads.append(jnp.where(mask, first, second))
        g1, g2, g3, g4, g5, g6, g7, g8 = grads
        a1, a2, a3, a4 = [power_ref[pair, k] for k in range(4)]
        g4 = g4 + pair_products((g8, a4), (a4, g8), (g7, a3), (g6, a2), (g5, a1))
        g3 = g3 + pair_products((a4, g7))
        g2 = g2 + pair_products((a4, g6))
        g1 = g1 + pair_products((a4, g5))
        g2 = g2 + pair_products((g4, a2), (a2, g4), (g3, a1))
        g1 = g1 + pair_products((a2, g3))
        g1 = g1 + pair_products((g2, a1), (a1, g2))
        factor, off, rows, mean = class_pair(
            table, nonsyn, omega_ref, pair, twice, pi_row, pi_col
        )
        d_rate = root_col * g1 * inverse_root_row
        rate = (off - twice * rows) / mean
        weighted = d_rate * rate
        diagonal = d_rate * twice
        total0 = jnp.sum(jnp.where(mask, weighted, 0.0), axis=1, keepdims=True)
        total1 = jnp.sum(jnp.where(mask, 0.0, weighted), axis=1, keepdims=True)
        total0 = jnp.sum(total0, axis=0, keepdims=True)
        total1 = jnp.sum(total1, axis=0, keepdims=True)
        diag0 = jnp.sum(jnp.where(mask, diagonal, 0.0), axis=1, keepdims=True)
        diag1 = jnp.sum(jnp.where(mask, 0.0, diagonal), axis=1, keepdims=True)
        row_grad = jnp.where(mask, diag0 + pi_col * total0, diag1 + pi_col * total1)
        flux_grad = (d_rate - row_grad) * pi_row / mean
        table_grad = table_grad + flux_grad * factor * single_ref[...]
        ratio = flux_grad * table * nonsyn
        ratio0 = jnp.sum(jnp.where(mask, ratio, 0.0), axis=1, keepdims=True)
        ratio1 = jnp.sum(jnp.where(mask, 0.0, ratio), axis=1, keepdims=True)
        ratio0 = jnp.sum(ratio0, axis=0, keepdims=True)
        ratio1 = jnp.sum(ratio1, axis=0, keepdims=True)
        omega_row = jnp.where(lane_row == 2 * pair, ratio0, omega_row)
        omega_row = jnp.where(lane_row == 2 * pair + 1, ratio1, omega_row)
    table_grad = table_grad + pltpu.roll(table_grad, 64, 1)
    one = table_grad[:, 0:64]
    both = 0.5 * (exact(one, twice) + exact_tn(one, twice))
    masks, picks = neighbours()
    packed = jnp.zeros((16, 128), F32)
    for at_position, pick in zip(masks, picks):
        packed = packed + exact_tn(pick, jnp.where(at_position, both, 0.0))
    packed = jnp.where(lax.broadcasted_iota(jnp.int32, (16, 128), 1) < 64, packed, 0.0)

    even = jnp.sum(jnp.where(mask, slopes, 0.0), axis=1, keepdims=True)
    other = jnp.sum(jnp.where(mask, 0.0, slopes), axis=1, keepdims=True)
    placed = jnp.where(lane == 2 * row, even, 0.0) + jnp.where(lane == 2 * row + 1, other, 0.0)
    length_row = jnp.sum(placed, axis=0, keepdims=True)
    line = lax.broadcasted_iota(jnp.int32, out_ref.shape, 0)
    omega_row = jnp.where(lane_row == CLASSES, log_ref[0:1, :], omega_row)
    omega_row = pltpu.roll(jnp.broadcast_to(omega_row, (8, 128)), 64, 1)[0:1]
    packed = packed + jnp.where(line == 0, omega_row, 0.0)
    out_ref[...] = packed + jnp.where(line == 12 + subtree, length_row, 0.0)


def last_kernel(total_sites, count, *refs):
    members = lax.axis_size("branch")
    subtree = lax.axis_index("branch")
    exch_ref, omega_ref, length_ref, log_ref = refs[count:]
    total = tree_sum([ref[...] for ref in refs[:count]])
    masks, picks = neighbours()
    table = jnp.zeros((64, 128), F32)
    for at_position, pick in zip(masks, picks):
        table = table + jnp.where(at_position, exact(pick, total), 0.0)
    exch_ref[...] = table[:, 0:64]
    moved = pltpu.roll(total[0:8], 64, 1)
    omega_ref[...] = moved[0:1, 0:CLASSES]
    line = lax.broadcasted_iota(jnp.int32, total.shape, 0)
    lengths = jnp.sum(jnp.where(line == 12 + subtree, total, 0.0), axis=0, keepdims=True)
    length_ref[...] = lengths[:, 0:EDGES]
    log_ref[...] = moved[0:1, CLASSES : CLASSES + 1] / total_sites / (LEAF_DEV * members)


def partners(x, axis, start, radix):
    size = lax.axis_size(axis)
    others = [
        lax.ppermute(x, axis, [(i, i ^ (step * start)) for i in range(size)])
        for step in range(1, radix)
    ]
    return [x] + others


def tree_sum(parts):
    while len(parts) > 1:
        parts = [parts[i] + parts[i + 1] for i in range(0, len(parts), 2)]
    return parts[0]


def axis_steps(axis):
    size, start, steps = lax.axis_size(axis), 1, []
    while start < size:
        radix = min(4, size // start)
        steps.append((axis, start, radix))
        start *= radix
    return steps


def body(
    total_sites, states, gap_mask, weights, leaf_order, exchanges, codon_freq, omega_ratio,
    lengths, classes,
):
    sites = states.shape[1]
    members = lax.axis_size("branch")
    sense, single, nonsyn = codon_tables()
    vmem = pl.BlockSpec(memory_space=pltpu.VMEM)
    smem = pl.BlockSpec(memory_space=pltpu.SMEM)
    shape = jax.ShapeDtypeStruct
    held = pltpu.VMEM
    limit = pltpu.CompilerParams(vmem_limit_bytes=20 * 2**20)

    def outside(x):
        return pltpu.with_memory_space_constraint(x, pltpu.HBM)

    def inside(xs):
        return [pltpu.with_memory_space_constraint(x, pltpu.VMEM) for x in xs]

    sense2 = outside(jnp.asarray(np.tile(sense[None, :], (1, 2))))
    single2 = outside(jnp.asarray(np.tile(single, (1, 2))))
    nonsyn2 = outside(jnp.asarray(np.tile(nonsyn, (1, 2))))
    freq = outside(codon_freq.reshape(1, 64))
    span, owner = outside(lengths.reshape(1, EDGES)), outside(classes.reshape(1, EDGES))
    table, omega = outside(exchanges), outside(omega_ratio)

    chain, last, up, powers, dup = inside(pl.pallas_call(
        matrix_kernel,
        out_shape=[
            held((4, 2, PAIRS, 64, 128), BF),
            held((PAIRS, 64, 128), F32),
            held((2 * PAIRS, 64, 256), BF),
            held((CLASSES // 2, 4, 64, 128), F32),
            held((ORDER * CLASSES * 32, 128), F32),
        ],
        in_specs=[vmem, vmem, smem] + [vmem] * 5,
        out_specs=[vmem] * 5,
        scratch_shapes=[pltpu.VMEM((PAIRS * 64, 128), F32)],
        compiler_params=limit,
        name="matrices",
    )(table, freq, omega, span, owner, sense2, single2, nonsyn2))
    top, *kept = pl.pallas_call(
        up_kernel,
        out_shape=[
            shape((64, sites), F32),
            held((PAIRS, 128, sites), F32),
            held((64, 64, sites), BF),
            held((64, 64, sites), BF),
            held((32, 128, sites), BF),
            held((64, sites), F32),
            held((64, sites), F32),
        ],
        in_specs=[vmem, vmem, smem, vmem],
        out_specs=[vmem] * 7,
        compiler_params=limit,
        name="up",
    )(outside(states), outside(gap_mask), outside(leaf_order), up)
    message, high, low, leaf, scale, inverse = inside(kept)
    tops = partners(top, "branch", 1, members)
    slope, matrix, turned = inside(pl.pallas_call(
        side_kernel,
        out_shape=[
            held((PAIRS * 64, 128), F32),
            held((64, 64, 256), BF),
            held((128, 128), F32),
        ],
        in_specs=[vmem] * 6,
        out_specs=[vmem] * 3,
        compiler_params=limit,
        name="side",
    )(dup, last, span, owner, freq, sense2))
    counts, logs = inside(pl.pallas_call(
        functools.partial(down_kernel, total_sites, members),
        out_shape=[held((PAIRS, 64, 128), F32), held((8, 128), F32)],
        in_specs=[vmem] * (10 + members),
        out_specs=[vmem] * 2,
        scratch_shapes=[
            pltpu.VMEM((32, 128, sites), BF),
            pltpu.VMEM((32, 128, sites), BF),
        ],
        compiler_params=limit,
        name="down",
    )(
        *tops, matrix, message, high, low, leaf, scale, inverse,
        outside(weights.reshape(1, sites)), freq, sense2,
    ))
    part = pl.pallas_call(
        functools.partial(adjoint_kernel, members),
        out_shape=shape((16, 128), F32),
        in_specs=[vmem] * 8 + [smem] + [vmem] * 3,
        out_specs=vmem,
        scratch_shapes=[
            pltpu.VMEM((PAIRS * 64, 128), F32),
            pltpu.VMEM((64 * 64, 128), F32),
        ],
        compiler_params=limit,
        name="adjoint",
    )(
        chain, turned, slope, powers, counts, logs, table, freq, omega,
        sense2, single2, nonsyn2,
    )
    steps = axis_steps("branch") + axis_steps("site")
    for step in steps[:-1]:
        part = tree_sum(partners(part, *step))
    parts = partners(part, *steps[-1])
    exch, ratio, length, loglik = pl.pallas_call(
        functools.partial(last_kernel, total_sites, len(parts)),
        out_shape=[shape((64, 64), F32), shape((1, CLASSES), F32), shape((1, EDGES), F32), shape((1, 1), F32)],
        in_specs=[vmem] * len(parts),
        out_specs=[vmem] * 4,
        compiler_params=limit,
        name="last",
    )(*parts)
    return (exch, ratio.reshape(CLASSES), length.reshape(EDGES), loglik.reshape(()))


def solution(mesh):
    def whole(states, *rest):
        total_sites = states.shape[1]
        return jax.shard_map(
            functools.partial(body, total_sites),
            mesh=mesh,
            in_specs=(
                P(None, "site"),
                P(None, "site"),
                P("site"),
                P(),
                P(),
                P(),
                P(),
                P("branch"),
                P("branch"),
            ),
            out_specs=(P(), P(), P("branch"), P()),
            check_vma=False,
        )(states, *rest)

    return whole
```

profile of v0, /device:TPU:0, one launch (start us, length us, event | category | flops | bytes accessed | tf_op | source)
XLA Modules:
  0.0 84.8 jit_solution(11526612717687649100)
XLA Ops:
  0.6 19.5 %matrices.1 = (bf16[4,2,64,64,128]{4,3,2,1,0:T(8,128)(2,1)S(1)}, f32[64,64,128]{2,1,0:T(8,128)S(1)}, bf16[128,64,256]{2,1,0:T(8,128)(2,1)S(1)}, f32[4,4,64,128]{3,2,1,0:T(8,128)S(1)}, f32[2048,128]{1,0:T(8,128)S(1)}) custom-call(f32[64,64]{1,0:T(8,128)} %ex_ref.3, f32[1,64]{1,0:T(1,128)} %bitcast.7, f32[8]{0:T(128)} %omega_ref.3, f32[1,127]{1,0:T(1,128)} %bitcast.11, ...), custom_call_target="tpu_custom_call" | custom-call | tf_op jit(solution)/shard_map/matrices/pallas_call | solution.py:635
  20.2 8.3 %up.1 = (f32[64,256]{1,0:T(8,128)S(1)}, f32[64,128,256]{2,1,0:T(8,128)S(1)}, bf16[64,64,256]{2,1,0:T(8,128)(2,1)S(1)}, bf16[64,64,256]{2,1,0:T(8,128)(2,1)S(1)},...) custom-call(s32[256,256]{1,0:T(8,128)} %states_ref.1, s32[256,256]{1,0:T(8,128)} %gap_ref.1, ...), custom_call_target="tpu_custom_call" | custom-call | tf_op jit(solution)/shard_map/up/pallas_call | solution.py:650
  28.5 2.4 %collective-permute-start.2 = (f32[64,256]{1,0:T(8,128)S(1)}, f32[64,256]{1,0:T(8,128)S(1)}, u32[]{:S(2)}, u32[]{:S(2)}) collective-permute-start(f32[64,256]{1,0:T(8,128)S(1)} %get-tuple-element.32.refs_0_), channel_id=1, source_target_pairs={{0,3},{1,2},{2,1},{3,0},{4,7},{5,6},{6,5},{7,4},{8,11},{9,10},{10,... | collective-permute-start | bytes 196616 | tf_op jit(solution)/shard_map/ppermute | solution.py:588
  30.9 0.6 collective-permute-start.1
  31.6 0.0 collective-permute-start
  31.6 4.4 %side.1 = (f32[4096,128]{1,0:T(8,128)S(1)}, bf16[64,64,256]{2,1,0:T(8,128)(2,1)S(1)}, f32[128,128]{1,0:T(8,128)S(1)}) custom-call(f32[2048,128]{1,0:T(8,128)S(1)} %get-tuple-element.26.dup_ref, f32[64,64,128]{2,1,0:T(8,128)S(1)} %get-tuple-element.27.last_ref, f32[1,127]{1,0:T(1,128)} %bitcast.12, s32[1,127]{1,0:T(1,128)} %bitcast.14, f32[1,64]{1,0:T(1,128)} %bitcast.8, ...), custom_call_target="tpu_custom_call" | custom-call | tf_op jit(solution)/shard_map/side/pallas_call | solution.py:668
  36.0 0.0 collective-permute-done.2.refs_3_
  36.0 0.0 collective-permute-done.1.refs_2_
  36.1 0.0 collective-permute-done.refs_1_
  36.1 9.1 %down.1 = (f32[64,64,128]{2,1,0:T(8,128)S(1)}, f32[8,128]{1,0:T(8,128)S(1)}) custom-call(f32[64,256]{1,0:T(8,128)S(1)} %get-tuple-element.32.refs_0_, f32[64,256]{1,0:T(8,128)S(1)} %collective-permute-done.refs_1_, f32[64,256]{1,0:T(8,128)S(1)} %collective-permute-done.1.refs_2_, f32[64,256]{1,0:T(8,128)S(1)} %collective-permute-done.2.refs_3_, ...), custom_call_target="tpu_custom_call" | custom-call | tf_op jit(solution)/shard_map/down/pallas_call | solution.py:680
  45.1 22.4 %adjoint.1 = f32[16,128]{1,0:T(8,128)S(1)} custom-call(bf16[4,2,64,64,128]{4,3,2,1,0:T(8,128)(2,1)S(1)} %get-tuple-element.25.chain_ref, f32[128,128]{1,0:T(8,128)S(1)} %get-tuple-element.28.turned_ref, f32[4096,128]{1,0:T(8,128)S(1)} %get-tuple-element.29.slope_ref, f32[4,4,64,128]{3,2,1,0:T(8,128)S(1)} %get-tuple-element.30.power_ref, ...), custom_call_target="tpu_custom_call" | custom-call | tf_op jit(solution)/shard_map/adjoint/pallas_call | solution.py:695
  67.6 1.5 %collective-permute-start.5 = (f32[16,128]{1,0:T(8,128)S(1)}, f32[16,128]{1,0:T(8,128)S(1)}, u32[]{:S(2)}, u32[]{:S(2)}) collective-permute-start(f32[16,128]{1,0:T(8,128)S(1)} %adjoint.1), channel_id=1, source_target_pairs={{0,3},{1,2},{2,1},{3,0},{4,7},{5,6},{6,5},{7,4},{8,11},{9,10},{10,... | collective-permute-start | bytes 24584 | tf_op jit(solution)/shard_map/ppermute | solution.py:588
  69.0 0.6 collective-permute-start.4
  69.7 0.0 collective-permute-start.3
  69.7 1.0 %collective-permute-done.5 = f32[16,128]{1,0:T(8,128)S(1)} collective-permute-done((f32[16,128]{1,0:T(8,128)S(1)}, f32[16,128]{1,0:T(8,128)S(1)}, u32[]{:S(2)}, u32[]{:S(2)}) %collective-permute-start.5) | collective-permute-done | bytes 8224 | tf_op jit(solution)/shard_map/ppermute | solution.py:588
  70.7 2.0 %collective-permute-done.4 = f32[16,128]{1,0:T(8,128)S(1)} collective-permute-done((f32[16,128]{1,0:T(8,128)S(1)}, f32[16,128]{1,0:T(8,128)S(1)}, u32[]{:S(2)}, u32[]{:S(2)}) %collective-permute-start.4) | collective-permute-done | bytes 8224 | tf_op jit(solution)/shard_map/ppermute | solution.py:588
  72.7 0.0 collective-permute-done.3
  72.7 2.6 %collective-permute-start.8 = (f32[16,128]{1,0:T(8,128)S(1)}, f32[16,128]{1,0:T(8,128)S(1)}, u32[]{:S(2)}, u32[]{:S(2)}) collective-permute-start(f32[16,128]{1,0:T(8,128)S(1)} %add_add_fusion.1), channel_id=1, source_target_pairs={{0,12},{4,8},{8,4},{12,0},{16,28},{20,24},{24,20},{28,16},{1,13},{... | collective-permute-start | bytes 24584 | tf_op jit(solution)/shard_map/ppermute | solution.py:588
  75.3 0.4 collective-permute-start.7
  75.7 0.5 collective-permute-start.6
  76.3 1.1 %collective-permute-done.8 = f32[16,128]{1,0:T(8,128)S(1)} collective-permute-done((f32[16,128]{1,0:T(8,128)S(1)}, f32[16,128]{1,0:T(8,128)S(1)}, u32[]{:S(2)}, u32[]{:S(2)}) %collective-permute-start.8) | collective-permute-done | bytes 8224 | tf_op jit(solution)/shard_map/ppermute | solution.py:588
  77.3 1.6 %collective-permute-done.7 = f32[16,128]{1,0:T(8,128)S(1)} collective-permute-done((f32[16,128]{1,0:T(8,128)S(1)}, f32[16,128]{1,0:T(8,128)S(1)}, u32[]{:S(2)}, u32[]{:S(2)}) %collective-permute-start.7) | collective-permute-done | bytes 8224 | tf_op jit(solution)/shard_map/ppermute | solution.py:588
  79.0 0.4 collective-permute-done.6
  79.4 2.6 %collective-permute-start.9 = (f32[16,128]{1,0:T(8,128)S(1)}, f32[16,128]{1,0:T(8,128)S(1)}, u32[]{:S(2)}, u32[]{:S(2)}) collective-permute-start(f32[16,128]{1,0:T(8,128)S(1)} %add_add_fusion.refs_0_), channel_id=1, source_target_pairs={{0,16},{4,20},{8,24},{12,28},{16,0},{20,4},{24,8},{28,12},{1,17},{... | collective-permute-start | bytes 24584 | tf_op jit(solution)/shard_map/ppermute | solution.py:588
  82.0 2.0 %collective-permute-done.9.refs_1_ = f32[16,128]{1,0:T(8,128)S(1)} collective-permute-done((f32[16,128]{1,0:T(8,128)S(1)}, f32[16,128]{1,0:T(8,128)S(1)}, u32[]{:S(2)}, u32[]{:S(2)}) %collective-permute-start.9) | collective-permute-done | bytes 8224 | tf_op jit(solution)/shard_map/ppermute | solution.py:588
  84.0 0.8 last.1
  (2 shorter events, 0.0 us)
Async XLA Ops:
  28.5 7.5 %collective-permute-start.2 = (f32[64,256]{1,0:T(8,128)S(1)}, f32[64,256]{1,0:T(8,128)S(1)}, u32[]{:S(2)}, u32[]{:S(2)}) collective-permute-start(f32[64,256]{1,0:T(8,128)S(1)} %get-tuple-element.32.refs_0_), channel_id=1, source_target_pairs={{0,3},{1,2},{2,1},{3,0},{4,7},{5,6},{6,5},{7,4},{8,11},{9,10},{10,... | collective-permute-start | bytes 196616 | tf_op jit(solution)/shard_map/ppermute | solution.py:588
  30.9 5.1 %collective-permute-start.1 = (f32[64,256]{1,0:T(8,128)S(1)}, f32[64,256]{1,0:T(8,128)S(1)}, u32[]{:S(2)}, u32[]{:S(2)}) collective-permute-start(f32[64,256]{1,0:T(8,128)S(1)} %get-tuple-element.32.refs_0_), channel_id=1, source_target_pairs={{0,2},{1,3},{2,0},{3,1},{4,6},{5,7},{6,4},{7,5},{8,10},{9,11},{10,... | collective-permute-start | bytes 196616 | tf_op jit(solution)/shard_map/ppermute | solution.py:588
  31.6 4.5 %collective-permute-start = (f32[64,256]{1,0:T(8,128)S(1)}, f32[64,256]{1,0:T(8,128)S(1)}, u32[]{:S(2)}, u32[]{:S(2)}) collective-permute-start(f32[64,256]{1,0:T(8,128)S(1)} %get-tuple-element.32.refs_0_), channel_id=1, source_target_pairs={{0,1},{1,0},{2,3},{3,2},{4,5},{5,4},{6,7},{7,6},{8,9},{9,8},{10,11... | collective-permute-start | bytes 196616 | tf_op jit(solution)/shard_map/ppermute | solution.py:588
  67.6 3.1 %collective-permute-start.5 = (f32[16,128]{1,0:T(8,128)S(1)}, f32[16,128]{1,0:T(8,128)S(1)}, u32[]{:S(2)}, u32[]{:S(2)}) collective-permute-start(f32[16,128]{1,0:T(8,128)S(1)} %adjoint.1), channel_id=1, source_target_pairs={{0,3},{1,2},{2,1},{3,0},{4,7},{5,6},{6,5},{7,4},{8,11},{9,10},{10,... | collective-permute-start | bytes 24584 | tf_op jit(solution)/shard_map/ppermute | solution.py:588
  69.0 3.7 %collective-permute-start.4 = (f32[16,128]{1,0:T(8,128)S(1)}, f32[16,128]{1,0:T(8,128)S(1)}, u32[]{:S(2)}, u32[]{:S(2)}) collective-permute-start(f32[16,128]{1,0:T(8,128)S(1)} %adjoint.1), channel_id=1, source_target_pairs={{0,2},{1,3},{2,0},{3,1},{4,6},{5,7},{6,4},{7,5},{8,10},{9,11},{10,... | collective-permute-start | bytes 24584 | tf_op jit(solution)/shard_map/ppermute | solution.py:588
  69.7 3.0 %collective-permute-start.3 = (f32[16,128]{1,0:T(8,128)S(1)}, f32[16,128]{1,0:T(8,128)S(1)}, u32[]{:S(2)}, u32[]{:S(2)}) collective-permute-start(f32[16,128]{1,0:T(8,128)S(1)} %adjoint.1), channel_id=1, source_target_pairs={{0,1},{1,0},{2,3},{3,2},{4,5},{5,4},{6,7},{7,6},{8,9},{9,8},{10,11... | collective-permute-start | bytes 24584 | tf_op jit(solution)/shard_map/ppermute | solution.py:588
  72.7 4.6 %collective-permute-start.8 = (f32[16,128]{1,0:T(8,128)S(1)}, f32[16,128]{1,0:T(8,128)S(1)}, u32[]{:S(2)}, u32[]{:S(2)}) collective-permute-start(f32[16,128]{1,0:T(8,128)S(1)} %add_add_fusion.1), channel_id=1, source_target_pairs={{0,12},{4,8},{8,4},{12,0},{16,28},{20,24},{24,20},{28,16},{1,13},{... | collective-permute-start | bytes 24584 | tf_op jit(solution)/shard_map/ppermute | solution.py:588
  75.3 3.7 %collective-permute-start.7 = (f32[16,128]{1,0:T(8,128)S(1)}, f32[16,128]{1,0:T(8,128)S(1)}, u32[]{:S(2)}, u32[]{:S(2)}) collective-permute-start(f32[16,128]{1,0:T(8,128)S(1)} %add_add_fusion.1), channel_id=1, source_target_pairs={{0,8},{4,12},{8,0},{12,4},{16,24},{20,28},{24,16},{28,20},{1,9},{5... | collective-permute-start | bytes 24584 | tf_op jit(solution)/shard_map/ppermute | solution.py:588
  75.7 3.7 %collective-permute-start.6 = (f32[16,128]{1,0:T(8,128)S(1)}, f32[16,128]{1,0:T(8,128)S(1)}, u32[]{:S(2)}, u32[]{:S(2)}) collective-permute-start(f32[16,128]{1,0:T(8,128)S(1)} %add_add_fusion.1), channel_id=1, source_target_pairs={{0,4},{4,0},{8,12},{12,8},{16,20},{20,16},{24,28},{28,24},{1,5},{5... | collective-permute-start | bytes 24584 | tf_op jit(solution)/shard_map/ppermute | solution.py:588
  79.4 4.5 %collective-permute-start.9 = (f32[16,128]{1,0:T(8,128)S(1)}, f32[16,128]{1,0:T(8,128)S(1)}, u32[]{:S(2)}, u32[]{:S(2)}) collective-permute-start(f32[16,128]{1,0:T(8,128)S(1)} %add_add_fusion.refs_0_), channel_id=1, source_target_pairs={{0,16},{4,20},{8,24},{12,28},{16,0},{20,4},{24,8},{28,12},{1,17},{... | collective-permute-start | bytes 24584 | tf_op jit(solution)/shard_map/ppermute | solution.py:588
where the time goes:
time: 85.1 us; the launch traced here: 84.8 us
  Pallas kernels  64.6 us (76%)
  starting transfers between devices  11.4 us (13%)
  waiting for transfers between devices  8.12 us (10%)
    pallas_call x1, Pallas kernels, body(): pl.pallas_call(functools.partial(adjoint_kernel, members), out_shape=shap...  22.4 us
    pallas_call x1, Pallas kernels, body(): pl.pallas_call(matrix_kernel, out_shape=[held((4, 2, PAIRS, 64, 128), BF)...  19.5 us
    ppermute x10, starting transfers between devices, partners(): lax.ppermute(x, axis, [(i, i ^ step * start) for i in range(size)])  11.4 us
    pallas_call x1, Pallas kernels, body(): pl.pallas_call(functools.partial(down_kernel, total_sites, members), out_...  9.06 us
    pallas_call x1, Pallas kernels, body(): pl.pallas_call(up_kernel, out_shape=[shape((64, sites), F32), held((PAIRS...  8.31 us
    ppermute x10, waiting for transfers between devices, partners(): lax.ppermute(x, axis, [(i, i ^ step * start) for i in range(size)])  8.12 us
    pallas_call x1, Pallas kernels, body(): pl.pallas_call(side_kernel, out_shape=[held((PAIRS * 64, 128), F32), held...  4.41 us
  transfers between devices with their start and end apart: 10, of which 6 were waited for; matrix products, arithmetic and copies ran while one was open for 0% of the time, Pallas kernels for 5%

commit v1 on v0

--- a/solution.py
+++ b/solution.py
@@ -46,6 +46,13 @@
     return jnp.concatenate([x * low, x * high], axis=0)
 
 
+def two_blocks(pairs, zero):
+    return jnp.concatenate([
+        jnp.concatenate([spread(pairs[0]), zero], axis=1),
+        jnp.concatenate([zero, spread(pairs[1])], axis=1),
+    ], axis=0)
+
+
 def mxu(left, right):
     return jnp.dot(left, right, preferred_element_type=F32)
 
@@ -86,16 +93,6 @@
     for e, both in enumerate((jnp.where(mask, x, swapped), jnp.where(mask, swapped, x))):
         high, low = split(both)
         ref[2 * p + e] = jnp.concatenate([high, low], axis=1)
-
-
-def transposes(first, second):
-    mask = low_half()
-    turned = jnp.concatenate([first, second], axis=0).T
-    top, bottom = turned[0:64], turned[64:128]
-    return (
-        jnp.where(mask, top, pltpu.roll(bottom, 64, 1)),
-        jnp.where(mask, pltpu.roll(top, 64, 1), bottom),
-    )
 
 
 def frequencies(freq_ref, sense_ref):
@@ -179,20 +176,24 @@
     return jnp.concatenate([high, low, high, low], axis=0)
 
 
-def expand(left, dup_ref, store):
-    mask = low_half()
+def expand(coefs, dup_ref, store):
+    high, low = split(coefs)
+    left = jnp.concatenate(
+        [jnp.concatenate([high, high], axis=1), jnp.concatenate([low, low], axis=1)], axis=0
+    )
 
     def some(step, carry):
-        for j in range(2):
-            i = step * 4 + 2 * j
-            rows = jnp.concatenate(
-                [dup_ref[rows_of(i, 64), :], dup_ref[rows_of(i + 1, 64), :]], axis=1
-            )
-            both = mxu(left, four_right(rows))
+        for j in range(4):
+            i = step * 8 + 2 * j
+            parts = [split(dup_ref[rows_of(i + t, 64), :]) for t in range(2)]
+            right = jnp.concatenate([
+                jnp.concatenate([spread(parts[0][h]), spread(parts[1][h])], axis=1)
+                for h in range(2)
+            ], axis=0)
+            both = mxu(left, right)
+            both = both[0:64] + both[64:128]
             for t in range(2):
-                even, odd = both[0:64, 128 * t : 128 * t + 128], both[64:128, 128 * t : 128 * t + 128]
-                store(i + t, jnp.where(mask, even, pltpu.roll(odd, 64, 1)))
-                store(i + t + 32, jnp.where(mask, pltpu.roll(even, 64, 1), odd))
+                store(i + t, both[:, 128 * t : 128 * t + 128])
         return carry
 
     lax.fori_loop(0, 8, some, 0)
@@ -226,9 +227,8 @@
             value = powers[pair][k]
             swapped = pltpu.roll(value, 64, 1)
             at = CLASSES * k + 2 * pair
-            top, half = value[0:32], low_half()[0:32]
-            dup_ref[pl.ds(at, 32, stride=64), :] = jnp.where(half, top, swapped[32:64])
-            dup_ref[pl.ds(at + 1, 32, stride=64), :] = jnp.where(half, swapped[0:32], value[32:64])
+            dup_ref[pl.ds(at, 64, stride=64), :] = jnp.where(mask, value, swapped)
+            dup_ref[pl.ds(at + 1, 64, stride=64), :] = jnp.where(mask, swapped, value)
             if k < 4:
                 power_ref[pair, k] = value
 
@@ -237,24 +237,26 @@
     def store(i, value):
         first_ref[rows_of(i, 64), :] = value
 
-    expand(four_left(jnp.concatenate([even, odd], axis=0)), dup_ref, store)
+    expand(jnp.where(low_half(), even, odd), dup_ref, store)
 
     def squarings(step, carry):
         held = [first_ref[pl.ds(step * 8 + j, 64, stride=64), :] for j in range(8)]
+        zero = jnp.zeros((128, 128), BF)
         for level in range(4):
-            parts = []
-            for j in range(8):
-                high, low = split(held[j])
-                chain_ref[level, 0, step * 8 + j] = high
-                chain_ref[level, 1, step * 8 + j] = low
-                parts.append(mxu(
-                    jnp.concatenate([high, high], axis=1),
-                    jnp.concatenate([spread(high, 0.5), spread(low)], axis=0),
-                ))
             for j in range(0, 8, 2):
-                turned = transposes(parts[j], parts[j + 1])
+                highs, lows = [], []
                 for t in range(2):
-                    held[j + t] = 2.0 * held[j + t] + parts[j + t] + turned[t]
+                    high, low = split(held[j + t])
+                    chain_ref[level, 0, step * 8 + j + t] = high
+                    chain_ref[level, 1, step * 8 + j + t] = low
+                    highs.append(high)
+                    lows.append(low)
+                upper, lower = jnp.concatenate(highs, axis=1), jnp.concatenate(lows, axis=1)
+                one = mxu(jnp.concatenate([upper, lower], axis=0), two_blocks(highs, zero))
+                two = mxu(upper, two_blocks(lows, zero))
+                both = one[0:64] + one[64:128] + two
+                for t in range(2):
+                    held[j + t] = 2.0 * held[j + t] + both[:, 128 * t : 128 * t + 128]
         for j in range(8):
             p = step * 8 + j
             last_ref[p] = held[j]
@@ -335,7 +337,7 @@
     def store(i, value):
         slope_ref[rows_of(i, 64), :] = value
 
-    expand(four_left(jnp.concatenate([even, odd], axis=0)), dup_ref, store)
+    expand(jnp.where(low_half(), even, odd), dup_ref, store)
     even, odd = coefficients(len_ref, cls_ref, False)
     turned_ref[...] = exact_tn(jnp.where(low_half(), even, odd), twice)
     inverse_root_row = 1.0 / root_row
@@ -446,35 +448,22 @@
     inverse_root_row = 1.0 / root_row
 
     def adjoint(step, carry):
-        held = []
-        for j in range(0, 8, 2):
-            here = [count_ref[step * 8 + j + t] for t in range(2)]
-            turned = transposes(*here)
-            held += [0.5 * (here[t] + turned[t]) for t in range(2)]
-        zero = jnp.zeros((128, 128), BF)
+        held = [count_ref[step * 8 + j] for j in range(8)]
         for level in range(3, -1, -1):
-            for j in range(0, 8, 2):
-                parts, highs, lows = [], [], []
-                for t in range(2):
-                    high, low = split(held[j + t])
-                    wide = spread(chain_ref[level, 0, step * 8 + j + t])
-                    lows.append(spread(chain_ref[level, 1, step * 8 + j + t]))
-                    highs.append(high)
-                    parts.append(mxu(
-                        jnp.concatenate([high, low], axis=1),
-                        jnp.concatenate([wide, wide], axis=0),
-                    ))
-                rest = mxu(
-                    jnp.concatenate(highs, axis=1),
-                    jnp.concatenate([
-                        jnp.concatenate([lows[0], zero], axis=1),
-                        jnp.concatenate([zero, lows[1]], axis=1),
-                    ], axis=0),
-                )
-                parts = [parts[t] + rest[:, 128 * t : 128 * t + 128] for t in range(2)]
-                turned = transposes(*parts)
-                for t in range(2):
-                    held[j + t] = 2.0 * held[j + t] + parts[t] + turned[t]
+            for j in range(8):
+                high, low = split(held[j])
+                e_high, e_low = chain_ref[level, 0, step * 8 + j], chain_ref[level, 1, step * 8 + j]
+                left = jnp.concatenate([
+                    jnp.concatenate([high, e_high], axis=1),
+                    jnp.concatenate([low, e_low], axis=1),
+                ], axis=0)
+                right = jnp.concatenate([
+                    jnp.concatenate([spread(e_high), spread(e_low)], axis=1),
+                    jnp.concatenate([spread(high), spread(low)], axis=1),
+                ], axis=0)
+                four = mxu(left, right)
+                four = four[0:64] + four[64:128]
+                held[j] = 2.0 * held[j] + four[:, 0:128] + four[:, 128:256]
         for j in range(8):
             back_ref[pl.ds(step * 8 + j, 64, stride=64), :] = held[j]
         return carry
@@ -639,7 +628,7 @@
             held((PAIRS, 64, 128), F32),
             held((2 * PAIRS, 64, 256), BF),
             held((CLASSES // 2, 4, 64, 128), F32),
-            held((ORDER * CLASSES * 32, 128), F32),
+            held((ORDER * CLASSES * 64, 128), F32),
         ],
         in_specs=[vmem, vmem, smem] + [vmem] * 5,
         out_specs=[vmem] * 5,

time: 85.1 us -> 71.3 us (0.84)
  Pallas kernels: 64.6 us -> 50.8 us
    pallas_call x1, Pallas kernels: 22.4 us -> 14.4 us  [body(): pl.pallas_call(functools.partial(adjoint_kernel, members), out_shape=shap...]
    pallas_call x1, Pallas kernels: 19.5 us -> 14.3 us  [body(): pl.pallas_call(matrix_kernel, out_shape=[held((4, 2, PAIRS, 64, 128), BF)...]
  transfers between devices with their start and end apart: 10 -> 10, of which waited for: 6 -> 6; matrix products, arithmetic and copies ran while one was open for 0% -> 0% of each run, Pallas kernels for 5% -> 6%
where the time goes in v1:
time: 71.3 us; the launch traced here: 71 us
  Pallas kernels  50.8 us (71%)
  starting transfers between devices  11.3 us (16%)
  waiting for transfers between devices  8.15 us (11%)
    pallas_call x1, Pallas kernels, body(): pl.pallas_call(functools.partial(adjoint_kernel, members), out_shape=shap...  14.4 us
    pallas_call x1, Pallas kernels, body(): pl.pallas_call(matrix_kernel, out_shape=[held((4, 2, PAIRS, 64, 128), BF)...  14.3 us
    ppermute x10, starting transfers between devices, partners(): lax.ppermute(x, axis, [(i, i ^ step * start) for i in range(size)])  11.3 us
    pallas_call x1, Pallas kernels, body(): pl.pallas_call(functools.partial(down_kernel, total_sites, members), out_...  9.07 us
    pallas_call x1, Pallas kernels, body(): pl.pallas_call(up_kernel, out_shape=[shape((64, sites), F32), held((PAIRS...  8.31 us
    ppermute x10, waiting for transfers between devices, partners(): lax.ppermute(x, axis, [(i, i ^ step * start) for i in range(size)])  8.15 us
    pallas_call x1, Pallas kernels, body(): pl.pallas_call(side_kernel, out_shape=[held((PAIRS * 64, 128), F32), held...  3.96 us
  transfers between devices with their start and end apart: 10, of which 6 were waited for; matrix products, arithmetic and copies ran while one was open for 0% of the time, Pallas kernels for 6%

profile of v1, /device:TPU:0, one launch (start us, length us, event | category | flops | bytes accessed | tf_op | source)
XLA Modules:
  0.0 71.0 jit_solution(15893161799702541652)
XLA Ops:
  0.6 14.3 %matrices.1 = (bf16[4,2,64,64,128]{4,3,2,1,0:T(8,128)(2,1)S(1)}, f32[64,64,128]{2,1,0:T(8,128)S(1)}, bf16[128,64,256]{2,1,0:T(8,128)(2,1)S(1)}, f32[4,4,64,128]{3,2,1,0:T(8,128)S(1)}, f32[4096,128]{1,0:T(8,128)S(1)}) custom-call(f32[64,64]{1,0:T(8,128)} %ex_ref.3, f32[1,64]{1,0:T(1,128)} %bitcast.7, f32[8]{0:T(128)} %omega_ref.3, f32[1,127]{1,0:T(1,128)} %bitcast.11, ...), custom_call_target="tpu_custom_call" | custom-call | tf_op jit(solution)/shard_map/matrices/pallas_call | solution.py:624
  14.9 8.3 %up.1 = (f32[64,256]{1,0:T(8,128)S(1)}, f32[64,128,256]{2,1,0:T(8,128)S(1)}, bf16[64,64,256]{2,1,0:T(8,128)(2,1)S(1)}, bf16[64,64,256]{2,1,0:T(8,128)(2,1)S(1)},...) custom-call(s32[256,256]{1,0:T(8,128)} %states_ref.1, s32[256,256]{1,0:T(8,128)} %gap_ref.1, ...), custom_call_target="tpu_custom_call" | custom-call | tf_op jit(solution)/shard_map/up/pallas_call | solution.py:639
  23.2 2.4 %collective-permute-start.2 = (f32[64,256]{1,0:T(8,128)S(1)}, f32[64,256]{1,0:T(8,128)S(1)}, u32[]{:S(2)}, u32[]{:S(2)}) collective-permute-start(f32[64,256]{1,0:T(8,128)S(1)} %get-tuple-element.32.refs_0_), channel_id=1, source_target_pairs={{0,3},{1,2},{2,1},{3,0},{4,7},{5,6},{6,5},{7,4},{8,11},{9,10},{10,... | collective-permute-start | bytes 196616 | tf_op jit(solution)/shard_map/ppermute | solution.py:577
  25.7 0.7 collective-permute-start.1
  26.3 0.0 collective-permute-start
  26.4 4.0 %side.1 = (f32[4096,128]{1,0:T(8,128)S(1)}, bf16[64,64,256]{2,1,0:T(8,128)(2,1)S(1)}, f32[128,128]{1,0:T(8,128)S(1)}) custom-call(f32[4096,128]{1,0:T(8,128)S(1)} %get-tuple-element.26.dup_ref, f32[64,64,128]{2,1,0:T(8,128)S(1)} %get-tuple-element.27.last_ref, f32[1,127]{1,0:T(1,128)} %bitcast.12, s32[1,127]{1,0:T(1,128)} %bitcast.14, f32[1,64]{1,0:T(1,128)} %bitcast.8, ...), custom_call_target="tpu_custom_call" | custom-call | tf_op jit(solution)/shard_map/side/pallas_call | solution.py:657
  30.3 0.0 collective-permute-done.2.refs_3_
  30.3 0.0 collective-permute-done.1.refs_2_
  30.4 0.0 collective-permute-done.refs_1_
  30.4 9.1 %down.1 = (f32[64,64,128]{2,1,0:T(8,128)S(1)}, f32[8,128]{1,0:T(8,128)S(1)}) custom-call(f32[64,256]{1,0:T(8,128)S(1)} %get-tuple-element.32.refs_0_, f32[64,256]{1,0:T(8,128)S(1)} %collective-permute-done.refs_1_, f32[64,256]{1,0:T(8,128)S(1)} %collective-permute-done.1.refs_2_, f32[64,256]{1,0:T(8,128)S(1)} %collective-permute-done.2.refs_3_, ...), custom_call_target="tpu_custom_call" | custom-call | tf_op jit(solution)/shard_map/down/pallas_call | solution.py:669
  39.4 14.4 %adjoint.1 = f32[16,128]{1,0:T(8,128)S(1)} custom-call(bf16[4,2,64,64,128]{4,3,2,1,0:T(8,128)(2,1)S(1)} %get-tuple-element.25.chain_ref, f32[128,128]{1,0:T(8,128)S(1)} %get-tuple-element.28.turned_ref, f32[4096,128]{1,0:T(8,128)S(1)} %get-tuple-element.29.slope_ref, f32[4,4,64,128]{3,2,1,0:T(8,128)S(1)} %get-tuple-element.30.power_ref, ...), custom_call_target="tpu_custom_call" | custom-call | tf_op jit(solution)/shard_map/adjoint/pallas_call | solution.py:684
  53.8 1.4 %collective-permute-start.5 = (f32[16,128]{1,0:T(8,128)S(1)}, f32[16,128]{1,0:T(8,128)S(1)}, u32[]{:S(2)}, u32[]{:S(2)}) collective-permute-start(f32[16,128]{1,0:T(8,128)S(1)} %adjoint.1), channel_id=1, source_target_pairs={{0,3},{1,2},{2,1},{3,0},{4,7},{5,6},{6,5},{7,4},{8,11},{9,10},{10,... | collective-permute-start | bytes 24584 | tf_op jit(solution)/shard_map/ppermute | solution.py:577
  55.2 0.7 collective-permute-start.4
  55.9 0.0 collective-permute-start.3
  55.9 1.0 %collective-permute-done.5 = f32[16,128]{1,0:T(8,128)S(1)} collective-permute-done((f32[16,128]{1,0:T(8,128)S(1)}, f32[16,128]{1,0:T(8,128)S(1)}, u32[]{:S(2)}, u32[]{:S(2)}) %collective-permute-start.5) | collective-permute-done | bytes 8224 | tf_op jit(solution)/shard_map/ppermute | solution.py:577
  56.9 2.0 %collective-permute-done.4 = f32[16,128]{1,0:T(8,128)S(1)} collective-permute-done((f32[16,128]{1,0:T(8,128)S(1)}, f32[16,128]{1,0:T(8,128)S(1)}, u32[]{:S(2)}, u32[]{:S(2)}) %collective-permute-start.4) | collective-permute-done | bytes 8224 | tf_op jit(solution)/shard_map/ppermute | solution.py:577
  58.9 0.0 collective-permute-done.3
  58.9 2.6 %collective-permute-start.8 = (f32[16,128]{1,0:T(8,128)S(1)}, f32[16,128]{1,0:T(8,128)S(1)}, u32[]{:S(2)}, u32[]{:S(2)}) collective-permute-start(f32[16,128]{1,0:T(8,128)S(1)} %add_add_fusion.1), channel_id=1, source_target_pairs={{0,12},{4,8},{8,4},{12,0},{16,28},{20,24},{24,20},{28,16},{1,13},{... | collective-permute-start | bytes 24584 | tf_op jit(solution)/shard_map/ppermute | solution.py:577
  61.5 0.5 collective-permute-start.7
  62.0 0.5 collective-permute-start.6
  62.4 1.1 %collective-permute-done.8 = f32[16,128]{1,0:T(8,128)S(1)} collective-permute-done((f32[16,128]{1,0:T(8,128)S(1)}, f32[16,128]{1,0:T(8,128)S(1)}, u32[]{:S(2)}, u32[]{:S(2)}) %collective-permute-start.8) | collective-permute-done | bytes 8224 | tf_op jit(solution)/shard_map/ppermute | solution.py:577
  63.5 1.6 %collective-permute-done.7 = f32[16,128]{1,0:T(8,128)S(1)} collective-permute-done((f32[16,128]{1,0:T(8,128)S(1)}, f32[16,128]{1,0:T(8,128)S(1)}, u32[]{:S(2)}, u32[]{:S(2)}) %collective-permute-start.7) | collective-permute-done | bytes 8224 | tf_op jit(solution)/shard_map/ppermute | solution.py:577
  65.1 0.5 collective-permute-done.6
  65.6 2.6 %collective-permute-start.9 = (f32[16,128]{1,0:T(8,128)S(1)}, f32[16,128]{1,0:T(8,128)S(1)}, u32[]{:S(2)}, u32[]{:S(2)}) collective-permute-start(f32[16,128]{1,0:T(8,128)S(1)} %add_add_fusion.refs_0_), channel_id=1, source_target_pairs={{0,16},{4,20},{8,24},{12,28},{16,0},{20,4},{24,8},{28,12},{1,17},{... | collective-permute-start | bytes 24584 | tf_op jit(solution)/shard_map/ppermute | solution.py:577
  68.2 2.0 %collective-permute-done.9.refs_1_ = f32[16,128]{1,0:T(8,128)S(1)} collective-permute-done((f32[16,128]{1,0:T(8,128)S(1)}, f32[16,128]{1,0:T(8,128)S(1)}, u32[]{:S(2)}, u32[]{:S(2)}) %collective-permute-start.9) | collective-permute-done | bytes 8224 | tf_op jit(solution)/shard_map/ppermute | solution.py:577
  70.2 0.8 %last.1 = (f32[64,64]{1,0:T(8,128)}, f32[1,8]{1,0:T(1,128)}, f32[1,127]{1,0:T(1,128)}, f32[1,1]{1,0:T(1,128)}) custom-call(f32[16,128]{1,0:T(8,128)S(1)} %add_add_fusion.refs_0_, f32[16,128]{1,0:T(8,128)S(1)} %collective-permute-done.9.refs_1_), custom_call_target="tpu_custom_call" | custom-call | tf_op jit(solution)/shard_map/last/pallas_call | solution.py:703
  (2 shorter events, 0.0 us)
Async XLA Ops:
  23.2 7.1 %collective-permute-start.2 = (f32[64,256]{1,0:T(8,128)S(1)}, f32[64,256]{1,0:T(8,128)S(1)}, u32[]{:S(2)}, u32[]{:S(2)}) collective-permute-start(f32[64,256]{1,0:T(8,128)S(1)} %get-tuple-element.32.refs_0_), channel_id=1, source_target_pairs={{0,3},{1,2},{2,1},{3,0},{4,7},{5,6},{6,5},{7,4},{8,11},{9,10},{10,... | collective-permute-start | bytes 196616 | tf_op jit(solution)/shard_map/ppermute | solution.py:577
  25.7 4.7 %collective-permute-start.1 = (f32[64,256]{1,0:T(8,128)S(1)}, f32[64,256]{1,0:T(8,128)S(1)}, u32[]{:S(2)}, u32[]{:S(2)}) collective-permute-start(f32[64,256]{1,0:T(8,128)S(1)} %get-tuple-element.32.refs_0_), channel_id=1, source_target_pairs={{0,2},{1,3},{2,0},{3,1},{4,6},{5,7},{6,4},{7,5},{8,10},{9,11},{10,... | collective-permute-start | bytes 196616 | tf_op jit(solution)/shard_map/ppermute | solution.py:577
  26.3 4.0 %collective-permute-start = (f32[64,256]{1,0:T(8,128)S(1)}, f32[64,256]{1,0:T(8,128)S(1)}, u32[]{:S(2)}, u32[]{:S(2)}) collective-permute-start(f32[64,256]{1,0:T(8,128)S(1)} %get-tuple-element.32.refs_0_), channel_id=1, source_target_pairs={{0,1},{1,0},{2,3},{3,2},{4,5},{5,4},{6,7},{7,6},{8,9},{9,8},{10,11... | collective-permute-start | bytes 196616 | tf_op jit(solution)/shard_map/ppermute | solution.py:577
  53.8 3.1 %collective-permute-start.5 = (f32[16,128]{1,0:T(8,128)S(1)}, f32[16,128]{1,0:T(8,128)S(1)}, u32[]{:S(2)}, u32[]{:S(2)}) collective-permute-start(f32[16,128]{1,0:T(8,128)S(1)} %adjoint.1), channel_id=1, source_target_pairs={{0,3},{1,2},{2,1},{3,0},{4,7},{5,6},{6,5},{7,4},{8,11},{9,10},{10,... | collective-permute-start | bytes 24584 | tf_op jit(solution)/shard_map/ppermute | solution.py:577
  55.2 3.7 %collective-permute-start.4 = (f32[16,128]{1,0:T(8,128)S(1)}, f32[16,128]{1,0:T(8,128)S(1)}, u32[]{:S(2)}, u32[]{:S(2)}) collective-permute-start(f32[16,128]{1,0:T(8,128)S(1)} %adjoint.1), channel_id=1, source_target_pairs={{0,2},{1,3},{2,0},{3,1},{4,6},{5,7},{6,4},{7,5},{8,10},{9,11},{10,... | collective-permute-start | bytes 24584 | tf_op jit(solution)/shard_map/ppermute | solution.py:577
  55.9 3.0 %collective-permute-start.3 = (f32[16,128]{1,0:T(8,128)S(1)}, f32[16,128]{1,0:T(8,128)S(1)}, u32[]{:S(2)}, u32[]{:S(2)}) collective-permute-start(f32[16,128]{1,0:T(8,128)S(1)} %adjoint.1), channel_id=1, source_target_pairs={{0,1},{1,0},{2,3},{3,2},{4,5},{5,4},{6,7},{7,6},{8,9},{9,8},{10,11... | collective-permute-start | bytes 24584 | tf_op jit(solution)/shard_map/ppermute | solution.py:577
  58.9 4.6 %collective-permute-start.8 = (f32[16,128]{1,0:T(8,128)S(1)}, f32[16,128]{1,0:T(8,128)S(1)}, u32[]{:S(2)}, u32[]{:S(2)}) collective-permute-start(f32[16,128]{1,0:T(8,128)S(1)} %add_add_fusion.1), channel_id=1, source_target_pairs={{0,12},{4,8},{8,4},{12,0},{16,28},{20,24},{24,20},{28,16},{1,13},{... | collective-permute-start | bytes 24584 | tf_op jit(solution)/shard_map/ppermute | solution.py:577
  61.5 3.7 %collective-permute-start.7 = (f32[16,128]{1,0:T(8,128)S(1)}, f32[16,128]{1,0:T(8,128)S(1)}, u32[]{:S(2)}, u32[]{:S(2)}) collective-permute-start(f32[16,128]{1,0:T(8,128)S(1)} %add_add_fusion.1), channel_id=1, source_target_pairs={{0,8},{4,12},{8,0},{12,4},{16,24},{20,28},{24,16},{28,20},{1,9},{5... | collective-permute-start | bytes 24584 | tf_op jit(solution)/shard_map/ppermute | solution.py:577
  62.0 3.7 %collective-permute-start.6 = (f32[16,128]{1,0:T(8,128)S(1)}, f32[16,128]{1,0:T(8,128)S(1)}, u32[]{:S(2)}, u32[]{:S(2)}) collective-permute-start(f32[16,128]{1,0:T(8,128)S(1)} %add_add_fusion.1), channel_id=1, source_target_pairs={{0,4},{4,0},{8,12},{12,8},{16,20},{20,16},{24,28},{28,24},{1,5},{5... | collective-permute-start | bytes 24584 | tf_op jit(solution)/shard_map/ppermute | solution.py:577
  65.6 4.5 %collective-permute-start.9 = (f32[16,128]{1,0:T(8,128)S(1)}, f32[16,128]{1,0:T(8,128)S(1)}, u32[]{:S(2)}, u32[]{:S(2)}) collective-permute-start(f32[16,128]{1,0:T(8,128)S(1)} %add_add_fusion.refs_0_), channel_id=1, source_target_pairs={{0,16},{4,20},{8,24},{12,28},{16,0},{20,4},{24,8},{28,12},{1,17},{... | collective-permute-start | bytes 24584 | tf_op jit(solution)/shard_map/ppermute | solution.py:577

commit v2 on v1

--- a/solution.py
+++ b/solution.py
@@ -44,13 +44,6 @@
     low = jnp.where(mask, scale, 0.0).astype(x.dtype)
     high = jnp.where(mask, 0.0, scale).astype(x.dtype)
     return jnp.concatenate([x * low, x * high], axis=0)
-
-
-def two_blocks(pairs, zero):
-    return jnp.concatenate([
-        jnp.concatenate([spread(pairs[0]), zero], axis=1),
-        jnp.concatenate([zero, spread(pairs[1])], axis=1),
-    ], axis=0)
 
 
 def mxu(left, right):
@@ -240,31 +233,26 @@
     expand(jnp.where(low_half(), even, odd), dup_ref, store)
 
     def squarings(step, carry):
-        held = [first_ref[pl.ds(step * 8 + j, 64, stride=64), :] for j in range(8)]
-        zero = jnp.zeros((128, 128), BF)
+        width = 16
+        held = [first_ref[pl.ds(step * width + j, 64, stride=64), :] for j in range(width)]
         for level in range(4):
-            for j in range(0, 8, 2):
-                highs, lows = [], []
-                for t in range(2):
-                    high, low = split(held[j + t])
-                    chain_ref[level, 0, step * 8 + j + t] = high
-                    chain_ref[level, 1, step * 8 + j + t] = low
-                    highs.append(high)
-                    lows.append(low)
-                upper, lower = jnp.concatenate(highs, axis=1), jnp.concatenate(lows, axis=1)
-                one = mxu(jnp.concatenate([upper, lower], axis=0), two_blocks(highs, zero))
-                two = mxu(upper, two_blocks(lows, zero))
-                both = one[0:64] + one[64:128] + two
-                for t in range(2):
-                    held[j + t] = 2.0 * held[j + t] + both[:, 128 * t : 128 * t + 128]
-        for j in range(8):
-            p = step * 8 + j
+            for j in range(width):
+                high, low = split(held[j])
+                chain_ref[level, 0, step * width + j] = high
+                chain_ref[level, 1, step * width + j] = low
+                wide_high, wide_low = spread(high), spread(low)
+                held[j] = 2.0 * held[j] + mxu(
+                    jnp.concatenate([high, high, low], axis=1),
+                    jnp.concatenate([wide_high, wide_low, wide_high], axis=0),
+                )
+        for j in range(width):
+            p = step * width + j
             last_ref[p] = held[j]
             double(up_ref, p, inverse_root_col * (held[j] + twice) * root_row)
         return carry
 
     inverse_root_col = 1.0 / root_col
-    lax.fori_loop(0, PAIRS // 8, squarings, 0)
+    lax.fori_loop(0, PAIRS // 16, squarings, 0)
 
 
 def up_kernel(
@@ -288,8 +276,8 @@
     codon = lax.broadcasted_iota(jnp.int32, (64, sites), 0)
 
     def leaf_level(step, carry):
-        for j in range(4):
-            p = step * 4 + j
+        for j in range(8):
+            p = step * 8 + j
             both = []
             for e in range(2):
                 taxon = order_ref[subtree * LEAF_DEV + 2 * p + e]
@@ -303,7 +291,7 @@
             finish(p, [messages(up_ref[2 * p + e], both[e], nothing) for e in range(2)])
         return carry
 
-    lax.fori_loop(0, LEAF_DEV // 8, leaf_level, 0)
+    lax.fori_loop(0, LEAF_DEV // 16, leaf_level, 0)
 
     def inner(p):
         child = 2 * p - 64
@@ -311,12 +299,8 @@
             messages(up_ref[2 * p + e], high_ref[child + e], low_ref[child + e]) for e in range(2)
         ]
 
-    def second_level(step, carry):
-        for j in range(4):
-            finish(32 + step * 4 + j, inner(32 + step * 4 + j))
-        return carry
-
-    lax.fori_loop(0, 4, second_level, 0)
+    for p in range(32, 48):
+        finish(p, inner(p))
     for p in range(48, 63):
         finish(p, inner(p))
     high_ref[63] = jnp.zeros((64, sites), BF)
@@ -422,8 +406,8 @@
         inner(r)
 
     def leaf_level(step, carry):
-        for j in range(2):
-            r = 32 + step * 2 + j
+        for j in range(4):
+            r = 32 + step * 4 + j
             down = descend(r)
             for e in range(2):
                 p = 2 * r + e - 64
@@ -432,7 +416,7 @@
                 store_counts(p, square[:, 0:128] + square[:, 128:256])
         return carry
 
-    lax.fori_loop(0, 8, leaf_level, 0)
+    lax.fori_loop(0, 4, leaf_level, 0)
 
 
 def adjoint_kernel(
@@ -448,11 +432,11 @@
     inverse_root_row = 1.0 / root_row
 
     def adjoint(step, carry):
-        held = [count_ref[step * 8 + j] for j in range(8)]
+        held = [count_ref[step * 16 + j] for j in range(16)]
         for level in range(3, -1, -1):
-            for j in range(8):
+            for j in range(16):
                 high, low = split(held[j])
-                e_high, e_low = chain_ref[level, 0, step * 8 + j], chain_ref[level, 1, step * 8 + j]
+                e_high, e_low = chain_ref[level, 0, step * 16 + j], chain_ref[level, 1, step * 16 + j]
                 left = jnp.concatenate([
                     jnp.concatenate([high, e_high], axis=1),
                     jnp.concatenate([low, e_low], axis=1),
@@ -464,11 +448,11 @@
                 four = mxu(left, right)
                 four = four[0:64] + four[64:128]
                 held[j] = 2.0 * held[j] + four[:, 0:128] + four[:, 128:256]
-        for j in range(8):
-            back_ref[pl.ds(step * 8 + j, 64, stride=64), :] = held[j]
+        for j in range(16):
+            back_ref[pl.ds(step * 16 + j, 64, stride=64), :] = held[j]
         return carry
 
-    lax.fori_loop(0, PAIRS // 8, adjoint, 0)
+    lax.fori_loop(0, PAIRS // 16, adjoint, 0)
 
     left = four_left(turned_ref[...])
 

time: 71.3 us -> 64.2 us (0.900)
  Pallas kernels: 50.8 us -> 43.7 us
    pallas_call x1, Pallas kernels: 8.31 us -> 5.32 us  [body(): pl.pallas_call(up_kernel, out_shape=[shape((64, sites), F32), held((PAIRS...]
    pallas_call x1, Pallas kernels: 14.3 us -> 11.6 us  [body(): pl.pallas_call(matrix_kernel, out_shape=[held((4, 2, PAIRS, 64, 128), BF)...]
    pallas_call x1, Pallas kernels: 14.4 us -> 13.5 us  [body(): pl.pallas_call(functools.partial(adjoint_kernel, members), out_shape=shap...]
where the time goes in v2:
time: 64.2 us; the launch traced here: 63.9 us
  Pallas kernels  43.7 us (68%)
  starting transfers between devices  11.4 us (18%)
  waiting for transfers between devices  8.14 us (13%)
  between operations  0.68 us (1%)
    pallas_call x1, Pallas kernels, body(): pl.pallas_call(functools.partial(adjoint_kernel, members), out_shape=shap...  13.5 us
    pallas_call x1, Pallas kernels, body(): pl.pallas_call(matrix_kernel, out_shape=[held((4, 2, PAIRS, 64, 128), BF)...  11.6 us
    ppermute x10, starting transfers between devices, partners(): lax.ppermute(x, axis, [(i, i ^ step * start) for i in range(size)])  11.4 us
    pallas_call x1, Pallas kernels, body(): pl.pallas_call(functools.partial(down_kernel, total_sites, members), out_...  8.46 us
    ppermute x10, waiting for transfers between devices, partners(): lax.ppermute(x, axis, [(i, i ^ step * start) for i in range(size)])  8.14 us
    pallas_call x1, Pallas kernels, body(): pl.pallas_call(up_kernel, out_shape=[shape((64, sites), F32), held((PAIRS...  5.32 us
    pallas_call x1, Pallas kernels, body(): pl.pallas_call(side_kernel, out_shape=[held((PAIRS * 64, 128), F32), held...  3.96 us
  transfers between devices with their start and end apart: 10, of which 6 were waited for; matrix products, arithmetic and copies ran while one was open for 0% of the time, Pallas kernels for 6%

profile of v2, /device:TPU:0, one launch (start us, length us, event | category | flops | bytes accessed | tf_op | source)
XLA Modules:
  0.0 63.9 jit_solution(16680955985171037567)
XLA Ops:
  0.6 11.6 %matrices.1 = (bf16[4,2,64,64,128]{4,3,2,1,0:T(8,128)(2,1)S(1)}, f32[64,64,128]{2,1,0:T(8,128)S(1)}, bf16[128,64,256]{2,1,0:T(8,128)(2,1)S(1)}, f32[4,4,64,128]{3,2,1,0:T(8,128)S(1)}, f32[4096,128]{1,0:T(8,128)S(1)}) custom-call(f32[64,64]{1,0:T(8,128)} %ex_ref.3, f32[1,64]{1,0:T(1,128)} %bitcast.7, f32[8]{0:T(128)} %omega_ref.3, f32[1,127]{1,0:T(1,128)} %bitcast.11, ...), custom_call_target="tpu_custom_call" | custom-call | tf_op jit(solution)/shard_map/matrices/pallas_call | solution.py:608
  12.2 5.3 %up.1 = (f32[64,256]{1,0:T(8,128)S(1)}, f32[64,128,256]{2,1,0:T(8,128)S(1)}, bf16[64,64,256]{2,1,0:T(8,128)(2,1)S(1)}, bf16[64,64,256]{2,1,0:T(8,128)(2,1)S(1)},...) custom-call(s32[256,256]{1,0:T(8,128)} %states_ref.1, s32[256,256]{1,0:T(8,128)} %gap_ref.1, ...), custom_call_target="tpu_custom_call" | custom-call | tf_op jit(solution)/shard_map/up/pallas_call | solution.py:623
  17.5 2.4 %collective-permute-start.2 = (f32[64,256]{1,0:T(8,128)S(1)}, f32[64,256]{1,0:T(8,128)S(1)}, u32[]{:S(2)}, u32[]{:S(2)}) collective-permute-start(f32[64,256]{1,0:T(8,128)S(1)} %get-tuple-element.32.refs_0_), channel_id=1, source_target_pairs={{0,3},{1,2},{2,1},{3,0},{4,7},{5,6},{6,5},{7,4},{8,11},{9,10},{10,... | collective-permute-start | bytes 196616 | tf_op jit(solution)/shard_map/ppermute | solution.py:561
  20.0 0.6 collective-permute-start.1
  20.6 0.0 collective-permute-start
  20.7 4.0 %side.1 = (f32[4096,128]{1,0:T(8,128)S(1)}, bf16[64,64,256]{2,1,0:T(8,128)(2,1)S(1)}, f32[128,128]{1,0:T(8,128)S(1)}) custom-call(f32[4096,128]{1,0:T(8,128)S(1)} %get-tuple-element.26.dup_ref, f32[64,64,128]{2,1,0:T(8,128)S(1)} %get-tuple-element.27.last_ref, f32[1,127]{1,0:T(1,128)} %bitcast.12, s32[1,127]{1,0:T(1,128)} %bitcast.14, f32[1,64]{1,0:T(1,128)} %bitcast.8, ...), custom_call_target="tpu_custom_call" | custom-call | tf_op jit(solution)/shard_map/side/pallas_call | solution.py:641
  24.6 0.0 collective-permute-done.2.refs_3_
  24.6 0.0 collective-permute-done.1.refs_2_
  24.7 0.0 collective-permute-done.refs_1_
  24.7 8.5 %down.1 = (f32[64,64,128]{2,1,0:T(8,128)S(1)}, f32[8,128]{1,0:T(8,128)S(1)}) custom-call(f32[64,256]{1,0:T(8,128)S(1)} %get-tuple-element.32.refs_0_, f32[64,256]{1,0:T(8,128)S(1)} %collective-permute-done.refs_1_, f32[64,256]{1,0:T(8,128)S(1)} %collective-permute-done.1.refs_2_, f32[64,256]{1,0:T(8,128)S(1)} %collective-permute-done.2.refs_3_, ...), custom_call_target="tpu_custom_call" | custom-call | tf_op jit(solution)/shard_map/down/pallas_call | solution.py:653
  33.1 13.5 %adjoint.1 = f32[16,128]{1,0:T(8,128)S(1)} custom-call(bf16[4,2,64,64,128]{4,3,2,1,0:T(8,128)(2,1)S(1)} %get-tuple-element.25.chain_ref, f32[128,128]{1,0:T(8,128)S(1)} %get-tuple-element.28.turned_ref, f32[4096,128]{1,0:T(8,128)S(1)} %get-tuple-element.29.slope_ref, f32[4,4,64,128]{3,2,1,0:T(8,128)S(1)} %get-tuple-element.30.power_ref, ...), custom_call_target="tpu_custom_call" | custom-call | tf_op jit(solution)/shard_map/adjoint/pallas_call | solution.py:668
  46.7 1.5 %collective-permute-start.5 = (f32[16,128]{1,0:T(8,128)S(1)}, f32[16,128]{1,0:T(8,128)S(1)}, u32[]{:S(2)}, u32[]{:S(2)}) collective-permute-start(f32[16,128]{1,0:T(8,128)S(1)} %adjoint.1), channel_id=1, source_target_pairs={{0,3},{1,2},{2,1},{3,0},{4,7},{5,6},{6,5},{7,4},{8,11},{9,10},{10,... | collective-permute-start | bytes 24584 | tf_op jit(solution)/shard_map/ppermute | solution.py:561
  48.1 0.6 collective-permute-start.4
  48.8 0.0 collective-permute-start.3
  48.8 1.0 %collective-permute-done.5 = f32[16,128]{1,0:T(8,128)S(1)} collective-permute-done((f32[16,128]{1,0:T(8,128)S(1)}, f32[16,128]{1,0:T(8,128)S(1)}, u32[]{:S(2)}, u32[]{:S(2)}) %collective-permute-start.5) | collective-permute-done | bytes 8224 | tf_op jit(solution)/shard_map/ppermute | solution.py:561
  49.8 2.0 %collective-permute-done.4 = f32[16,128]{1,0:T(8,128)S(1)} collective-permute-done((f32[16,128]{1,0:T(8,128)S(1)}, f32[16,128]{1,0:T(8,128)S(1)}, u32[]{:S(2)}, u32[]{:S(2)}) %collective-permute-start.4) | collective-permute-done | bytes 8224 | tf_op jit(solution)/shard_map/ppermute | solution.py:561
  51.8 0.0 collective-permute-done.3
  51.8 2.6 %collective-permute-start.8 = (f32[16,128]{1,0:T(8,128)S(1)}, f32[16,128]{1,0:T(8,128)S(1)}, u32[]{:S(2)}, u32[]{:S(2)}) collective-permute-start(f32[16,128]{1,0:T(8,128)S(1)} %add_add_fusion.1), channel_id=1, source_target_pairs={{0,12},{4,8},{8,4},{12,0},{16,28},{20,24},{24,20},{28,16},{1,13},{... | collective-permute-start | bytes 24584 | tf_op jit(solution)/shard_map/ppermute | solution.py:561
  54.4 0.4 collective-permute-start.7
  54.9 0.5 collective-permute-start.6
  55.4 1.1 %collective-permute-done.8 = f32[16,128]{1,0:T(8,128)S(1)} collective-permute-done((f32[16,128]{1,0:T(8,128)S(1)}, f32[16,128]{1,0:T(8,128)S(1)}, u32[]{:S(2)}, u32[]{:S(2)}) %collective-permute-start.8) | collective-permute-done | bytes 8224 | tf_op jit(solution)/shard_map/ppermute | solution.py:561
  56.4 1.6 %collective-permute-done.7 = f32[16,128]{1,0:T(8,128)S(1)} collective-permute-done((f32[16,128]{1,0:T(8,128)S(1)}, f32[16,128]{1,0:T(8,128)S(1)}, u32[]{:S(2)}, u32[]{:S(2)}) %collective-permute-start.7) | collective-permute-done | bytes 8224 | tf_op jit(solution)/shard_map/ppermute | solution.py:561
  58.1 0.4 collective-permute-done.6
  58.5 2.6 %collective-permute-start.9 = (f32[16,128]{1,0:T(8,128)S(1)}, f32[16,128]{1,0:T(8,128)S(1)}, u32[]{:S(2)}, u32[]{:S(2)}) collective-permute-start(f32[16,128]{1,0:T(8,128)S(1)} %add_add_fusion.refs_0_), channel_id=1, source_target_pairs={{0,16},{4,20},{8,24},{12,28},{16,0},{20,4},{24,8},{28,12},{1,17},{... | collective-permute-start | bytes 24584 | tf_op jit(solution)/shard_map/ppermute | solution.py:561
  61.1 2.0 %collective-permute-done.9.refs_1_ = f32[16,128]{1,0:T(8,128)S(1)} collective-permute-done((f32[16,128]{1,0:T(8,128)S(1)}, f32[16,128]{1,0:T(8,128)S(1)}, u32[]{:S(2)}, u32[]{:S(2)}) %collective-permute-start.9) | collective-permute-done | bytes 8224 | tf_op jit(solution)/shard_map/ppermute | solution.py:561
  63.1 0.8 %last.1 = (f32[64,64]{1,0:T(8,128)}, f32[1,8]{1,0:T(1,128)}, f32[1,127]{1,0:T(1,128)}, f32[1,1]{1,0:T(1,128)}) custom-call(f32[16,128]{1,0:T(8,128)S(1)} %add_add_fusion.refs_0_, f32[16,128]{1,0:T(8,128)S(1)} %collective-permute-done.9.refs_1_), custom_call_target="tpu_custom_call" | custom-call | tf_op jit(solution)/shard_map/last/pallas_call | solution.py:687
  (2 shorter events, 0.0 us)
Async XLA Ops:
  17.5 7.1 %collective-permute-start.2 = (f32[64,256]{1,0:T(8,128)S(1)}, f32[64,256]{1,0:T(8,128)S(1)}, u32[]{:S(2)}, u32[]{:S(2)}) collective-permute-start(f32[64,256]{1,0:T(8,128)S(1)} %get-tuple-element.32.refs_0_), channel_id=1, source_target_pairs={{0,3},{1,2},{2,1},{3,0},{4,7},{5,6},{6,5},{7,4},{8,11},{9,10},{10,... | collective-permute-start | bytes 196616 | tf_op jit(solution)/shard_map/ppermute | solution.py:561
  20.0 4.7 %collective-permute-start.1 = (f32[64,256]{1,0:T(8,128)S(1)}, f32[64,256]{1,0:T(8,128)S(1)}, u32[]{:S(2)}, u32[]{:S(2)}) collective-permute-start(f32[64,256]{1,0:T(8,128)S(1)} %get-tuple-element.32.refs_0_), channel_id=1, source_target_pairs={{0,2},{1,3},{2,0},{3,1},{4,6},{5,7},{6,4},{7,5},{8,10},{9,11},{10,... | collective-permute-start | bytes 196616 | tf_op jit(solution)/shard_map/ppermute | solution.py:561
  20.6 4.0 %collective-permute-start = (f32[64,256]{1,0:T(8,128)S(1)}, f32[64,256]{1,0:T(8,128)S(1)}, u32[]{:S(2)}, u32[]{:S(2)}) collective-permute-start(f32[64,256]{1,0:T(8,128)S(1)} %get-tuple-element.32.refs_0_), channel_id=1, source_target_pairs={{0,1},{1,0},{2,3},{3,2},{4,5},{5,4},{6,7},{7,6},{8,9},{9,8},{10,11... | collective-permute-start | bytes 196616 | tf_op jit(solution)/shard_map/ppermute | solution.py:561
  46.7 3.1 %collective-permute-start.5 = (f32[16,128]{1,0:T(8,128)S(1)}, f32[16,128]{1,0:T(8,128)S(1)}, u32[]{:S(2)}, u32[]{:S(2)}) collective-permute-start(f32[16,128]{1,0:T(8,128)S(1)} %adjoint.1), channel_id=1, source_target_pairs={{0,3},{1,2},{2,1},{3,0},{4,7},{5,6},{6,5},{7,4},{8,11},{9,10},{10,... | collective-permute-start | bytes 24584 | tf_op jit(solution)/shard_map/ppermute | solution.py:561
  48.1 3.7 %collective-permute-start.4 = (f32[16,128]{1,0:T(8,128)S(1)}, f32[16,128]{1,0:T(8,128)S(1)}, u32[]{:S(2)}, u32[]{:S(2)}) collective-permute-start(f32[16,128]{1,0:T(8,128)S(1)} %adjoint.1), channel_id=1, source_target_pairs={{0,2},{1,3},{2,0},{3,1},{4,6},{5,7},{6,4},{7,5},{8,10},{9,11},{10,... | collective-permute-start | bytes 24584 | tf_op jit(solution)/shard_map/ppermute | solution.py:561
  48.8 3.0 %collective-permute-start.3 = (f32[16,128]{1,0:T(8,128)S(1)}, f32[16,128]{1,0:T(8,128)S(1)}, u32[]{:S(2)}, u32[]{:S(2)}) collective-permute-start(f32[16,128]{1,0:T(8,128)S(1)} %adjoint.1), channel_id=1, source_target_pairs={{0,1},{1,0},{2,3},{3,2},{4,5},{5,4},{6,7},{7,6},{8,9},{9,8},{10,11... | collective-permute-start | bytes 24584 | tf_op jit(solution)/shard_map/ppermute | solution.py:561
  51.8 4.6 %collective-permute-start.8 = (f32[16,128]{1,0:T(8,128)S(1)}, f32[16,128]{1,0:T(8,128)S(1)}, u32[]{:S(2)}, u32[]{:S(2)}) collective-permute-start(f32[16,128]{1,0:T(8,128)S(1)} %add_add_fusion.1), channel_id=1, source_target_pairs={{0,12},{4,8},{8,4},{12,0},{16,28},{20,24},{24,20},{28,16},{1,13},{... | collective-permute-start | bytes 24584 | tf_op jit(solution)/shard_map/ppermute | solution.py:561
  54.4 3.7 %collective-permute-start.7 = (f32[16,128]{1,0:T(8,128)S(1)}, f32[16,128]{1,0:T(8,128)S(1)}, u32[]{:S(2)}, u32[]{:S(2)}) collective-permute-start(f32[16,128]{1,0:T(8,128)S(1)} %add_add_fusion.1), channel_id=1, source_target_pairs={{0,8},{4,12},{8,0},{12,4},{16,24},{20,28},{24,16},{28,20},{1,9},{5... | collective-permute-start | bytes 24584 | tf_op jit(solution)/shard_map/ppermute | solution.py:561
  54.9 3.7 %collective-permute-start.6 = (f32[16,128]{1,0:T(8,128)S(1)}, f32[16,128]{1,0:T(8,128)S(1)}, u32[]{:S(2)}, u32[]{:S(2)}) collective-permute-start(f32[16,128]{1,0:T(8,128)S(1)} %add_add_fusion.1), channel_id=1, source_target_pairs={{0,4},{4,0},{8,12},{12,8},{16,20},{20,16},{24,28},{28,24},{1,5},{5... | collective-permute-start | bytes 24584 | tf_op jit(solution)/shard_map/ppermute | solution.py:561
  58.5 4.5 %collective-permute-start.9 = (f32[16,128]{1,0:T(8,128)S(1)}, f32[16,128]{1,0:T(8,128)S(1)}, u32[]{:S(2)}, u32[]{:S(2)}) collective-permute-start(f32[16,128]{1,0:T(8,128)S(1)} %add_add_fusion.refs_0_), channel_id=1, source_target_pairs={{0,16},{4,20},{8,24},{12,28},{16,0},{20,4},{24,8},{28,12},{1,17},{... | collective-permute-start | bytes 24584 | tf_op jit(solution)/shard_map/ppermute | solution.py:561

commit v3 on v2

--- a/solution.py
+++ b/solution.py
@@ -88,10 +88,14 @@
         ref[2 * p + e] = jnp.concatenate([high, low], axis=1)
 
 
-def frequencies(freq_ref, sense_ref):
+def identity_twice():
     row = lax.broadcasted_iota(jnp.int32, (64, 128), 0)
     lane = lax.broadcasted_iota(jnp.int32, (64, 128), 1)
-    twice = (row == lane % 64).astype(F32)
+    return (row == lane % 64).astype(F32)
+
+
+def frequencies(freq_ref, sense_ref):
+    twice = identity_twice()
     sense2 = sense_ref[...]
     freq2 = exact(jnp.broadcast_to(freq_ref[...], (8, 64)), twice)[0:1] * sense2
     total = 0.5 * jnp.sum(freq2, axis=1, keepdims=True)
@@ -176,8 +180,8 @@
     )
 
     def some(step, carry):
-        for j in range(4):
-            i = step * 8 + 2 * j
+        for j in range(16):
+            i = step * 32 + 2 * j
             parts = [split(dup_ref[rows_of(i + t, 64), :]) for t in range(2)]
             right = jnp.concatenate([
                 jnp.concatenate([spread(parts[0][h]), spread(parts[1][h])], axis=1)
@@ -189,22 +193,29 @@
                 store(i + t, both[:, 128 * t : 128 * t + 128])
         return carry
 
-    lax.fori_loop(0, 8, some, 0)
+    lax.fori_loop(0, 2, some, 0)
 
 
 def rows_of(step, width):
     return pl.ds(pl.multiple_of(step * width, width), width)
 
 
-def matrix_kernel(
+def up_kernel(
+    states_ref, gap_ref, order_ref,
     ex_ref, freq_ref, omega_ref, len_ref, cls_ref, sense_ref, single_ref, nonsyn_ref,
-    chain_ref, last_ref, up_ref, power_ref, dup_ref,
-    first_ref,
+    top_ref, chain_ref, last_ref, power_ref, dup_ref, fixed_ref,
+    message_ref, high_ref, low_ref, leaf_ref, scale_ref, inverse_ref,
+    first_ref, up_ref,
 ):
+    subtree = lax.axis_index("branch")
     mask = low_half()
     twice, pi_row, pi_col, root_row, root_col = frequencies(freq_ref, sense_ref)
     table = symmetric_table(ex_ref, single_ref, twice)
     nonsyn = nonsyn_ref[...]
+    for at, value in enumerate(
+        (pi_row, pi_col, root_row, root_col, 1.0 / root_row, 1.0 / root_col, table)
+    ):
+        fixed_ref[at] = jnp.broadcast_to(value, (64, 128))
 
     powers = []
     for pair in range(CLASSES // 2):
@@ -254,13 +265,6 @@
     inverse_root_col = 1.0 / root_col
     lax.fori_loop(0, PAIRS // 16, squarings, 0)
 
-
-def up_kernel(
-    states_ref, gap_ref, order_ref, up_ref,
-    top_ref, message_ref, high_ref, low_ref, leaf_ref, scale_ref, inverse_ref,
-):
-    subtree = lax.axis_index("branch")
-
     def finish(p, message):
         message_ref[p] = jnp.concatenate(message, axis=0)
         raw = message[0] * message[1]
@@ -313,9 +317,9 @@
 
 
 def side_kernel(
-    dup_ref, last_ref, len_ref, cls_ref, freq_ref, sense_ref, slope_ref, matrix_ref, turned_ref,
+    dup_ref, last_ref, len_ref, cls_ref, fixed_ref, slope_ref, matrix_ref, turned_ref,
 ):
-    twice, pi_row, pi_col, root_row, root_col = frequencies(freq_ref, sense_ref)
+    twice = identity_twice()
     even, odd = coefficients(len_ref, cls_ref, True)
 
     def store(i, value):
@@ -324,7 +328,7 @@
     expand(jnp.where(low_half(), even, odd), dup_ref, store)
     even, odd = coefficients(len_ref, cls_ref, False)
     turned_ref[...] = exact_tn(jnp.where(low_half(), even, odd), twice)
-    inverse_root_row = 1.0 / root_row
+    root_col, inverse_root_row = fixed_ref[3], fixed_ref[4]
 
     def matrices(step, carry):
         for j in range(8):
@@ -339,25 +343,26 @@
     tops = refs[:members]
     (
         matrix_ref, message_ref, high_ref, low_ref, leaf_ref, scale_ref, inverse_ref,
-        weights_ref, freq_ref, sense_ref,
-        count_ref, log_ref,
-        a_high_ref, a_low_ref,
+        chain_ref, turned_ref, slope_ref, power_ref, fixed_ref,
+        weights_ref, omega_ref, single_ref, nonsyn_ref,
+        out_ref,
+        a_high_ref, a_low_ref, count_ref, back_ref, bins_ref,
     ) = refs[members:]
     subtree = lax.axis_index("branch")
     mask = low_half()
-    twice, pi_row, pi_col, root_row, root_col = frequencies(freq_ref, sense_ref)
-    inverse_root_row, inverse_root_col = 1.0 / root_row, 1.0 / root_col
+    twice = identity_twice()
+    pi_row, pi_col, root_col, inverse_root_row = [fixed_ref[at] for at in (0, 1, 3, 4)]
     sites = weights_ref.shape[1]
     weight = weights_ref[...].astype(F32)
 
-    above = jnp.broadcast_to(pi_col, (64, sites))
+    above = jnp.broadcast_to(pi_col[:, 0:1], (64, sites))
     for other in tops[1:]:
         above = above * other[...]
     own = tops[0][...]
     likelihood = jnp.sum(above * own, axis=0, keepdims=True)
     logs = jnp.sum(jnp.log(scale_ref[...]), axis=0, keepdims=True)
     logs = logs + jnp.where(subtree == 0, jnp.log(likelihood), 0.0)
-    log_ref[...] = jnp.broadcast_to(jnp.sum(weight * logs, axis=1, keepdims=True), (8, 128))
+    log_part = jnp.sum(weight * logs, axis=1, keepdims=True)
     high, low = split(above * (weight / (likelihood * total_sites)))
     a_high_ref[31, 0:64, :] = high
     a_low_ref[31, 0:64, :] = low
@@ -418,18 +423,6 @@
 
     lax.fori_loop(0, 4, leaf_level, 0)
 
-
-def adjoint_kernel(
-    members,
-    chain_ref, turned_ref, slope_ref, power_ref, count_ref, log_ref, ex_ref, freq_ref, omega_ref,
-    sense_ref, single_ref, nonsyn_ref,
-    out_ref,
-    back_ref, bins_ref,
-):
-    subtree = lax.axis_index("branch")
-    mask = low_half()
-    twice, pi_row, pi_col, root_row, root_col = frequencies(freq_ref, sense_ref)
-    inverse_root_row = 1.0 / root_row
 
     def adjoint(step, carry):
         held = [count_ref[step * 16 + j] for j in range(16)]
@@ -457,8 +450,8 @@
     left = four_left(turned_ref[...])
 
     def sums(step, total):
-        for j in range(4):
-            ats = [rows_of(step * 8 + 2 * j + t, 64) for t in range(2)]
+        for j in range(16):
+            ats = [rows_of(step * 32 + 2 * j + t, 64) for t in range(2)]
             values = [back_ref[at, :] for at in ats]
             both = mxu(left, four_right(jnp.concatenate(values, axis=1)))
             for t in range(2):
@@ -467,10 +460,9 @@
                 bins_ref[ats[t], :] = jnp.where(mask, here[0:64], here[64:128])
         return total
 
-    slopes = lax.fori_loop(0, 8, sums, jnp.zeros((64, 128), F32)) * 0.0625
-
-    table = symmetric_table(ex_ref, single_ref, twice)
-    nonsyn = nonsyn_ref[...]
+    slopes = lax.fori_loop(0, 2, sums, jnp.zeros((64, 128), F32)) * 0.0625
+
+    table, nonsyn = fixed_ref[6], nonsyn_ref[...]
     row = lax.broadcasted_iota(jnp.int32, (64, 128), 0)
     lane = lax.broadcasted_iota(jnp.int32, (64, 128), 1)
     table_grad = jnp.zeros((64, 128), F32)
@@ -518,12 +510,11 @@
         omega_row = jnp.where(lane_row == 2 * pair, ratio0, omega_row)
         omega_row = jnp.where(lane_row == 2 * pair + 1, ratio1, omega_row)
     table_grad = table_grad + pltpu.roll(table_grad, 64, 1)
-    one = table_grad[:, 0:64]
-    both = 0.5 * (exact(one, twice) + exact_tn(one, twice))
     masks, picks = neighbours()
     packed = jnp.zeros((16, 128), F32)
     for at_position, pick in zip(masks, picks):
-        packed = packed + exact_tn(pick, jnp.where(at_position, both, 0.0))
+        some = jnp.where(at_position, 0.5 * table_grad, 0.0)
+        packed = packed + exact_tn(pick, some) + exact_tn(pick, exact_tn(some[:, 0:64], twice))
     packed = jnp.where(lax.broadcasted_iota(jnp.int32, (16, 128), 1) < 64, packed, 0.0)
 
     even = jnp.sum(jnp.where(mask, slopes, 0.0), axis=1, keepdims=True)
@@ -531,7 +522,7 @@
     placed = jnp.where(lane == 2 * row, even, 0.0) + jnp.where(lane == 2 * row + 1, other, 0.0)
     length_row = jnp.sum(placed, axis=0, keepdims=True)
     line = lax.broadcasted_iota(jnp.int32, out_ref.shape, 0)
-    omega_row = jnp.where(lane_row == CLASSES, log_ref[0:1, :], omega_row)
+    omega_row = jnp.where(lane_row == CLASSES, log_part, omega_row)
     omega_row = pltpu.roll(jnp.broadcast_to(omega_row, (8, 128)), 64, 1)[0:1]
     packed = packed + jnp.where(line == 0, omega_row, 0.0)
     out_ref[...] = packed + jnp.where(line == 12 + subtree, length_row, 0.0)
@@ -573,10 +564,10 @@
 def axis_steps(axis):
     size, start, steps = lax.axis_size(axis), 1, []
     while start < size:
-        radix = min(4, size // start)
+        radix = 2 if size // start in (2, 8) else 4
         steps.append((axis, start, radix))
         start *= radix
-    return steps
+    return steps[::-1]
 
 
 def body(
@@ -605,25 +596,15 @@
     span, owner = outside(lengths.reshape(1, EDGES)), outside(classes.reshape(1, EDGES))
     table, omega = outside(exchanges), outside(omega_ratio)
 
-    chain, last, up, powers, dup = inside(pl.pallas_call(
-        matrix_kernel,
-        out_shape=[
-            held((4, 2, PAIRS, 64, 128), BF),
-            held((PAIRS, 64, 128), F32),
-            held((2 * PAIRS, 64, 256), BF),
-            held((CLASSES // 2, 4, 64, 128), F32),
-            held((ORDER * CLASSES * 64, 128), F32),
-        ],
-        in_specs=[vmem, vmem, smem] + [vmem] * 5,
-        out_specs=[vmem] * 5,
-        scratch_shapes=[pltpu.VMEM((PAIRS * 64, 128), F32)],
-        compiler_params=limit,
-        name="matrices",
-    )(table, freq, omega, span, owner, sense2, single2, nonsyn2))
     top, *kept = pl.pallas_call(
         up_kernel,
         out_shape=[
             shape((64, sites), F32),
+            held((4, 2, PAIRS, 64, 128), BF),
+            held((PAIRS, 64, 128), F32),
+            held((CLASSES // 2, 4, 64, 128), F32),
+            held((ORDER * CLASSES * 64, 128), F32),
+            held((7, 64, 128), F32),
             held((PAIRS, 128, sites), F32),
             held((64, 64, sites), BF),
             held((64, 64, sites), BF),
@@ -631,12 +612,21 @@
             held((64, sites), F32),
             held((64, sites), F32),
         ],
-        in_specs=[vmem, vmem, smem, vmem],
-        out_specs=[vmem] * 7,
+        in_specs=[vmem, vmem, smem, vmem, vmem, smem] + [vmem] * 5,
+        out_specs=[vmem] * 12,
+        scratch_shapes=[
+            pltpu.VMEM((PAIRS * 64, 128), F32),
+            pltpu.VMEM((2 * PAIRS, 64, 256), BF),
+        ],
         compiler_params=limit,
         name="up",
-    )(outside(states), outside(gap_mask), outside(leaf_order), up)
-    message, high, low, leaf, scale, inverse = inside(kept)
+    )(
+        outside(states), outside(gap_mask), outside(leaf_order),
+        table, freq, omega, span, owner, sense2, single2, nonsyn2,
+    )
+    (
+        chain, last, powers, dup, fixed, message, high, low, leaf, scale, inverse,
+    ) = inside(kept)
     tops = partners(top, "branch", 1, members)
     slope, matrix, turned = inside(pl.pallas_call(
         side_kernel,
@@ -645,40 +635,29 @@
             held((64, 64, 256), BF),
             held((128, 128), F32),
         ],
-        in_specs=[vmem] * 6,
+        in_specs=[vmem] * 5,
         out_specs=[vmem] * 3,
         compiler_params=limit,
         name="side",
-    )(dup, last, span, owner, freq, sense2))
-    counts, logs = inside(pl.pallas_call(
+    )(dup, last, span, owner, fixed))
+    part = pl.pallas_call(
         functools.partial(down_kernel, total_sites, members),
-        out_shape=[held((PAIRS, 64, 128), F32), held((8, 128), F32)],
-        in_specs=[vmem] * (10 + members),
-        out_specs=[vmem] * 2,
+        out_shape=shape((16, 128), F32),
+        in_specs=[vmem] * (13 + members) + [smem, vmem, vmem],
+        out_specs=vmem,
         scratch_shapes=[
             pltpu.VMEM((32, 128, sites), BF),
             pltpu.VMEM((32, 128, sites), BF),
+            pltpu.VMEM((PAIRS, 64, 128), F32),
+            pltpu.VMEM((PAIRS * 64, 128), F32),
+            pltpu.VMEM((64 * 64, 128), F32),
         ],
         compiler_params=limit,
         name="down",
     )(
         *tops, matrix, message, high, low, leaf, scale, inverse,
-        outside(weights.reshape(1, sites)), freq, sense2,
-    ))
-    part = pl.pallas_call(
-        functools.partial(adjoint_kernel, members),
-        out_shape=shape((16, 128), F32),
-        in_specs=[vmem] * 8 + [smem] + [vmem] * 3,
-        out_specs=vmem,
-        scratch_shapes=[
-            pltpu.VMEM((PAIRS * 64, 128), F32),
-            pltpu.VMEM((64 * 64, 128), F32),
-        ],
-        compiler_params=limit,
-        name="adjoint",
-    )(
-        chain, turned, slope, powers, counts, logs, table, freq, omega,
-        sense2, single2, nonsyn2,
+        chain, turned, slope, powers, fixed,
+        outside(weights.reshape(1, sites)), omega, single2, nonsyn2,
     )
     steps = axis_steps("branch") + axis_steps("site")
     for step in steps[:-1]:

time: 64.2 us -> 61 us (0.950)
  Pallas kernels: 43.7 us -> 38.7 us
  waiting for transfers between devices: 8.14 us -> 10.3 us
    pallas_call x3 -> x1, Pallas kernels: 30.4 us -> 15.1 us  [body(): pl.pallas_call(up_kernel, out_shape=[shape((64, sites), F32), held((4, 2,...]
    pallas_call x1, Pallas kernels: 8.46 us -> 20.1 us  [body(): pl.pallas_call(functools.partial(down_kernel, total_sites, members), out_...]
    ppermute x10, waiting for transfers between devices: 8.14 us -> 10.3 us  [partners(): lax.ppermute(x, axis, [(i, i ^ step * start) for i in range(size)])]
    pallas_call x1, Pallas kernels: 3.96 us -> 2.74 us  [body(): pl.pallas_call(side_kernel, out_shape=[held((PAIRS * 64, 128), F32), held...]
  transfers between devices with their start and end apart: 10 -> 10, of which waited for: 6 -> 6; matrix products, arithmetic and copies ran while one was open for 0% -> 0% of each run, Pallas kernels for 6% -> 5%
where the time goes in v3:
time: 61 us; the launch traced here: 60.8 us
  Pallas kernels  38.7 us (63%)
  starting transfers between devices  11 us (18%)
  waiting for transfers between devices  10.3 us (17%)
  between operations  0.67 us (1%)
    pallas_call x1, Pallas kernels, body(): pl.pallas_call(functools.partial(down_kernel, total_sites, members), out_...  20.1 us
    pallas_call x1, Pallas kernels, body(): pl.pallas_call(up_kernel, out_shape=[shape((64, sites), F32), held((4, 2,...  15.1 us
    ppermute x10, starting transfers between devices, partners(): lax.ppermute(x, axis, [(i, i ^ step * start) for i in range(size)])  11 us
    ppermute x10, waiting for transfers between devices, partners(): lax.ppermute(x, axis, [(i, i ^ step * start) for i in range(size)])  10.3 us
    pallas_call x1, Pallas kernels, body(): pl.pallas_call(side_kernel, out_shape=[held((PAIRS * 64, 128), F32), held...  2.74 us
  transfers between devices with their start and end apart: 10, of which 6 were waited for; matrix products, arithmetic and copies ran while one was open for 0% of the time, Pallas kernels for 5%

profile of v3, /device:TPU:0, one launch (start us, length us, event | category | flops | bytes accessed | tf_op | source)
XLA Modules:
  0.0 60.8 jit_solution(9288141976345317675)
XLA Ops:
  0.6 15.1 %up.1 = (f32[64,256]{1,0:T(8,128)S(1)}, bf16[4,2,64,64,128]{4,3,2,1,0:T(8,128)(2,1)S(1)}, f32[64,64,128]{2,1,0:T(8,128)S(1)}, f32[4,4,64,128]{3,2,1,0:T(8,128)S(...) custom-call(s32[256,256]{1,0:T(8,128)} %states_ref.1, ...), custom_call_target="tpu_custom_call" | custom-call | tf_op jit(solution)/shard_map/up/pallas_call | solution.py:599
  15.7 2.4 %collective-permute-start.2 = (f32[64,256]{1,0:T(8,128)S(1)}, f32[64,256]{1,0:T(8,128)S(1)}, u32[]{:S(2)}, u32[]{:S(2)}) collective-permute-start(f32[64,256]{1,0:T(8,128)S(1)} %get-tuple-element.23.refs_0_), channel_id=1, source_target_pairs={{0,3},{1,2},{2,1},{3,0},{4,7},{5,6},{6,5},{7,4},{8,11},{9,10},{10,... | collective-permute-start | bytes 196616 | tf_op jit(solution)/shard_map/ppermute | solution.py:552
  18.2 0.6 %collective-permute-start.1 = (f32[64,256]{1,0:T(8,128)S(1)}, f32[64,256]{1,0:T(8,128)S(1)}, u32[]{:S(2)}, u32[]{:S(2)}) collective-permute-start(f32[64,256]{1,0:T(8,128)S(1)} %get-tuple-element.23.refs_0_), channel_id=1, source_target_pairs={{0,2},{1,3},{2,0},{3,1},{4,6},{5,7},{6,4},{7,5},{8,10},{9,11},{10,... | collective-permute-start | bytes 196616 | tf_op jit(solution)/shard_map/ppermute | solution.py:552
  18.8 0.0 collective-permute-start
  18.9 2.7 %side.1 = (f32[4096,128]{1,0:T(8,128)S(1)}, bf16[64,64,256]{2,1,0:T(8,128)(2,1)S(1)}, f32[128,128]{1,0:T(8,128)S(1)}) custom-call(f32[4096,128]{1,0:T(8,128)S(1)} %get-tuple-element.24.dup_ref, f32[64,64,128]{2,1,0:T(8,128)S(1)} %get-tuple-element.25.last_ref, f32[1,127]{1,0:T(1,128)} %bitcast.8, s32[1,127]{1,0:T(1,128)} %bitcast.10, ...), custom_call_target="tpu_custom_call" | custom-call | tf_op jit(solution)/shard_map/side/pallas_call | solution.py:631
  21.6 0.0 collective-permute-done.2.refs_3_
  21.6 1.2 %collective-permute-done.1.refs_2_ = f32[64,256]{1,0:T(8,128)S(1)} collective-permute-done((f32[64,256]{1,0:T(8,128)S(1)}, f32[64,256]{1,0:T(8,128)S(1)}, u32[]{:S(2)}, u32[]{:S(2)}) %collective-permute-start.1) | collective-permute-done | bytes 65568 | tf_op jit(solution)/shard_map/ppermute | solution.py:552
  22.8 0.0 collective-permute-done.refs_1_
  22.8 20.1 %down.1 = f32[16,128]{1,0:T(8,128)S(1)} custom-call(f32[64,256]{1,0:T(8,128)S(1)} %get-tuple-element.23.refs_0_, f32[64,256]{1,0:T(8,128)S(1)} %collective-permute-done.refs_1_, f32[64,256]{1,0:T(8,128)S(1)} %collective-permute-done.1.refs_2_, f32[64,256]{1,0:T(8,128)S(1)} %collective-permute-done.2.refs_3_, ...), custom_call_target="tpu_custom_call" | custom-call | tf_op jit(solution)/shard_map/down/pallas_call | solution.py:643
  42.9 1.4 %collective-permute-start.5 = (f32[16,128]{1,0:T(8,128)S(1)}, f32[16,128]{1,0:T(8,128)S(1)}, u32[]{:S(2)}, u32[]{:S(2)}) collective-permute-start(f32[16,128]{1,0:T(8,128)S(1)} %down.1), channel_id=1, source_target_pairs={{0,3},{1,2},{2,1},{3,0},{4,7},{5,6},{6,5},{7,4},{8,11},{9,10},{10,... | collective-permute-start | bytes 24584 | tf_op jit(solution)/shard_map/ppermute | solution.py:552
  44.3 0.3 collective-permute-start.4
  44.6 0.1 collective-permute-start.3
  44.8 1.2 %collective-permute-done.5 = f32[16,128]{1,0:T(8,128)S(1)} collective-permute-done((f32[16,128]{1,0:T(8,128)S(1)}, f32[16,128]{1,0:T(8,128)S(1)}, u32[]{:S(2)}, u32[]{:S(2)}) %collective-permute-start.5) | collective-permute-done | bytes 8224 | tf_op jit(solution)/shard_map/ppermute | solution.py:552
  46.0 2.0 %collective-permute-done.4 = f32[16,128]{1,0:T(8,128)S(1)} collective-permute-done((f32[16,128]{1,0:T(8,128)S(1)}, f32[16,128]{1,0:T(8,128)S(1)}, u32[]{:S(2)}, u32[]{:S(2)}) %collective-permute-start.4) | collective-permute-done | bytes 8224 | tf_op jit(solution)/shard_map/ppermute | solution.py:552
  48.0 0.0 collective-permute-done.3
  48.0 3.7 %collective-permute-start.8 = (f32[16,128]{1,0:T(8,128)S(1)}, f32[16,128]{1,0:T(8,128)S(1)}, u32[]{:S(2)}, u32[]{:S(2)}) collective-permute-start(f32[16,128]{1,0:T(8,128)S(1)} %add_add_fusion.1), channel_id=1, source_target_pairs={{0,24},{4,28},{8,16},{12,20},{16,8},{20,12},{24,0},{28,4},{1,25},{... | collective-permute-start | bytes 24584 | tf_op jit(solution)/shard_map/ppermute | solution.py:552
  51.6 0.0 collective-permute-start.7
  51.6 0.8 %collective-permute-start.6 = (f32[16,128]{1,0:T(8,128)S(1)}, f32[16,128]{1,0:T(8,128)S(1)}, u32[]{:S(2)}, u32[]{:S(2)}) collective-permute-start(f32[16,128]{1,0:T(8,128)S(1)} %add_add_fusion.1), channel_id=1, source_target_pairs={{0,8},{4,12},{8,0},{12,4},{16,24},{20,28},{24,16},{28,20},{1,9},{5... | collective-permute-start | bytes 24584 | tf_op jit(solution)/shard_map/ppermute | solution.py:552
  52.4 1.1 %collective-permute-done.8 = f32[16,128]{1,0:T(8,128)S(1)} collective-permute-done((f32[16,128]{1,0:T(8,128)S(1)}, f32[16,128]{1,0:T(8,128)S(1)}, u32[]{:S(2)}, u32[]{:S(2)}) %collective-permute-start.8) | collective-permute-done | bytes 8224 | tf_op jit(solution)/shard_map/ppermute | solution.py:552
  53.5 2.7 %collective-permute-done.7 = f32[16,128]{1,0:T(8,128)S(1)} collective-permute-done((f32[16,128]{1,0:T(8,128)S(1)}, f32[16,128]{1,0:T(8,128)S(1)}, u32[]{:S(2)}, u32[]{:S(2)}) %collective-permute-start.7) | collective-permute-done | bytes 8224 | tf_op jit(solution)/shard_map/ppermute | solution.py:552
  56.2 0.0 collective-permute-done.6
  56.2 1.6 %collective-permute-start.9 = (f32[16,128]{1,0:T(8,128)S(1)}, f32[16,128]{1,0:T(8,128)S(1)}, u32[]{:S(2)}, u32[]{:S(2)}) collective-permute-start(f32[16,128]{1,0:T(8,128)S(1)} %add_add_fusion.refs_0_), channel_id=1, source_target_pairs={{0,4},{4,0},{8,12},{12,8},{16,20},{20,16},{24,28},{28,24},{1,5},{5... | collective-permute-start | bytes 24584 | tf_op jit(solution)/shard_map/ppermute | solution.py:552
  57.8 2.1 %collective-permute-done.9.refs_1_ = f32[16,128]{1,0:T(8,128)S(1)} collective-permute-done((f32[16,128]{1,0:T(8,128)S(1)}, f32[16,128]{1,0:T(8,128)S(1)}, u32[]{:S(2)}, u32[]{:S(2)}) %collective-permute-start.9) | collective-permute-done | bytes 8224 | tf_op jit(solution)/shard_map/ppermute | solution.py:552
  59.9 0.8 %last.1 = (f32[64,64]{1,0:T(8,128)}, f32[1,8]{1,0:T(1,128)}, f32[1,127]{1,0:T(1,128)}, f32[1,1]{1,0:T(1,128)}) custom-call(f32[16,128]{1,0:T(8,128)S(1)} %add_add_fusion.refs_0_, f32[16,128]{1,0:T(8,128)S(1)} %collective-permute-done.9.refs_1_), custom_call_target="tpu_custom_call" | custom-call | tf_op jit(solution)/shard_map/last/pallas_call | solution.py:666
  (2 shorter events, 0.0 us)
Async XLA Ops:
  15.7 5.9 %collective-permute-start.2 = (f32[64,256]{1,0:T(8,128)S(1)}, f32[64,256]{1,0:T(8,128)S(1)}, u32[]{:S(2)}, u32[]{:S(2)}) collective-permute-start(f32[64,256]{1,0:T(8,128)S(1)} %get-tuple-element.23.refs_0_), channel_id=1, source_target_pairs={{0,3},{1,2},{2,1},{3,0},{4,7},{5,6},{6,5},{7,4},{8,11},{9,10},{10,... | collective-permute-start | bytes 196616 | tf_op jit(solution)/shard_map/ppermute | solution.py:552
  18.2 4.7 %collective-permute-start.1 = (f32[64,256]{1,0:T(8,128)S(1)}, f32[64,256]{1,0:T(8,128)S(1)}, u32[]{:S(2)}, u32[]{:S(2)}) collective-permute-start(f32[64,256]{1,0:T(8,128)S(1)} %get-tuple-element.23.refs_0_), channel_id=1, source_target_pairs={{0,2},{1,3},{2,0},{3,1},{4,6},{5,7},{6,4},{7,5},{8,10},{9,11},{10,... | collective-permute-start | bytes 196616 | tf_op jit(solution)/shard_map/ppermute | solution.py:552
  18.8 4.0 %collective-permute-start = (f32[64,256]{1,0:T(8,128)S(1)}, f32[64,256]{1,0:T(8,128)S(1)}, u32[]{:S(2)}, u32[]{:S(2)}) collective-permute-start(f32[64,256]{1,0:T(8,128)S(1)} %get-tuple-element.23.refs_0_), channel_id=1, source_target_pairs={{0,1},{1,0},{2,3},{3,2},{4,5},{5,4},{6,7},{7,6},{8,9},{9,8},{10,11... | collective-permute-start | bytes 196616 | tf_op jit(solution)/shard_map/ppermute | solution.py:552
  42.9 3.1 %collective-permute-start.5 = (f32[16,128]{1,0:T(8,128)S(1)}, f32[16,128]{1,0:T(8,128)S(1)}, u32[]{:S(2)}, u32[]{:S(2)}) collective-permute-start(f32[16,128]{1,0:T(8,128)S(1)} %down.1), channel_id=1, source_target_pairs={{0,3},{1,2},{2,1},{3,0},{4,7},{5,6},{6,5},{7,4},{8,11},{9,10},{10,... | collective-permute-start | bytes 24584 | tf_op jit(solution)/shard_map/ppermute | solution.py:552
  44.3 3.7 %collective-permute-start.4 = (f32[16,128]{1,0:T(8,128)S(1)}, f32[16,128]{1,0:T(8,128)S(1)}, u32[]{:S(2)}, u32[]{:S(2)}) collective-permute-start(f32[16,128]{1,0:T(8,128)S(1)} %down.1), channel_id=1, source_target_pairs={{0,2},{1,3},{2,0},{3,1},{4,6},{5,7},{6,4},{7,5},{8,10},{9,11},{10,... | collective-permute-start | bytes 24584 | tf_op jit(solution)/shard_map/ppermute | solution.py:552
  44.6 3.3 %collective-permute-start.3 = (f32[16,128]{1,0:T(8,128)S(1)}, f32[16,128]{1,0:T(8,128)S(1)}, u32[]{:S(2)}, u32[]{:S(2)}) collective-permute-start(f32[16,128]{1,0:T(8,128)S(1)} %down.1), channel_id=1, source_target_pairs={{0,1},{1,0},{2,3},{3,2},{4,5},{5,4},{6,7},{7,6},{8,9},{9,8},{10,11... | collective-permute-start | bytes 24584 | tf_op jit(solution)/shard_map/ppermute | solution.py:552
  48.0 5.5 %collective-permute-start.8 = (f32[16,128]{1,0:T(8,128)S(1)}, f32[16,128]{1,0:T(8,128)S(1)}, u32[]{:S(2)}, u32[]{:S(2)}) collective-permute-start(f32[16,128]{1,0:T(8,128)S(1)} %add_add_fusion.1), channel_id=1, source_target_pairs={{0,24},{4,28},{8,16},{12,20},{16,8},{20,12},{24,0},{28,4},{1,25},{... | collective-permute-start | bytes 24584 | tf_op jit(solution)/shard_map/ppermute | solution.py:552
  51.6 4.5 %collective-permute-start.7 = (f32[16,128]{1,0:T(8,128)S(1)}, f32[16,128]{1,0:T(8,128)S(1)}, u32[]{:S(2)}, u32[]{:S(2)}) collective-permute-start(f32[16,128]{1,0:T(8,128)S(1)} %add_add_fusion.1), channel_id=1, source_target_pairs={{0,16},{4,20},{8,24},{12,28},{16,0},{20,4},{24,8},{28,12},{1,17},{... | collective-permute-start | bytes 24584 | tf_op jit(solution)/shard_map/ppermute | solution.py:552
  51.6 4.5 %collective-permute-start.6 = (f32[16,128]{1,0:T(8,128)S(1)}, f32[16,128]{1,0:T(8,128)S(1)}, u32[]{:S(2)}, u32[]{:S(2)}) collective-permute-start(f32[16,128]{1,0:T(8,128)S(1)} %add_add_fusion.1), channel_id=1, source_target_pairs={{0,8},{4,12},{8,0},{12,4},{16,24},{20,28},{24,16},{28,20},{1,9},{5... | collective-permute-start | bytes 24584 | tf_op jit(solution)/shard_map/ppermute | solution.py:552
  56.2 3.7 %collective-permute-start.9 = (f32[16,128]{1,0:T(8,128)S(1)}, f32[16,128]{1,0:T(8,128)S(1)}, u32[]{:S(2)}, u32[]{:S(2)}) collective-permute-start(f32[16,128]{1,0:T(8,128)S(1)} %add_add_fusion.refs_0_), channel_id=1, source_target_pairs={{0,4},{4,0},{8,12},{12,8},{16,20},{20,16},{24,28},{28,24},{1,5},{5... | collective-permute-start | bytes 24584 | tf_op jit(solution)/shard_map/ppermute | solution.py:552

commit v4 on v3

--- a/solution.py
+++ b/solution.py
@@ -244,7 +244,7 @@
     expand(jnp.where(low_half(), even, odd), dup_ref, store)
 
     def squarings(step, carry):
-        width = 16
+        width = 32
         held = [first_ref[pl.ds(step * width + j, 64, stride=64), :] for j in range(width)]
         for level in range(4):
             for j in range(width):
@@ -263,7 +263,7 @@
         return carry
 
     inverse_root_col = 1.0 / root_col
-    lax.fori_loop(0, PAIRS // 16, squarings, 0)
+    lax.fori_loop(0, PAIRS // 32, squarings, 0)
 
     def finish(p, message):
         message_ref[p] = jnp.concatenate(message, axis=0)
@@ -351,7 +351,9 @@
     subtree = lax.axis_index("branch")
     mask = low_half()
     twice = identity_twice()
-    pi_row, pi_col, root_col, inverse_root_row = [fixed_ref[at] for at in (0, 1, 3, 4)]
+    pi_row, pi_col, root_row, root_col, inverse_root_row, inverse_root_col = [
+        fixed_ref[at] for at in range(6)
+    ]
     sites = weights_ref.shape[1]
     weight = weights_ref[...].astype(F32)
 
@@ -371,16 +373,16 @@
 
     def store_counts(p, square):
         counts = jnp.where(mask, square[0:64], square[64:128])
-        count_ref[p] = root_col * counts * inverse_root_row
+        count_ref[p] = inverse_root_col * counts * root_row
 
     def descend(r):
         a_high, a_low = a_high_ref[r - 32], a_low_ref[r - 32]
         child = 2 * r - 64
         u_high = jnp.concatenate([high_ref[child], high_ref[child + 1]], axis=0)
         u_low = jnp.concatenate([low_ref[child], low_ref[child + 1]], axis=0)
-        first = mxu_nt(u_high, jnp.concatenate([a_high, a_low], axis=0))
-        second = mxu_nt(u_low, a_high)
-        store_counts(r, first[:, 0:128] + first[:, 128:256] + second)
+        first = mxu_nt(jnp.concatenate([a_high, a_low], axis=0), u_high)
+        second = mxu_nt(a_high, u_low)
+        store_counts(r, first[0:128] + first[128:256] + second)
         return [
             messages(
                 matrix_ref[2 * (r - 32) + e], a_high[64 * e : 64 * e + 64], a_low[64 * e : 64 * e + 64]
@@ -417,8 +419,8 @@
             for e in range(2):
                 p = 2 * r + e - 64
                 high, low = children(down, e, p)
-                square = mxu_nt(leaf_ref[p], jnp.concatenate([high, low], axis=0))
-                store_counts(p, square[:, 0:128] + square[:, 128:256])
+                square = mxu_nt(jnp.concatenate([high, low], axis=0), leaf_ref[p])
+                store_counts(p, square[0:128] + square[128:256])
         return carry
 
     lax.fori_loop(0, 4, leaf_level, 0)

time: 61 us -> 59.7 us (0.979)
  Pallas kernels: 38.7 us -> 37.4 us
    pallas_call x1, Pallas kernels: 20.1 us -> 18.8 us  [body(): pl.pallas_call(functools.partial(down_kernel, total_sites, members), out_...]
where the time goes in v4:
time: 59.7 us; the launch traced here: 59.5 us
  Pallas kernels  37.4 us (63%)
  starting transfers between devices  11 us (18%)
  waiting for transfers between devices  10.3 us (17%)
  between operations  0.67 us (1%)
    pallas_call x1, Pallas kernels, body(): pl.pallas_call(functools.partial(down_kernel, total_sites, members), out_...  18.8 us
    pallas_call x1, Pallas kernels, body(): pl.pallas_call(up_kernel, out_shape=[shape((64, sites), F32), held((4, 2,...  15 us
    ppermute x10, starting transfers between devices, partners(): lax.ppermute(x, axis, [(i, i ^ step * start) for i in range(size)])  11 us
    ppermute x10, waiting for transfers between devices, partners(): lax.ppermute(x, axis, [(i, i ^ step * start) for i in range(size)])  10.3 us
    pallas_call x1, Pallas kernels, body(): pl.pallas_call(side_kernel, out_shape=[held((PAIRS * 64, 128), F32), held...  2.74 us
  transfers between devices with their start and end apart: 10, of which 6 were waited for; matrix products, arithmetic and copies ran while one was open for 0% of the time, Pallas kernels for 5%

profile of v4, /device:TPU:0, one launch (start us, length us, event | category | flops | bytes accessed | tf_op | source)
XLA Modules:
  0.0 59.5 jit_solution(199800008879240842)
XLA Ops:
  0.6 15.0 %up.1 = (f32[64,256]{1,0:T(8,128)S(1)}, bf16[4,2,64,64,128]{4,3,2,1,0:T(8,128)(2,1)S(1)}, f32[64,64,128]{2,1,0:T(8,128)S(1)}, f32[4,4,64,128]{3,2,1,0:T(8,128)S(...) custom-call(s32[256,256]{1,0:T(8,128)} %states_ref.1, ...), custom_call_target="tpu_custom_call" | custom-call | tf_op jit(solution)/shard_map/up/pallas_call | solution.py:601
  15.7 2.4 %collective-permute-start.2 = (f32[64,256]{1,0:T(8,128)S(1)}, f32[64,256]{1,0:T(8,128)S(1)}, u32[]{:S(2)}, u32[]{:S(2)}) collective-permute-start(f32[64,256]{1,0:T(8,128)S(1)} %get-tuple-element.23.refs_0_), channel_id=1, source_target_pairs={{0,3},{1,2},{2,1},{3,0},{4,7},{5,6},{6,5},{7,4},{8,11},{9,10},{10,... | collective-permute-start | bytes 196616 | tf_op jit(solution)/shard_map/ppermute | solution.py:554
  18.1 0.6 %collective-permute-start.1 = (f32[64,256]{1,0:T(8,128)S(1)}, f32[64,256]{1,0:T(8,128)S(1)}, u32[]{:S(2)}, u32[]{:S(2)}) collective-permute-start(f32[64,256]{1,0:T(8,128)S(1)} %get-tuple-element.23.refs_0_), channel_id=1, source_target_pairs={{0,2},{1,3},{2,0},{3,1},{4,6},{5,7},{6,4},{7,5},{8,10},{9,11},{10,... | collective-permute-start | bytes 196616 | tf_op jit(solution)/shard_map/ppermute | solution.py:554
  18.7 0.0 collective-permute-start
  18.8 2.7 %side.1 = (f32[4096,128]{1,0:T(8,128)S(1)}, bf16[64,64,256]{2,1,0:T(8,128)(2,1)S(1)}, f32[128,128]{1,0:T(8,128)S(1)}) custom-call(f32[4096,128]{1,0:T(8,128)S(1)} %get-tuple-element.24.dup_ref, f32[64,64,128]{2,1,0:T(8,128)S(1)} %get-tuple-element.25.last_ref, f32[1,127]{1,0:T(1,128)} %bitcast.8, s32[1,127]{1,0:T(1,128)} %bitcast.10, ...), custom_call_target="tpu_custom_call" | custom-call | tf_op jit(solution)/shard_map/side/pallas_call | solution.py:633
  21.5 0.0 collective-permute-done.2.refs_3_
  21.5 1.2 %collective-permute-done.1.refs_2_ = f32[64,256]{1,0:T(8,128)S(1)} collective-permute-done((f32[64,256]{1,0:T(8,128)S(1)}, f32[64,256]{1,0:T(8,128)S(1)}, u32[]{:S(2)}, u32[]{:S(2)}) %collective-permute-start.1) | collective-permute-done | bytes 65568 | tf_op jit(solution)/shard_map/ppermute | solution.py:554
  22.8 0.0 collective-permute-done.refs_1_
  22.8 18.8 %down.1 = f32[16,128]{1,0:T(8,128)S(1)} custom-call(f32[64,256]{1,0:T(8,128)S(1)} %get-tuple-element.23.refs_0_, f32[64,256]{1,0:T(8,128)S(1)} %collective-permute-done.refs_1_, f32[64,256]{1,0:T(8,128)S(1)} %collective-permute-done.1.refs_2_, f32[64,256]{1,0:T(8,128)S(1)} %collective-permute-done.2.refs_3_, ...), custom_call_target="tpu_custom_call" | custom-call | tf_op jit(solution)/shard_map/down/pallas_call | solution.py:645
  41.6 1.4 %collective-permute-start.5 = (f32[16,128]{1,0:T(8,128)S(1)}, f32[16,128]{1,0:T(8,128)S(1)}, u32[]{:S(2)}, u32[]{:S(2)}) collective-permute-start(f32[16,128]{1,0:T(8,128)S(1)} %down.1), channel_id=1, source_target_pairs={{0,3},{1,2},{2,1},{3,0},{4,7},{5,6},{6,5},{7,4},{8,11},{9,10},{10,... | collective-permute-start | bytes 24584 | tf_op jit(solution)/shard_map/ppermute | solution.py:554
  43.0 0.4 collective-permute-start.4
  43.4 0.1 collective-permute-start.3
  43.5 1.2 %collective-permute-done.5 = f32[16,128]{1,0:T(8,128)S(1)} collective-permute-done((f32[16,128]{1,0:T(8,128)S(1)}, f32[16,128]{1,0:T(8,128)S(1)}, u32[]{:S(2)}, u32[]{:S(2)}) %collective-permute-start.5) | collective-permute-done | bytes 8224 | tf_op jit(solution)/shard_map/ppermute | solution.py:554
  44.7 2.0 %collective-permute-done.4 = f32[16,128]{1,0:T(8,128)S(1)} collective-permute-done((f32[16,128]{1,0:T(8,128)S(1)}, f32[16,128]{1,0:T(8,128)S(1)}, u32[]{:S(2)}, u32[]{:S(2)}) %collective-permute-start.4) | collective-permute-done | bytes 8224 | tf_op jit(solution)/shard_map/ppermute | solution.py:554
  46.7 0.0 collective-permute-done.3
  46.7 3.7 %collective-permute-start.8 = (f32[16,128]{1,0:T(8,128)S(1)}, f32[16,128]{1,0:T(8,128)S(1)}, u32[]{:S(2)}, u32[]{:S(2)}) collective-permute-start(f32[16,128]{1,0:T(8,128)S(1)} %add_add_fusion.1), channel_id=1, source_target_pairs={{0,24},{4,28},{8,16},{12,20},{16,8},{20,12},{24,0},{28,4},{1,25},{... | collective-permute-start | bytes 24584 | tf_op jit(solution)/shard_map/ppermute | solution.py:554
  50.3 0.0 collective-permute-start.7
  50.4 0.8 %collective-permute-start.6 = (f32[16,128]{1,0:T(8,128)S(1)}, f32[16,128]{1,0:T(8,128)S(1)}, u32[]{:S(2)}, u32[]{:S(2)}) collective-permute-start(f32[16,128]{1,0:T(8,128)S(1)} %add_add_fusion.1), channel_id=1, source_target_pairs={{0,8},{4,12},{8,0},{12,4},{16,24},{20,28},{24,16},{28,20},{1,9},{5... | collective-permute-start | bytes 24584 | tf_op jit(solution)/shard_map/ppermute | solution.py:554
  51.1 1.1 %collective-permute-done.8 = f32[16,128]{1,0:T(8,128)S(1)} collective-permute-done((f32[16,128]{1,0:T(8,128)S(1)}, f32[16,128]{1,0:T(8,128)S(1)}, u32[]{:S(2)}, u32[]{:S(2)}) %collective-permute-start.8) | collective-permute-done | bytes 8224 | tf_op jit(solution)/shard_map/ppermute | solution.py:554
  52.2 2.7 %collective-permute-done.7 = f32[16,128]{1,0:T(8,128)S(1)} collective-permute-done((f32[16,128]{1,0:T(8,128)S(1)}, f32[16,128]{1,0:T(8,128)S(1)}, u32[]{:S(2)}, u32[]{:S(2)}) %collective-permute-start.7) | collective-permute-done | bytes 8224 | tf_op jit(solution)/shard_map/ppermute | solution.py:554
  54.9 0.0 collective-permute-done.6
  54.9 1.6 %collective-permute-start.9 = (f32[16,128]{1,0:T(8,128)S(1)}, f32[16,128]{1,0:T(8,128)S(1)}, u32[]{:S(2)}, u32[]{:S(2)}) collective-permute-start(f32[16,128]{1,0:T(8,128)S(1)} %add_add_fusion.refs_0_), channel_id=1, source_target_pairs={{0,4},{4,0},{8,12},{12,8},{16,20},{20,16},{24,28},{28,24},{1,5},{5... | collective-permute-start | bytes 24584 | tf_op jit(solution)/shard_map/ppermute | solution.py:554
  56.5 2.1 %collective-permute-done.9.refs_1_ = f32[16,128]{1,0:T(8,128)S(1)} collective-permute-done((f32[16,128]{1,0:T(8,128)S(1)}, f32[16,128]{1,0:T(8,128)S(1)}, u32[]{:S(2)}, u32[]{:S(2)}) %collective-permute-start.9) | collective-permute-done | bytes 8224 | tf_op jit(solution)/shard_map/ppermute | solution.py:554
  58.6 0.8 %last.1 = (f32[64,64]{1,0:T(8,128)}, f32[1,8]{1,0:T(1,128)}, f32[1,127]{1,0:T(1,128)}, f32[1,1]{1,0:T(1,128)}) custom-call(f32[16,128]{1,0:T(8,128)S(1)} %add_add_fusion.refs_0_, f32[16,128]{1,0:T(8,128)S(1)} %collective-permute-done.9.refs_1_), custom_call_target="tpu_custom_call" | custom-call | tf_op jit(solution)/shard_map/last/pallas_call | solution.py:668
  (2 shorter events, 0.0 us)
Async XLA Ops:
  15.7 5.9 %collective-permute-start.2 = (f32[64,256]{1,0:T(8,128)S(1)}, f32[64,256]{1,0:T(8,128)S(1)}, u32[]{:S(2)}, u32[]{:S(2)}) collective-permute-start(f32[64,256]{1,0:T(8,128)S(1)} %get-tuple-element.23.refs_0_), channel_id=1, source_target_pairs={{0,3},{1,2},{2,1},{3,0},{4,7},{5,6},{6,5},{7,4},{8,11},{9,10},{10,... | collective-permute-start | bytes 196616 | tf_op jit(solution)/shard_map/ppermute | solution.py:554
  18.1 4.7 %collective-permute-start.1 = (f32[64,256]{1,0:T(8,128)S(1)}, f32[64,256]{1,0:T(8,128)S(1)}, u32[]{:S(2)}, u32[]{:S(2)}) collective-permute-start(f32[64,256]{1,0:T(8,128)S(1)} %get-tuple-element.23.refs_0_), channel_id=1, source_target_pairs={{0,2},{1,3},{2,0},{3,1},{4,6},{5,7},{6,4},{7,5},{8,10},{9,11},{10,... | collective-permute-start | bytes 196616 | tf_op jit(solution)/shard_map/ppermute | solution.py:554
  18.7 4.0 %collective-permute-start = (f32[64,256]{1,0:T(8,128)S(1)}, f32[64,256]{1,0:T(8,128)S(1)}, u32[]{:S(2)}, u32[]{:S(2)}) collective-permute-start(f32[64,256]{1,0:T(8,128)S(1)} %get-tuple-element.23.refs_0_), channel_id=1, source_target_pairs={{0,1},{1,0},{2,3},{3,2},{4,5},{5,4},{6,7},{7,6},{8,9},{9,8},{10,11... | collective-permute-start | bytes 196616 | tf_op jit(solution)/shard_map/ppermute | solution.py:554
  41.6 3.1 %collective-permute-start.5 = (f32[16,128]{1,0:T(8,128)S(1)}, f32[16,128]{1,0:T(8,128)S(1)}, u32[]{:S(2)}, u32[]{:S(2)}) collective-permute-start(f32[16,128]{1,0:T(8,128)S(1)} %down.1), channel_id=1, source_target_pairs={{0,3},{1,2},{2,1},{3,0},{4,7},{5,6},{6,5},{7,4},{8,11},{9,10},{10,... | collective-permute-start | bytes 24584 | tf_op jit(solution)/shard_map/ppermute | solution.py:554
  43.0 3.7 %collective-permute-start.4 = (f32[16,128]{1,0:T(8,128)S(1)}, f32[16,128]{1,0:T(8,128)S(1)}, u32[]{:S(2)}, u32[]{:S(2)}) collective-permute-start(f32[16,128]{1,0:T(8,128)S(1)} %down.1), channel_id=1, source_target_pairs={{0,2},{1,3},{2,0},{3,1},{4,6},{5,7},{6,4},{7,5},{8,10},{9,11},{10,... | collective-permute-start | bytes 24584 | tf_op jit(solution)/shard_map/ppermute | solution.py:554
  43.4 3.3 %collective-permute-start.3 = (f32[16,128]{1,0:T(8,128)S(1)}, f32[16,128]{1,0:T(8,128)S(1)}, u32[]{:S(2)}, u32[]{:S(2)}) collective-permute-start(f32[16,128]{1,0:T(8,128)S(1)} %down.1), channel_id=1, source_target_pairs={{0,1},{1,0},{2,3},{3,2},{4,5},{5,4},{6,7},{7,6},{8,9},{9,8},{10,11... | collective-permute-start | bytes 24584 | tf_op jit(solution)/shard_map/ppermute | solution.py:554
  46.7 5.5 %collective-permute-start.8 = (f32[16,128]{1,0:T(8,128)S(1)}, f32[16,128]{1,0:T(8,128)S(1)}, u32[]{:S(2)}, u32[]{:S(2)}) collective-permute-start(f32[16,128]{1,0:T(8,128)S(1)} %add_add_fusion.1), channel_id=1, source_target_pairs={{0,24},{4,28},{8,16},{12,20},{16,8},{20,12},{24,0},{28,4},{1,25},{... | collective-permute-start | bytes 24584 | tf_op jit(solution)/shard_map/ppermute | solution.py:554
  50.3 4.5 %collective-permute-start.7 = (f32[16,128]{1,0:T(8,128)S(1)}, f32[16,128]{1,0:T(8,128)S(1)}, u32[]{:S(2)}, u32[]{:S(2)}) collective-permute-start(f32[16,128]{1,0:T(8,128)S(1)} %add_add_fusion.1), channel_id=1, source_target_pairs={{0,16},{4,20},{8,24},{12,28},{16,0},{20,4},{24,8},{28,12},{1,17},{... | collective-permute-start | bytes 24584 | tf_op jit(solution)/shard_map/ppermute | solution.py:554
  50.4 4.5 %collective-permute-start.6 = (f32[16,128]{1,0:T(8,128)S(1)}, f32[16,128]{1,0:T(8,128)S(1)}, u32[]{:S(2)}, u32[]{:S(2)}) collective-permute-start(f32[16,128]{1,0:T(8,128)S(1)} %add_add_fusion.1), channel_id=1, source_target_pairs={{0,8},{4,12},{8,0},{12,4},{16,24},{20,28},{24,16},{28,20},{1,9},{5... | collective-permute-start | bytes 24584 | tf_op jit(solution)/shard_map/ppermute | solution.py:554
  54.9 3.7 %collective-permute-start.9 = (f32[16,128]{1,0:T(8,128)S(1)}, f32[16,128]{1,0:T(8,128)S(1)}, u32[]{:S(2)}, u32[]{:S(2)}) collective-permute-start(f32[16,128]{1,0:T(8,128)S(1)} %add_add_fusion.refs_0_), channel_id=1, source_target_pairs={{0,4},{4,0},{8,12},{12,8},{16,20},{20,16},{24,28},{28,24},{1,5},{5... | collective-permute-start | bytes 24584 | tf_op jit(solution)/shard_map/ppermute | solution.py:554

commit v5 on v4

--- a/solution.py
+++ b/solution.py
@@ -217,6 +217,17 @@
     ):
         fixed_ref[at] = jnp.broadcast_to(value, (64, 128))
 
+    sites = states_ref.shape[1]
+    codon = lax.broadcasted_iota(jnp.int32, (64, sites), 0)
+    for p in range(32):
+        both = []
+        for e in range(2):
+            taxon = order_ref[subtree * LEAF_DEV + 2 * p + e]
+            state = jnp.where(gap_ref[pl.ds(taxon, 1), :] > 0, -1, states_ref[pl.ds(taxon, 1), :])
+            hit = (codon == state) | (state < 0)
+            both.append(jnp.where(hit, 1.0, 0.0).astype(BF))
+        leaf_ref[p] = jnp.concatenate(both, axis=0)
+
     powers = []
     for pair in range(CLASSES // 2):
         factor, off, rows, mean = class_pair(
@@ -244,18 +255,30 @@
     expand(jnp.where(low_half(), even, odd), dup_ref, store)
 
     def squarings(step, carry):
-        width = 32
+        width = 16
         held = [first_ref[pl.ds(step * width + j, 64, stride=64), :] for j in range(width)]
+        zero = jnp.zeros((128, 128), BF)
         for level in range(4):
-            for j in range(width):
-                high, low = split(held[j])
-                chain_ref[level, 0, step * width + j] = high
-                chain_ref[level, 1, step * width + j] = low
-                wide_high, wide_low = spread(high), spread(low)
-                held[j] = 2.0 * held[j] + mxu(
-                    jnp.concatenate([high, high, low], axis=1),
-                    jnp.concatenate([wide_high, wide_low, wide_high], axis=0),
-                )
+            for j in range(0, width, 2):
+                highs, lows, products = [], [], []
+                for t in range(2):
+                    high, low = split(held[j + t])
+                    chain_ref[level, 0, step * width + j + t] = high
+                    chain_ref[level, 1, step * width + j + t] = low
+                    wide = spread(high)
+                    highs.append(high)
+                    lows.append(spread(low))
+                    products.append(mxu(
+                        jnp.concatenate([high, low], axis=1), jnp.concatenate([wide, wide], axis=0)
+                    ))
+                rest = mxu(jnp.concatenate(highs, axis=1), jnp.concatenate([
+                    jnp.concatenate([lows[0], zero], axis=1),
+                    jnp.concatenate([zero, lows[1]], axis=1),
+                ], axis=0))
+                for t in range(2):
+                    held[j + t] = (
+                        2.0 * held[j + t] + products[t] + rest[:, 128 * t : 128 * t + 128]
+                    )
         for j in range(width):
             p = step * width + j
             last_ref[p] = held[j]
@@ -263,7 +286,7 @@
         return carry
 
     inverse_root_col = 1.0 / root_col
-    lax.fori_loop(0, PAIRS // 32, squarings, 0)
+    lax.fori_loop(0, PAIRS // 16, squarings, 0)
 
     def finish(p, message):
         message_ref[p] = jnp.concatenate(message, axis=0)
@@ -276,26 +299,10 @@
         high_ref[p] = high
         low_ref[p] = low
 
-    sites = states_ref.shape[1]
-    codon = lax.broadcasted_iota(jnp.int32, (64, sites), 0)
-
-    def leaf_level(step, carry):
-        for j in range(8):
-            p = step * 8 + j
-            both = []
-            for e in range(2):
-                taxon = order_ref[subtree * LEAF_DEV + 2 * p + e]
-                state = jnp.where(
-                    gap_ref[pl.ds(taxon, 1), :] > 0, -1, states_ref[pl.ds(taxon, 1), :]
-                )
-                hit = (codon == state) | (state < 0)
-                both.append(jnp.where(hit, 1.0, 0.0).astype(BF))
-            leaf_ref[p] = jnp.concatenate(both, axis=0)
-            nothing = jnp.zeros_like(both[0])
-            finish(p, [messages(up_ref[2 * p + e], both[e], nothing) for e in range(2)])
-        return carry
-
-    lax.fori_loop(0, LEAF_DEV // 16, leaf_level, 0)
+    for p in range(32):
+        both = [leaf_ref[p, 64 * e : 64 * e + 64, :] for e in range(2)]
+        nothing = jnp.zeros_like(both[0])
+        finish(p, [messages(up_ref[2 * p + e], both[e], nothing) for e in range(2)])
 
     def inner(p):
         child = 2 * p - 64
@@ -412,19 +419,13 @@
     for r in range(63, 47, -1):
         inner(r)
 
-    def leaf_level(step, carry):
-        for j in range(4):
-            r = 32 + step * 4 + j
-            down = descend(r)
-            for e in range(2):
-                p = 2 * r + e - 64
-                high, low = children(down, e, p)
-                square = mxu_nt(jnp.concatenate([high, low], axis=0), leaf_ref[p])
-                store_counts(p, square[0:128] + square[128:256])
-        return carry
-
-    lax.fori_loop(0, 4, leaf_level, 0)
-
+    for r in range(47, 31, -1):
+        down = descend(r)
+        for e in range(2):
+            p = 2 * r + e - 64
+            high, low = children(down, e, p)
+            square = mxu_nt(jnp.concatenate([high, low], axis=0), leaf_ref[p])
+            store_counts(p, square[0:128] + square[128:256])
 
     def adjoint(step, carry):
         held = [count_ref[step * 16 + j] for j in range(16)]
@@ -441,8 +442,9 @@
                     jnp.concatenate([spread(high), spread(low)], axis=1),
                 ], axis=0)
                 four = mxu(left, right)
-                four = four[0:64] + four[64:128]
-                held[j] = 2.0 * held[j] + four[:, 0:128] + four[:, 128:256]
+                held[j] = 2.0 * held[j] + (
+                    four[0:64, 0:128] + four[0:64, 128:256] + four[64:128, 0:128]
+                )
         for j in range(16):
             back_ref[pl.ds(step * 16 + j, 64, stride=64), :] = held[j]
         return carry

time: 59.7 us -> 59.7 us (level)
  no operation moved by 1% of the time
where the time goes in v5:
time: 59.7 us; the launch traced here: 59.5 us
  Pallas kernels  37.4 us (63%)
  starting transfers between devices  11 us (18%)
  waiting for transfers between devices  10.4 us (17%)
  between operations  0.67 us (1%)
    pallas_call x1, Pallas kernels, body(): pl.pallas_call(functools.partial(down_kernel, total_sites, members), out_...  18.7 us
    pallas_call x1, Pallas kernels, body(): pl.pallas_call(up_kernel, out_shape=[shape((64, sites), F32), held((4, 2,...  15.1 us
    ppermute x10, starting transfers between devices, partners(): lax.ppermute(x, axis, [(i, i ^ step * start) for i in range(size)])  11 us
    ppermute x10, waiting for transfers between devices, partners(): lax.ppermute(x, axis, [(i, i ^ step * start) for i in range(size)])  10.4 us
    pallas_call x1, Pallas kernels, body(): pl.pallas_call(side_kernel, out_shape=[held((PAIRS * 64, 128), F32), held...  2.74 us
  transfers between devices with their start and end apart: 10, of which 6 were waited for; matrix products, arithmetic and copies ran while one was open for 0% of the time, Pallas kernels for 5%

profile of v5, /device:TPU:0, one launch (start us, length us, event | category | flops | bytes accessed | tf_op | source)
XLA Modules:
  0.0 59.5 jit_solution(3207180146779463763)
XLA Ops:
  0.6 15.1 %up.1 = (f32[64,256]{1,0:T(8,128)S(1)}, bf16[4,2,64,64,128]{4,3,2,1,0:T(8,128)(2,1)S(1)}, f32[64,64,128]{2,1,0:T(8,128)S(1)}, f32[4,4,64,128]{3,2,1,0:T(8,128)S(...) custom-call(s32[256,256]{1,0:T(8,128)} %states_ref.1, ...), custom_call_target="tpu_custom_call" | custom-call | tf_op jit(solution)/shard_map/up/pallas_call | solution.py:603
  15.7 2.4 %collective-permute-start.2 = (f32[64,256]{1,0:T(8,128)S(1)}, f32[64,256]{1,0:T(8,128)S(1)}, u32[]{:S(2)}, u32[]{:S(2)}) collective-permute-start(f32[64,256]{1,0:T(8,128)S(1)} %get-tuple-element.23.refs_0_), channel_id=1, source_target_pairs={{0,3},{1,2},{2,1},{3,0},{4,7},{5,6},{6,5},{7,4},{8,11},{9,10},{10,... | collective-permute-start | bytes 196616 | tf_op jit(solution)/shard_map/ppermute | solution.py:556
  18.2 0.6 %collective-permute-start.1 = (f32[64,256]{1,0:T(8,128)S(1)}, f32[64,256]{1,0:T(8,128)S(1)}, u32[]{:S(2)}, u32[]{:S(2)}) collective-permute-start(f32[64,256]{1,0:T(8,128)S(1)} %get-tuple-element.23.refs_0_), channel_id=1, source_target_pairs={{0,2},{1,3},{2,0},{3,1},{4,6},{5,7},{6,4},{7,5},{8,10},{9,11},{10,... | collective-permute-start | bytes 196616 | tf_op jit(solution)/shard_map/ppermute | solution.py:556
  18.8 0.0 collective-permute-start
  18.9 2.7 %side.1 = (f32[4096,128]{1,0:T(8,128)S(1)}, bf16[64,64,256]{2,1,0:T(8,128)(2,1)S(1)}, f32[128,128]{1,0:T(8,128)S(1)}) custom-call(f32[4096,128]{1,0:T(8,128)S(1)} %get-tuple-element.24.dup_ref, f32[64,64,128]{2,1,0:T(8,128)S(1)} %get-tuple-element.25.last_ref, f32[1,127]{1,0:T(1,128)} %bitcast.8, s32[1,127]{1,0:T(1,128)} %bitcast.10, ...), custom_call_target="tpu_custom_call" | custom-call | tf_op jit(solution)/shard_map/side/pallas_call | solution.py:635
  21.6 0.0 collective-permute-done.2.refs_3_
  21.6 1.2 %collective-permute-done.1.refs_2_ = f32[64,256]{1,0:T(8,128)S(1)} collective-permute-done((f32[64,256]{1,0:T(8,128)S(1)}, f32[64,256]{1,0:T(8,128)S(1)}, u32[]{:S(2)}, u32[]{:S(2)}) %collective-permute-start.1) | collective-permute-done | bytes 65568 | tf_op jit(solution)/shard_map/ppermute | solution.py:556
  22.9 0.0 collective-permute-done.refs_1_
  22.9 18.7 %down.1 = f32[16,128]{1,0:T(8,128)S(1)} custom-call(f32[64,256]{1,0:T(8,128)S(1)} %get-tuple-element.23.refs_0_, f32[64,256]{1,0:T(8,128)S(1)} %collective-permute-done.refs_1_, f32[64,256]{1,0:T(8,128)S(1)} %collective-permute-done.1.refs_2_, f32[64,256]{1,0:T(8,128)S(1)} %collective-permute-done.2.refs_3_, ...), custom_call_target="tpu_custom_call" | custom-call | tf_op jit(solution)/shard_map/down/pallas_call | solution.py:647
  41.6 1.4 %collective-permute-start.5 = (f32[16,128]{1,0:T(8,128)S(1)}, f32[16,128]{1,0:T(8,128)S(1)}, u32[]{:S(2)}, u32[]{:S(2)}) collective-permute-start(f32[16,128]{1,0:T(8,128)S(1)} %down.1), channel_id=1, source_target_pairs={{0,3},{1,2},{2,1},{3,0},{4,7},{5,6},{6,5},{7,4},{8,11},{9,10},{10,... | collective-permute-start | bytes 24584 | tf_op jit(solution)/shard_map/ppermute | solution.py:556
  43.0 0.4 collective-permute-start.4
  43.3 0.1 collective-permute-start.3
  43.5 1.2 %collective-permute-done.5 = f32[16,128]{1,0:T(8,128)S(1)} collective-permute-done((f32[16,128]{1,0:T(8,128)S(1)}, f32[16,128]{1,0:T(8,128)S(1)}, u32[]{:S(2)}, u32[]{:S(2)}) %collective-permute-start.5) | collective-permute-done | bytes 8224 | tf_op jit(solution)/shard_map/ppermute | solution.py:556
  44.7 2.0 %collective-permute-done.4 = f32[16,128]{1,0:T(8,128)S(1)} collective-permute-done((f32[16,128]{1,0:T(8,128)S(1)}, f32[16,128]{1,0:T(8,128)S(1)}, u32[]{:S(2)}, u32[]{:S(2)}) %collective-permute-start.4) | collective-permute-done | bytes 8224 | tf_op jit(solution)/shard_map/ppermute | solution.py:556
  46.6 0.0 collective-permute-done.3
  46.6 3.7 %collective-permute-start.8 = (f32[16,128]{1,0:T(8,128)S(1)}, f32[16,128]{1,0:T(8,128)S(1)}, u32[]{:S(2)}, u32[]{:S(2)}) collective-permute-start(f32[16,128]{1,0:T(8,128)S(1)} %add_add_fusion.1), channel_id=1, source_target_pairs={{0,24},{4,28},{8,16},{12,20},{16,8},{20,12},{24,0},{28,4},{1,25},{... | collective-permute-start | bytes 24584 | tf_op jit(solution)/shard_map/ppermute | solution.py:556
  50.3 0.0 collective-permute-start.7
  50.3 0.8 %collective-permute-start.6 = (f32[16,128]{1,0:T(8,128)S(1)}, f32[16,128]{1,0:T(8,128)S(1)}, u32[]{:S(2)}, u32[]{:S(2)}) collective-permute-start(f32[16,128]{1,0:T(8,128)S(1)} %add_add_fusion.1), channel_id=1, source_target_pairs={{0,8},{4,12},{8,0},{12,4},{16,24},{20,28},{24,16},{28,20},{1,9},{5... | collective-permute-start | bytes 24584 | tf_op jit(solution)/shard_map/ppermute | solution.py:556
  51.1 1.1 %collective-permute-done.8 = f32[16,128]{1,0:T(8,128)S(1)} collective-permute-done((f32[16,128]{1,0:T(8,128)S(1)}, f32[16,128]{1,0:T(8,128)S(1)}, u32[]{:S(2)}, u32[]{:S(2)}) %collective-permute-start.8) | collective-permute-done | bytes 8224 | tf_op jit(solution)/shard_map/ppermute | solution.py:556
  52.2 2.7 %collective-permute-done.7 = f32[16,128]{1,0:T(8,128)S(1)} collective-permute-done((f32[16,128]{1,0:T(8,128)S(1)}, f32[16,128]{1,0:T(8,128)S(1)}, u32[]{:S(2)}, u32[]{:S(2)}) %collective-permute-start.7) | collective-permute-done | bytes 8224 | tf_op jit(solution)/shard_map/ppermute | solution.py:556
  54.9 0.0 collective-permute-done.6
  54.9 1.5 %collective-permute-start.9 = (f32[16,128]{1,0:T(8,128)S(1)}, f32[16,128]{1,0:T(8,128)S(1)}, u32[]{:S(2)}, u32[]{:S(2)}) collective-permute-start(f32[16,128]{1,0:T(8,128)S(1)} %add_add_fusion.refs_0_), channel_id=1, source_target_pairs={{0,4},{4,0},{8,12},{12,8},{16,20},{20,16},{24,28},{28,24},{1,5},{5... | collective-permute-start | bytes 24584 | tf_op jit(solution)/shard_map/ppermute | solution.py:556
  56.4 2.2 %collective-permute-done.9.refs_1_ = f32[16,128]{1,0:T(8,128)S(1)} collective-permute-done((f32[16,128]{1,0:T(8,128)S(1)}, f32[16,128]{1,0:T(8,128)S(1)}, u32[]{:S(2)}, u32[]{:S(2)}) %collective-permute-start.9) | collective-permute-done | bytes 8224 | tf_op jit(solution)/shard_map/ppermute | solution.py:556
  58.6 0.8 %last.1 = (f32[64,64]{1,0:T(8,128)}, f32[1,8]{1,0:T(1,128)}, f32[1,127]{1,0:T(1,128)}, f32[1,1]{1,0:T(1,128)}) custom-call(f32[16,128]{1,0:T(8,128)S(1)} %add_add_fusion.refs_0_, f32[16,128]{1,0:T(8,128)S(1)} %collective-permute-done.9.refs_1_), custom_call_target="tpu_custom_call" | custom-call | tf_op jit(solution)/shard_map/last/pallas_call | solution.py:670
  (2 shorter events, 0.0 us)
Async XLA Ops:
  15.7 5.9 %collective-permute-start.2 = (f32[64,256]{1,0:T(8,128)S(1)}, f32[64,256]{1,0:T(8,128)S(1)}, u32[]{:S(2)}, u32[]{:S(2)}) collective-permute-start(f32[64,256]{1,0:T(8,128)S(1)} %get-tuple-element.23.refs_0_), channel_id=1, source_target_pairs={{0,3},{1,2},{2,1},{3,0},{4,7},{5,6},{6,5},{7,4},{8,11},{9,10},{10,... | collective-permute-start | bytes 196616 | tf_op jit(solution)/shard_map/ppermute | solution.py:556
  18.2 4.7 %collective-permute-start.1 = (f32[64,256]{1,0:T(8,128)S(1)}, f32[64,256]{1,0:T(8,128)S(1)}, u32[]{:S(2)}, u32[]{:S(2)}) collective-permute-start(f32[64,256]{1,0:T(8,128)S(1)} %get-tuple-element.23.refs_0_), channel_id=1, source_target_pairs={{0,2},{1,3},{2,0},{3,1},{4,6},{5,7},{6,4},{7,5},{8,10},{9,11},{10,... | collective-permute-start | bytes 196616 | tf_op jit(solution)/shard_map/ppermute | solution.py:556
  18.8 4.0 %collective-permute-start = (f32[64,256]{1,0:T(8,128)S(1)}, f32[64,256]{1,0:T(8,128)S(1)}, u32[]{:S(2)}, u32[]{:S(2)}) collective-permute-start(f32[64,256]{1,0:T(8,128)S(1)} %get-tuple-element.23.refs_0_), channel_id=1, source_target_pairs={{0,1},{1,0},{2,3},{3,2},{4,5},{5,4},{6,7},{7,6},{8,9},{9,8},{10,11... | collective-permute-start | bytes 196616 | tf_op jit(solution)/shard_map/ppermute | solution.py:556
  41.6 3.1 %collective-permute-start.5 = (f32[16,128]{1,0:T(8,128)S(1)}, f32[16,128]{1,0:T(8,128)S(1)}, u32[]{:S(2)}, u32[]{:S(2)}) collective-permute-start(f32[16,128]{1,0:T(8,128)S(1)} %down.1), channel_id=1, source_target_pairs={{0,3},{1,2},{2,1},{3,0},{4,7},{5,6},{6,5},{7,4},{8,11},{9,10},{10,... | collective-permute-start | bytes 24584 | tf_op jit(solution)/shard_map/ppermute | solution.py:556
  43.0 3.7 %collective-permute-start.4 = (f32[16,128]{1,0:T(8,128)S(1)}, f32[16,128]{1,0:T(8,128)S(1)}, u32[]{:S(2)}, u32[]{:S(2)}) collective-permute-start(f32[16,128]{1,0:T(8,128)S(1)} %down.1), channel_id=1, source_target_pairs={{0,2},{1,3},{2,0},{3,1},{4,6},{5,7},{6,4},{7,5},{8,10},{9,11},{10,... | collective-permute-start | bytes 24584 | tf_op jit(solution)/shard_map/ppermute | solution.py:556
  43.3 3.3 %collective-permute-start.3 = (f32[16,128]{1,0:T(8,128)S(1)}, f32[16,128]{1,0:T(8,128)S(1)}, u32[]{:S(2)}, u32[]{:S(2)}) collective-permute-start(f32[16,128]{1,0:T(8,128)S(1)} %down.1), channel_id=1, source_target_pairs={{0,1},{1,0},{2,3},{3,2},{4,5},{5,4},{6,7},{7,6},{8,9},{9,8},{10,11... | collective-permute-start | bytes 24584 | tf_op jit(solution)/shard_map/ppermute | solution.py:556
  46.6 5.5 %collective-permute-start.8 = (f32[16,128]{1,0:T(8,128)S(1)}, f32[16,128]{1,0:T(8,128)S(1)}, u32[]{:S(2)}, u32[]{:S(2)}) collective-permute-start(f32[16,128]{1,0:T(8,128)S(1)} %add_add_fusion.1), channel_id=1, source_target_pairs={{0,24},{4,28},{8,16},{12,20},{16,8},{20,12},{24,0},{28,4},{1,25},{... | collective-permute-start | bytes 24584 | tf_op jit(solution)/shard_map/ppermute | solution.py:556
  50.3 4.5 %collective-permute-start.7 = (f32[16,128]{1,0:T(8,128)S(1)}, f32[16,128]{1,0:T(8,128)S(1)}, u32[]{:S(2)}, u32[]{:S(2)}) collective-permute-start(f32[16,128]{1,0:T(8,128)S(1)} %add_add_fusion.1), channel_id=1, source_target_pairs={{0,16},{4,20},{8,24},{12,28},{16,0},{20,4},{24,8},{28,12},{1,17},{... | collective-permute-start | bytes 24584 | tf_op jit(solution)/shard_map/ppermute | solution.py:556
  50.3 4.5 %collective-permute-start.6 = (f32[16,128]{1,0:T(8,128)S(1)}, f32[16,128]{1,0:T(8,128)S(1)}, u32[]{:S(2)}, u32[]{:S(2)}) collective-permute-start(f32[16,128]{1,0:T(8,128)S(1)} %add_add_fusion.1), channel_id=1, source_target_pairs={{0,8},{4,12},{8,0},{12,4},{16,24},{20,28},{24,16},{28,20},{1,9},{5... | collective-permute-start | bytes 24584 | tf_op jit(solution)/shard_map/ppermute | solution.py:556
  54.9 3.7 %collective-permute-start.9 = (f32[16,128]{1,0:T(8,128)S(1)}, f32[16,128]{1,0:T(8,128)S(1)}, u32[]{:S(2)}, u32[]{:S(2)}) collective-permute-start(f32[16,128]{1,0:T(8,128)S(1)} %add_add_fusion.refs_0_), channel_id=1, source_target_pairs={{0,4},{4,0},{8,12},{12,8},{16,20},{20,16},{24,28},{28,24},{1,5},{5... | collective-permute-start | bytes 24584 | tf_op jit(solution)/shard_map/ppermute | solution.py:556

commit v6 on v5

--- a/solution.py
+++ b/solution.py
@@ -12,6 +12,7 @@
 PAIRS = 64
 CLASSES = 8
 ORDER = 8
+STRIDE = 65
 BF = jnp.bfloat16
 F32 = jnp.float32
 
@@ -178,26 +179,19 @@
     left = jnp.concatenate(
         [jnp.concatenate([high, high], axis=1), jnp.concatenate([low, low], axis=1)], axis=0
     )
-
-    def some(step, carry):
-        for j in range(16):
-            i = step * 32 + 2 * j
-            parts = [split(dup_ref[rows_of(i + t, 64), :]) for t in range(2)]
-            right = jnp.concatenate([
-                jnp.concatenate([spread(parts[0][h]), spread(parts[1][h])], axis=1)
-                for h in range(2)
-            ], axis=0)
-            both = mxu(left, right)
-            both = both[0:64] + both[64:128]
-            for t in range(2):
-                store(i + t, both[:, 128 * t : 128 * t + 128])
-        return carry
-
-    lax.fori_loop(0, 2, some, 0)
-
-
-def rows_of(step, width):
-    return pl.ds(pl.multiple_of(step * width, width), width)
+    for i in range(0, 64, 2):
+        parts = [split(dup_ref[rows_of(i + t), :]) for t in range(2)]
+        right = jnp.concatenate([
+            jnp.concatenate([spread(parts[0][h]), spread(parts[1][h])], axis=1) for h in range(2)
+        ], axis=0)
+        both = mxu(left, right)
+        both = both[0:64] + both[64:128]
+        for t in range(2):
+            store(i + t, both[:, 128 * t : 128 * t + 128])
+
+
+def rows_of(i):
+    return pl.ds(STRIDE * i, 64)
 
 
 def up_kernel(
@@ -242,21 +236,21 @@
             value = powers[pair][k]
             swapped = pltpu.roll(value, 64, 1)
             at = CLASSES * k + 2 * pair
-            dup_ref[pl.ds(at, 64, stride=64), :] = jnp.where(mask, value, swapped)
-            dup_ref[pl.ds(at + 1, 64, stride=64), :] = jnp.where(mask, swapped, value)
+            dup_ref[pl.ds(at, 64, stride=STRIDE), :] = jnp.where(mask, value, swapped)
+            dup_ref[pl.ds(at + 1, 64, stride=STRIDE), :] = jnp.where(mask, swapped, value)
             if k < 4:
                 power_ref[pair, k] = value
 
     even, odd = coefficients(len_ref, cls_ref, False)
 
     def store(i, value):
-        first_ref[rows_of(i, 64), :] = value
+        first_ref[rows_of(i), :] = value
 
     expand(jnp.where(low_half(), even, odd), dup_ref, store)
 
     def squarings(step, carry):
         width = 16
-        held = [first_ref[pl.ds(step * width + j, 64, stride=64), :] for j in range(width)]
+        held = [first_ref[pl.ds(step * width + j, 64, stride=STRIDE), :] for j in range(width)]
         zero = jnp.zeros((128, 128), BF)
         for level in range(4):
             for j in range(0, width, 2):
@@ -330,7 +324,7 @@
     even, odd = coefficients(len_ref, cls_ref, True)
 
     def store(i, value):
-        slope_ref[rows_of(i, 64), :] = value
+        slope_ref[rows_of(i), :] = value
 
     expand(jnp.where(low_half(), even, odd), dup_ref, store)
     even, odd = coefficients(len_ref, cls_ref, False)
@@ -446,25 +440,22 @@
                     four[0:64, 0:128] + four[0:64, 128:256] + four[64:128, 0:128]
                 )
         for j in range(16):
-            back_ref[pl.ds(step * 16 + j, 64, stride=64), :] = held[j]
+            back_ref[pl.ds(step * 16 + j, 64, stride=STRIDE), :] = held[j]
         return carry
 
     lax.fori_loop(0, PAIRS // 16, adjoint, 0)
 
     left = four_left(turned_ref[...])
 
-    def sums(step, total):
-        for j in range(16):
-            ats = [rows_of(step * 32 + 2 * j + t, 64) for t in range(2)]
-            values = [back_ref[at, :] for at in ats]
-            both = mxu(left, four_right(jnp.concatenate(values, axis=1)))
-            for t in range(2):
-                total = total + values[t] * slope_ref[ats[t], :]
-                here = both[:, 128 * t : 128 * t + 128]
-                bins_ref[ats[t], :] = jnp.where(mask, here[0:64], here[64:128])
-        return total
-
-    slopes = lax.fori_loop(0, 2, sums, jnp.zeros((64, 128), F32)) * 0.0625
+    total = jnp.zeros((64, 128), F32)
+    for i in range(0, 64, 2):
+        values = [back_ref[rows_of(i + t), :] for t in range(2)]
+        both = mxu(left, four_right(jnp.concatenate(values, axis=1)))
+        for t in range(2):
+            total = total + values[t] * slope_ref[rows_of(i + t), :]
+            here = both[:, 128 * t : 128 * t + 128]
+            bins_ref[rows_of(i + t), :] = jnp.where(mask, here[0:64], here[64:128])
+    slopes = total * 0.0625
 
     table, nonsyn = fixed_ref[6], nonsyn_ref[...]
     row = lax.broadcasted_iota(jnp.int32, (64, 128), 0)
@@ -476,8 +467,8 @@
         grads = []
         for k in range(ORDER):
             at = CLASSES * k + 2 * pair
-            first = bins_ref[pl.ds(at, 64, stride=64), :]
-            second = bins_ref[pl.ds(at + 1, 64, stride=64), :]
+            first = bins_ref[pl.ds(at, 64, stride=STRIDE), :]
+            second = bins_ref[pl.ds(at + 1, 64, stride=STRIDE), :]
             first = first + pltpu.roll(first, 64, 1)
             second = second + pltpu.roll(second, 64, 1)
             grads.append(jnp.where(mask, first, second))
@@ -607,7 +598,7 @@
             held((4, 2, PAIRS, 64, 128), BF),
             held((PAIRS, 64, 128), F32),
             held((CLASSES // 2, 4, 64, 128), F32),
-            held((ORDER * CLASSES * 64, 128), F32),
+            held((STRIDE * 64, 128), F32),
             held((7, 64, 128), F32),
             held((PAIRS, 128, sites), F32),
             held((64, 64, sites), BF),
@@ -619,7 +610,7 @@
         in_specs=[vmem, vmem, smem, vmem, vmem, smem] + [vmem] * 5,
         out_specs=[vmem] * 12,
         scratch_shapes=[
-            pltpu.VMEM((PAIRS * 64, 128), F32),
+            pltpu.VMEM((STRIDE * 64, 128), F32),
             pltpu.VMEM((2 * PAIRS, 64, 256), BF),
         ],
         compiler_params=limit,
@@ -635,7 +626,7 @@
     slope, matrix, turned = inside(pl.pallas_call(
         side_kernel,
         out_shape=[
-            held((PAIRS * 64, 128), F32),
+            held((STRIDE * 64, 128), F32),
             held((64, 64, 256), BF),
             held((128, 128), F32),
         ],
@@ -653,8 +644,8 @@
             pltpu.VMEM((32, 128, sites), BF),
             pltpu.VMEM((32, 128, sites), BF),
             pltpu.VMEM((PAIRS, 64, 128), F32),
-            pltpu.VMEM((PAIRS * 64, 128), F32),
-            pltpu.VMEM((64 * 64, 128), F32),
+            pltpu.VMEM((STRIDE * 64, 128), F32),
+            pltpu.VMEM((STRIDE * 64, 128), F32),
         ],
         compiler_params=limit,
         name="down",

time: 59.7 us -> 55.8 us (0.935)
  Pallas kernels: 37.4 us -> 33 us
    pallas_call x1, Pallas kernels: 15.1 us -> 13.1 us  [body(): pl.pallas_call(up_kernel, out_shape=[shape((64, sites), F32), held((4, 2,...]
    pallas_call x1, Pallas kernels: 18.7 us -> 16.9 us  [body(): pl.pallas_call(functools.partial(down_kernel, total_sites, members), out_...]
  transfers between devices with their start and end apart: 10 -> 10, of which waited for: 6 -> 6; matrix products, arithmetic and copies ran while one was open for 0% -> 0% of each run, Pallas kernels for 5% -> 4%
where the time goes in v6:
time: 55.8 us; the launch traced here: 55.6 us
  Pallas kernels  33 us (59%)
  starting transfers between devices  11 us (20%)
  waiting for transfers between devices  10.9 us (20%)
  between operations  0.67 us (1%)
    pallas_call x1, Pallas kernels, body(): pl.pallas_call(functools.partial(down_kernel, total_sites, members), out_...  16.9 us
    pallas_call x1, Pallas kernels, body(): pl.pallas_call(up_kernel, out_shape=[shape((64, sites), F32), held((4, 2,...  13.1 us
    ppermute x10, starting transfers between devices, partners(): lax.ppermute(x, axis, [(i, i ^ step * start) for i in range(size)])  11 us
    ppermute x10, waiting for transfers between devices, partners(): lax.ppermute(x, axis, [(i, i ^ step * start) for i in range(size)])  10.9 us
    pallas_call x1, Pallas kernels, body(): pl.pallas_call(side_kernel, out_shape=[held((STRIDE * 64, 128), F32), hel...  2.21 us
  transfers between devices with their start and end apart: 10, of which 6 were waited for; matrix products, arithmetic and copies ran while one was open for 0% of the time, Pallas kernels for 4%

profile of v6, /device:TPU:0, one launch (start us, length us, event | category | flops | bytes accessed | tf_op | source)
XLA Modules:
  0.0 55.6 jit_solution(5275123834939280788)
XLA Ops:
  0.6 13.1 %up.1 = (f32[64,256]{1,0:T(8,128)S(1)}, bf16[4,2,64,64,128]{4,3,2,1,0:T(8,128)(2,1)S(1)}, f32[64,64,128]{2,1,0:T(8,128)S(1)}, f32[4,4,64,128]{3,2,1,0:T(8,128)S(...) custom-call(s32[256,256]{1,0:T(8,128)} %states_ref.1, ...), custom_call_target="tpu_custom_call" | custom-call | tf_op jit(solution)/shard_map/up/pallas_call | solution.py:594
  13.7 2.5 %collective-permute-start.2 = (f32[64,256]{1,0:T(8,128)S(1)}, f32[64,256]{1,0:T(8,128)S(1)}, u32[]{:S(2)}, u32[]{:S(2)}) collective-permute-start(f32[64,256]{1,0:T(8,128)S(1)} %get-tuple-element.23.refs_0_), channel_id=1, source_target_pairs={{0,3},{1,2},{2,1},{3,0},{4,7},{5,6},{6,5},{7,4},{8,11},{9,10},{10,... | collective-permute-start | bytes 196616 | tf_op jit(solution)/shard_map/ppermute | solution.py:547
  16.2 0.6 %collective-permute-start.1 = (f32[64,256]{1,0:T(8,128)S(1)}, f32[64,256]{1,0:T(8,128)S(1)}, u32[]{:S(2)}, u32[]{:S(2)}) collective-permute-start(f32[64,256]{1,0:T(8,128)S(1)} %get-tuple-element.23.refs_0_), channel_id=1, source_target_pairs={{0,2},{1,3},{2,0},{3,1},{4,6},{5,7},{6,4},{7,5},{8,10},{9,11},{10,... | collective-permute-start | bytes 196616 | tf_op jit(solution)/shard_map/ppermute | solution.py:547
  16.8 0.0 collective-permute-start
  16.8 2.2 %side.1 = (f32[4160,128]{1,0:T(8,128)S(1)}, bf16[64,64,256]{2,1,0:T(8,128)(2,1)S(1)}, f32[128,128]{1,0:T(8,128)S(1)}) custom-call(f32[4160,128]{1,0:T(8,128)S(1)} %get-tuple-element.24.dup_ref, f32[64,64,128]{2,1,0:T(8,128)S(1)} %get-tuple-element.25.last_ref, f32[1,127]{1,0:T(1,128)} %bitcast.8, s32[1,127]{1,0:T(1,128)} %bitcast.10, ...), custom_call_target="tpu_custom_call" | custom-call | tf_op jit(solution)/shard_map/side/pallas_call | solution.py:626
  19.1 0.0 collective-permute-done.2.refs_3_
  19.1 1.8 %collective-permute-done.1.refs_2_ = f32[64,256]{1,0:T(8,128)S(1)} collective-permute-done((f32[64,256]{1,0:T(8,128)S(1)}, f32[64,256]{1,0:T(8,128)S(1)}, u32[]{:S(2)}, u32[]{:S(2)}) %collective-permute-start.1) | collective-permute-done | bytes 65568 | tf_op jit(solution)/shard_map/ppermute | solution.py:547
  20.8 0.0 collective-permute-done.refs_1_
  20.8 16.9 %down.1 = f32[16,128]{1,0:T(8,128)S(1)} custom-call(f32[64,256]{1,0:T(8,128)S(1)} %get-tuple-element.23.refs_0_, f32[64,256]{1,0:T(8,128)S(1)} %collective-permute-done.refs_1_, f32[64,256]{1,0:T(8,128)S(1)} %collective-permute-done.1.refs_2_, f32[64,256]{1,0:T(8,128)S(1)} %collective-permute-done.2.refs_3_, ...), custom_call_target="tpu_custom_call" | custom-call | tf_op jit(solution)/shard_map/down/pallas_call | solution.py:638
  37.7 1.4 %collective-permute-start.5 = (f32[16,128]{1,0:T(8,128)S(1)}, f32[16,128]{1,0:T(8,128)S(1)}, u32[]{:S(2)}, u32[]{:S(2)}) collective-permute-start(f32[16,128]{1,0:T(8,128)S(1)} %down.1), channel_id=1, source_target_pairs={{0,3},{1,2},{2,1},{3,0},{4,7},{5,6},{6,5},{7,4},{8,11},{9,10},{10,... | collective-permute-start | bytes 24584 | tf_op jit(solution)/shard_map/ppermute | solution.py:547
  39.1 0.4 collective-permute-start.4
  39.6 0.1 collective-permute-start.3
  39.6 1.2 %collective-permute-done.5 = f32[16,128]{1,0:T(8,128)S(1)} collective-permute-done((f32[16,128]{1,0:T(8,128)S(1)}, f32[16,128]{1,0:T(8,128)S(1)}, u32[]{:S(2)}, u32[]{:S(2)}) %collective-permute-start.5) | collective-permute-done | bytes 8224 | tf_op jit(solution)/shard_map/ppermute | solution.py:547
  40.8 2.0 %collective-permute-done.4 = f32[16,128]{1,0:T(8,128)S(1)} collective-permute-done((f32[16,128]{1,0:T(8,128)S(1)}, f32[16,128]{1,0:T(8,128)S(1)}, u32[]{:S(2)}, u32[]{:S(2)}) %collective-permute-start.4) | collective-permute-done | bytes 8224 | tf_op jit(solution)/shard_map/ppermute | solution.py:547
  42.8 0.0 collective-permute-done.3
  42.8 3.7 %collective-permute-start.8 = (f32[16,128]{1,0:T(8,128)S(1)}, f32[16,128]{1,0:T(8,128)S(1)}, u32[]{:S(2)}, u32[]{:S(2)}) collective-permute-start(f32[16,128]{1,0:T(8,128)S(1)} %add_add_fusion.1), channel_id=1, source_target_pairs={{0,24},{4,28},{8,16},{12,20},{16,8},{20,12},{24,0},{28,4},{1,25},{... | collective-permute-start | bytes 24584 | tf_op jit(solution)/shard_map/ppermute | solution.py:547
  46.5 0.0 collective-permute-start.7
  46.5 0.8 %collective-permute-start.6 = (f32[16,128]{1,0:T(8,128)S(1)}, f32[16,128]{1,0:T(8,128)S(1)}, u32[]{:S(2)}, u32[]{:S(2)}) collective-permute-start(f32[16,128]{1,0:T(8,128)S(1)} %add_add_fusion.1), channel_id=1, source_target_pairs={{0,8},{4,12},{8,0},{12,4},{16,24},{20,28},{24,16},{28,20},{1,9},{5... | collective-permute-start | bytes 24584 | tf_op jit(solution)/shard_map/ppermute | solution.py:547
  47.3 1.1 %collective-permute-done.8 = f32[16,128]{1,0:T(8,128)S(1)} collective-permute-done((f32[16,128]{1,0:T(8,128)S(1)}, f32[16,128]{1,0:T(8,128)S(1)}, u32[]{:S(2)}, u32[]{:S(2)}) %collective-permute-start.8) | collective-permute-done | bytes 8224 | tf_op jit(solution)/shard_map/ppermute | solution.py:547
  48.3 2.7 %collective-permute-done.7 = f32[16,128]{1,0:T(8,128)S(1)} collective-permute-done((f32[16,128]{1,0:T(8,128)S(1)}, f32[16,128]{1,0:T(8,128)S(1)}, u32[]{:S(2)}, u32[]{:S(2)}) %collective-permute-start.7) | collective-permute-done | bytes 8224 | tf_op jit(solution)/shard_map/ppermute | solution.py:547
  51.0 0.0 collective-permute-done.6
  51.0 1.6 %collective-permute-start.9 = (f32[16,128]{1,0:T(8,128)S(1)}, f32[16,128]{1,0:T(8,128)S(1)}, u32[]{:S(2)}, u32[]{:S(2)}) collective-permute-start(f32[16,128]{1,0:T(8,128)S(1)} %add_add_fusion.refs_0_), channel_id=1, source_target_pairs={{0,4},{4,0},{8,12},{12,8},{16,20},{20,16},{24,28},{28,24},{1,5},{5... | collective-permute-start | bytes 24584 | tf_op jit(solution)/shard_map/ppermute | solution.py:547
  52.6 2.2 %collective-permute-done.9.refs_1_ = f32[16,128]{1,0:T(8,128)S(1)} collective-permute-done((f32[16,128]{1,0:T(8,128)S(1)}, f32[16,128]{1,0:T(8,128)S(1)}, u32[]{:S(2)}, u32[]{:S(2)}) %collective-permute-start.9) | collective-permute-done | bytes 8224 | tf_op jit(solution)/shard_map/ppermute | solution.py:547
  54.8 0.8 %last.1 = (f32[64,64]{1,0:T(8,128)}, f32[1,8]{1,0:T(1,128)}, f32[1,127]{1,0:T(1,128)}, f32[1,1]{1,0:T(1,128)}) custom-call(f32[16,128]{1,0:T(8,128)S(1)} %add_add_fusion.refs_0_, f32[16,128]{1,0:T(8,128)S(1)} %collective-permute-done.9.refs_1_), custom_call_target="tpu_custom_call" | custom-call | tf_op jit(solution)/shard_map/last/pallas_call | solution.py:661
  (2 shorter events, 0.0 us)
Async XLA Ops:
  13.7 5.3 %collective-permute-start.2 = (f32[64,256]{1,0:T(8,128)S(1)}, f32[64,256]{1,0:T(8,128)S(1)}, u32[]{:S(2)}, u32[]{:S(2)}) collective-permute-start(f32[64,256]{1,0:T(8,128)S(1)} %get-tuple-element.23.refs_0_), channel_id=1, source_target_pairs={{0,3},{1,2},{2,1},{3,0},{4,7},{5,6},{6,5},{7,4},{8,11},{9,10},{10,... | collective-permute-start | bytes 196616 | tf_op jit(solution)/shard_map/ppermute | solution.py:547
  16.2 4.7 %collective-permute-start.1 = (f32[64,256]{1,0:T(8,128)S(1)}, f32[64,256]{1,0:T(8,128)S(1)}, u32[]{:S(2)}, u32[]{:S(2)}) collective-permute-start(f32[64,256]{1,0:T(8,128)S(1)} %get-tuple-element.23.refs_0_), channel_id=1, source_target_pairs={{0,2},{1,3},{2,0},{3,1},{4,6},{5,7},{6,4},{7,5},{8,10},{9,11},{10,... | collective-permute-start | bytes 196616 | tf_op jit(solution)/shard_map/ppermute | solution.py:547
  16.8 4.0 %collective-permute-start = (f32[64,256]{1,0:T(8,128)S(1)}, f32[64,256]{1,0:T(8,128)S(1)}, u32[]{:S(2)}, u32[]{:S(2)}) collective-permute-start(f32[64,256]{1,0:T(8,128)S(1)} %get-tuple-element.23.refs_0_), channel_id=1, source_target_pairs={{0,1},{1,0},{2,3},{3,2},{4,5},{5,4},{6,7},{7,6},{8,9},{9,8},{10,11... | collective-permute-start | bytes 196616 | tf_op jit(solution)/shard_map/ppermute | solution.py:547
  37.7 3.1 %collective-permute-start.5 = (f32[16,128]{1,0:T(8,128)S(1)}, f32[16,128]{1,0:T(8,128)S(1)}, u32[]{:S(2)}, u32[]{:S(2)}) collective-permute-start(f32[16,128]{1,0:T(8,128)S(1)} %down.1), channel_id=1, source_target_pairs={{0,3},{1,2},{2,1},{3,0},{4,7},{5,6},{6,5},{7,4},{8,11},{9,10},{10,... | collective-permute-start | bytes 24584 | tf_op jit(solution)/shard_map/ppermute | solution.py:547
  39.1 3.7 %collective-permute-start.4 = (f32[16,128]{1,0:T(8,128)S(1)}, f32[16,128]{1,0:T(8,128)S(1)}, u32[]{:S(2)}, u32[]{:S(2)}) collective-permute-start(f32[16,128]{1,0:T(8,128)S(1)} %down.1), channel_id=1, source_target_pairs={{0,2},{1,3},{2,0},{3,1},{4,6},{5,7},{6,4},{7,5},{8,10},{9,11},{10,... | collective-permute-start | bytes 24584 | tf_op jit(solution)/shard_map/ppermute | solution.py:547
  39.6 3.2 %collective-permute-start.3 = (f32[16,128]{1,0:T(8,128)S(1)}, f32[16,128]{1,0:T(8,128)S(1)}, u32[]{:S(2)}, u32[]{:S(2)}) collective-permute-start(f32[16,128]{1,0:T(8,128)S(1)} %down.1), channel_id=1, source_target_pairs={{0,1},{1,0},{2,3},{3,2},{4,5},{5,4},{6,7},{7,6},{8,9},{9,8},{10,11... | collective-permute-start | bytes 24584 | tf_op jit(solution)/shard_map/ppermute | solution.py:547
  42.8 5.5 %collective-permute-start.8 = (f32[16,128]{1,0:T(8,128)S(1)}, f32[16,128]{1,0:T(8,128)S(1)}, u32[]{:S(2)}, u32[]{:S(2)}) collective-permute-start(f32[16,128]{1,0:T(8,128)S(1)} %add_add_fusion.1), channel_id=1, source_target_pairs={{0,24},{4,28},{8,16},{12,20},{16,8},{20,12},{24,0},{28,4},{1,25},{... | collective-permute-start | bytes 24584 | tf_op jit(solution)/shard_map/ppermute | solution.py:547
  46.5 4.5 %collective-permute-start.7 = (f32[16,128]{1,0:T(8,128)S(1)}, f32[16,128]{1,0:T(8,128)S(1)}, u32[]{:S(2)}, u32[]{:S(2)}) collective-permute-start(f32[16,128]{1,0:T(8,128)S(1)} %add_add_fusion.1), channel_id=1, source_target_pairs={{0,16},{4,20},{8,24},{12,28},{16,0},{20,4},{24,8},{28,12},{1,17},{... | collective-permute-start | bytes 24584 | tf_op jit(solution)/shard_map/ppermute | solution.py:547
  46.5 4.5 %collective-permute-start.6 = (f32[16,128]{1,0:T(8,128)S(1)}, f32[16,128]{1,0:T(8,128)S(1)}, u32[]{:S(2)}, u32[]{:S(2)}) collective-permute-start(f32[16,128]{1,0:T(8,128)S(1)} %add_add_fusion.1), channel_id=1, source_target_pairs={{0,8},{4,12},{8,0},{12,4},{16,24},{20,28},{24,16},{28,20},{1,9},{5... | collective-permute-start | bytes 24584 | tf_op jit(solution)/shard_map/ppermute | solution.py:547
  51.0 3.7 %collective-permute-start.9 = (f32[16,128]{1,0:T(8,128)S(1)}, f32[16,128]{1,0:T(8,128)S(1)}, u32[]{:S(2)}, u32[]{:S(2)}) collective-permute-start(f32[16,128]{1,0:T(8,128)S(1)} %add_add_fusion.refs_0_), channel_id=1, source_target_pairs={{0,4},{4,0},{8,12},{12,8},{16,20},{20,16},{24,28},{28,24},{1,5},{5... | collective-permute-start | bytes 24584 | tf_op jit(solution)/shard_map/ppermute | solution.py:547

commit v7 on v6

--- a/solution.py
+++ b/solution.py
@@ -98,7 +98,7 @@
 def frequencies(freq_ref, sense_ref):
     twice = identity_twice()
     sense2 = sense_ref[...]
-    freq2 = exact(jnp.broadcast_to(freq_ref[...], (8, 64)), twice)[0:1] * sense2
+    freq2 = jnp.concatenate([freq_ref[...]] * 2, axis=1) * sense2
     total = 0.5 * jnp.sum(freq2, axis=1, keepdims=True)
     pi_row = freq2 / total
     pi_col = 0.5 * jnp.sum(twice * pi_row, axis=1, keepdims=True)
@@ -110,7 +110,8 @@
 
 def symmetric_table(ex_ref, single_ref, twice):
     ex = ex_ref[...]
-    return 0.5 * (exact(ex, twice) + exact_tn(ex, twice)) * single_ref[...]
+    both = ex + ex.T
+    return 0.5 * jnp.concatenate([both, both], axis=1) * single_ref[...]
 
 
 def class_pair(table, nonsyn, omega_ref, pair, twice, pi_row, pi_col):
@@ -506,10 +507,25 @@
         omega_row = jnp.where(lane_row == 2 * pair + 1, ratio1, omega_row)
     table_grad = table_grad + pltpu.roll(table_grad, 64, 1)
     masks, picks = neighbours()
-    packed = jnp.zeros((16, 128), F32)
-    for at_position, pick in zip(masks, picks):
-        some = jnp.where(at_position, 0.5 * table_grad, 0.0)
-        packed = packed + exact_tn(pick, some) + exact_tn(pick, exact_tn(some[:, 0:64], twice))
+    codon = lax.broadcasted_iota(jnp.int32, (16, 128), 1)
+    column = lax.broadcasted_iota(jnp.int32, (16, 128), 0)
+    lefts, rights = [], []
+    for p, digit in enumerate((codon // 16, codon // 4 % 4, codon % 4)):
+        left = jnp.where((column == 4 * p + digit) & (codon < 64), 1.0, 0.0).astype(BF)
+        for part in split(jnp.where(masks[p], 0.5 * table_grad, 0.0)):
+            lefts.append(left)
+            rights.append(part)
+    packed = mxu(
+        jnp.concatenate(lefts, axis=1),
+        jnp.concatenate([jnp.concatenate([part, jnp.zeros_like(part)], axis=0) for part in rights], axis=0),
+    )
+    turned = mxu_nt(
+        jnp.concatenate(lefts, axis=1),
+        jnp.concatenate([
+            jnp.concatenate([part, jnp.zeros_like(part)], axis=0) for part in rights
+        ], axis=1),
+    )
+    packed = packed + turned
     packed = jnp.where(lax.broadcasted_iota(jnp.int32, (16, 128), 1) < 64, packed, 0.0)
 
     even = jnp.sum(jnp.where(mask, slopes, 0.0), axis=1, keepdims=True)

time: 55.8 us -> 55.4 us (level)
  no operation moved by 1% of the time
where the time goes in v7:
time: 55.4 us; the launch traced here: 55.2 us
  Pallas kernels  32.6 us (59%)
  starting transfers between devices  11.1 us (20%)
  waiting for transfers between devices  10.8 us (19%)
  between operations  0.67 us (1%)
    pallas_call x1, Pallas kernels, body(): pl.pallas_call(functools.partial(down_kernel, total_sites, members), out_...  16.4 us
    pallas_call x1, Pallas kernels, body(): pl.pallas_call(up_kernel, out_shape=[shape((64, sites), F32), held((4, 2,...  13.1 us
    ppermute x10, starting transfers between devices, partners(): lax.ppermute(x, axis, [(i, i ^ step * start) for i in range(size)])  11.1 us
    ppermute x10, waiting for transfers between devices, partners(): lax.ppermute(x, axis, [(i, i ^ step * start) for i in range(size)])  10.8 us
    pallas_call x1, Pallas kernels, body(): pl.pallas_call(side_kernel, out_shape=[held((STRIDE * 64, 128), F32), hel...  2.21 us
  transfers between devices with their start and end apart: 10, of which 6 were waited for; matrix products, arithmetic and copies ran while one was open for 0% of the time, Pallas kernels for 4%

profile of v7, /device:TPU:0, one launch (start us, length us, event | category | flops | bytes accessed | tf_op | source)
XLA Modules:
  0.0 55.2 jit_solution(10274879789444080235)
XLA Ops:
  0.6 13.1 %up.1 = (f32[64,256]{1,0:T(8,128)S(1)}, bf16[4,2,64,64,128]{4,3,2,1,0:T(8,128)(2,1)S(1)}, f32[64,64,128]{2,1,0:T(8,128)S(1)}, f32[4,4,64,128]{3,2,1,0:T(8,128)S(...) custom-call(s32[256,256]{1,0:T(8,128)} %states_ref.1, ...), custom_call_target="tpu_custom_call" | custom-call | tf_op jit(solution)/shard_map/up/pallas_call | solution.py:610
  13.8 2.4 %collective-permute-start.2 = (f32[64,256]{1,0:T(8,128)S(1)}, f32[64,256]{1,0:T(8,128)S(1)}, u32[]{:S(2)}, u32[]{:S(2)}) collective-permute-start(f32[64,256]{1,0:T(8,128)S(1)} %get-tuple-element.23.refs_0_), channel_id=1, source_target_pairs={{0,3},{1,2},{2,1},{3,0},{4,7},{5,6},{6,5},{7,4},{8,11},{9,10},{10,... | collective-permute-start | bytes 196616 | tf_op jit(solution)/shard_map/ppermute | solution.py:563
  16.2 0.6 %collective-permute-start.1 = (f32[64,256]{1,0:T(8,128)S(1)}, f32[64,256]{1,0:T(8,128)S(1)}, u32[]{:S(2)}, u32[]{:S(2)}) collective-permute-start(f32[64,256]{1,0:T(8,128)S(1)} %get-tuple-element.23.refs_0_), channel_id=1, source_target_pairs={{0,2},{1,3},{2,0},{3,1},{4,6},{5,7},{6,4},{7,5},{8,10},{9,11},{10,... | collective-permute-start | bytes 196616 | tf_op jit(solution)/shard_map/ppermute | solution.py:563
  16.9 0.0 collective-permute-start
  16.9 2.2 %side.1 = (f32[4160,128]{1,0:T(8,128)S(1)}, bf16[64,64,256]{2,1,0:T(8,128)(2,1)S(1)}, f32[128,128]{1,0:T(8,128)S(1)}) custom-call(f32[4160,128]{1,0:T(8,128)S(1)} %get-tuple-element.24.dup_ref, f32[64,64,128]{2,1,0:T(8,128)S(1)} %get-tuple-element.25.last_ref, f32[1,127]{1,0:T(1,128)} %bitcast.8, s32[1,127]{1,0:T(1,128)} %bitcast.10, ...), custom_call_target="tpu_custom_call" | custom-call | tf_op jit(solution)/shard_map/side/pallas_call | solution.py:642
  19.1 0.0 collective-permute-done.2.refs_3_
  19.1 1.8 %collective-permute-done.1.refs_2_ = f32[64,256]{1,0:T(8,128)S(1)} collective-permute-done((f32[64,256]{1,0:T(8,128)S(1)}, f32[64,256]{1,0:T(8,128)S(1)}, u32[]{:S(2)}, u32[]{:S(2)}) %collective-permute-start.1) | collective-permute-done | bytes 65568 | tf_op jit(solution)/shard_map/ppermute | solution.py:563
  20.9 0.0 collective-permute-done.refs_1_
  20.9 16.4 %down.1 = f32[16,128]{1,0:T(8,128)S(1)} custom-call(f32[64,256]{1,0:T(8,128)S(1)} %get-tuple-element.23.refs_0_, f32[64,256]{1,0:T(8,128)S(1)} %collective-permute-done.refs_1_, f32[64,256]{1,0:T(8,128)S(1)} %collective-permute-done.1.refs_2_, f32[64,256]{1,0:T(8,128)S(1)} %collective-permute-done.2.refs_3_, ...), custom_call_target="tpu_custom_call" | custom-call | tf_op jit(solution)/shard_map/down/pallas_call | solution.py:654
  37.4 1.4 %collective-permute-start.5 = (f32[16,128]{1,0:T(8,128)S(1)}, f32[16,128]{1,0:T(8,128)S(1)}, u32[]{:S(2)}, u32[]{:S(2)}) collective-permute-start(f32[16,128]{1,0:T(8,128)S(1)} %down.1), channel_id=1, source_target_pairs={{0,3},{1,2},{2,1},{3,0},{4,7},{5,6},{6,5},{7,4},{8,11},{9,10},{10,... | collective-permute-start | bytes 24584 | tf_op jit(solution)/shard_map/ppermute | solution.py:563
  38.8 0.4 collective-permute-start.4
  39.2 0.1 collective-permute-start.3
  39.3 1.2 %collective-permute-done.5 = f32[16,128]{1,0:T(8,128)S(1)} collective-permute-done((f32[16,128]{1,0:T(8,128)S(1)}, f32[16,128]{1,0:T(8,128)S(1)}, u32[]{:S(2)}, u32[]{:S(2)}) %collective-permute-start.5) | collective-permute-done | bytes 8224 | tf_op jit(solution)/shard_map/ppermute | solution.py:563
  40.5 2.0 %collective-permute-done.4 = f32[16,128]{1,0:T(8,128)S(1)} collective-permute-done((f32[16,128]{1,0:T(8,128)S(1)}, f32[16,128]{1,0:T(8,128)S(1)}, u32[]{:S(2)}, u32[]{:S(2)}) %collective-permute-start.4) | collective-permute-done | bytes 8224 | tf_op jit(solution)/shard_map/ppermute | solution.py:563
  42.4 0.0 collective-permute-done.3
  42.4 3.7 %collective-permute-start.8 = (f32[16,128]{1,0:T(8,128)S(1)}, f32[16,128]{1,0:T(8,128)S(1)}, u32[]{:S(2)}, u32[]{:S(2)}) collective-permute-start(f32[16,128]{1,0:T(8,128)S(1)} %add_add_fusion.1), channel_id=1, source_target_pairs={{0,24},{4,28},{8,16},{12,20},{16,8},{20,12},{24,0},{28,4},{1,25},{... | collective-permute-start | bytes 24584 | tf_op jit(solution)/shard_map/ppermute | solution.py:563
  46.1 0.0 collective-permute-start.7
  46.1 0.8 %collective-permute-start.6 = (f32[16,128]{1,0:T(8,128)S(1)}, f32[16,128]{1,0:T(8,128)S(1)}, u32[]{:S(2)}, u32[]{:S(2)}) collective-permute-start(f32[16,128]{1,0:T(8,128)S(1)} %add_add_fusion.1), channel_id=1, source_target_pairs={{0,8},{4,12},{8,0},{12,4},{16,24},{20,28},{24,16},{28,20},{1,9},{5... | collective-permute-start | bytes 24584 | tf_op jit(solution)/shard_map/ppermute | solution.py:563
  46.9 1.1 %collective-permute-done.8 = f32[16,128]{1,0:T(8,128)S(1)} collective-permute-done((f32[16,128]{1,0:T(8,128)S(1)}, f32[16,128]{1,0:T(8,128)S(1)}, u32[]{:S(2)}, u32[]{:S(2)}) %collective-permute-start.8) | collective-permute-done | bytes 8224 | tf_op jit(solution)/shard_map/ppermute | solution.py:563
  48.0 2.7 %collective-permute-done.7 = f32[16,128]{1,0:T(8,128)S(1)} collective-permute-done((f32[16,128]{1,0:T(8,128)S(1)}, f32[16,128]{1,0:T(8,128)S(1)}, u32[]{:S(2)}, u32[]{:S(2)}) %collective-permute-start.7) | collective-permute-done | bytes 8224 | tf_op jit(solution)/shard_map/ppermute | solution.py:563
  50.7 0.0 collective-permute-done.6
  50.7 1.6 %collective-permute-start.9 = (f32[16,128]{1,0:T(8,128)S(1)}, f32[16,128]{1,0:T(8,128)S(1)}, u32[]{:S(2)}, u32[]{:S(2)}) collective-permute-start(f32[16,128]{1,0:T(8,128)S(1)} %add_add_fusion.refs_0_), channel_id=1, source_target_pairs={{0,4},{4,0},{8,12},{12,8},{16,20},{20,16},{24,28},{28,24},{1,5},{5... | collective-permute-start | bytes 24584 | tf_op jit(solution)/shard_map/ppermute | solution.py:563
  52.3 2.1 %collective-permute-done.9.refs_1_ = f32[16,128]{1,0:T(8,128)S(1)} collective-permute-done((f32[16,128]{1,0:T(8,128)S(1)}, f32[16,128]{1,0:T(8,128)S(1)}, u32[]{:S(2)}, u32[]{:S(2)}) %collective-permute-start.9) | collective-permute-done | bytes 8224 | tf_op jit(solution)/shard_map/ppermute | solution.py:563
  54.4 0.8 %last.1 = (f32[64,64]{1,0:T(8,128)}, f32[1,8]{1,0:T(1,128)}, f32[1,127]{1,0:T(1,128)}, f32[1,1]{1,0:T(1,128)}) custom-call(f32[16,128]{1,0:T(8,128)S(1)} %add_add_fusion.refs_0_, f32[16,128]{1,0:T(8,128)S(1)} %collective-permute-done.9.refs_1_), custom_call_target="tpu_custom_call" | custom-call | tf_op jit(solution)/shard_map/last/pallas_call | solution.py:677
  (2 shorter events, 0.0 us)
Async XLA Ops:
  13.8 5.3 %collective-permute-start.2 = (f32[64,256]{1,0:T(8,128)S(1)}, f32[64,256]{1,0:T(8,128)S(1)}, u32[]{:S(2)}, u32[]{:S(2)}) collective-permute-start(f32[64,256]{1,0:T(8,128)S(1)} %get-tuple-element.23.refs_0_), channel_id=1, source_target_pairs={{0,3},{1,2},{2,1},{3,0},{4,7},{5,6},{6,5},{7,4},{8,11},{9,10},{10,... | collective-permute-start | bytes 196616 | tf_op jit(solution)/shard_map/ppermute | solution.py:563
  16.2 4.7 %collective-permute-start.1 = (f32[64,256]{1,0:T(8,128)S(1)}, f32[64,256]{1,0:T(8,128)S(1)}, u32[]{:S(2)}, u32[]{:S(2)}) collective-permute-start(f32[64,256]{1,0:T(8,128)S(1)} %get-tuple-element.23.refs_0_), channel_id=1, source_target_pairs={{0,2},{1,3},{2,0},{3,1},{4,6},{5,7},{6,4},{7,5},{8,10},{9,11},{10,... | collective-permute-start | bytes 196616 | tf_op jit(solution)/shard_map/ppermute | solution.py:563
  16.9 4.0 %collective-permute-start = (f32[64,256]{1,0:T(8,128)S(1)}, f32[64,256]{1,0:T(8,128)S(1)}, u32[]{:S(2)}, u32[]{:S(2)}) collective-permute-start(f32[64,256]{1,0:T(8,128)S(1)} %get-tuple-element.23.refs_0_), channel_id=1, source_target_pairs={{0,1},{1,0},{2,3},{3,2},{4,5},{5,4},{6,7},{7,6},{8,9},{9,8},{10,11... | collective-permute-start | bytes 196616 | tf_op jit(solution)/shard_map/ppermute | solution.py:563
  37.4 3.1 %collective-permute-start.5 = (f32[16,128]{1,0:T(8,128)S(1)}, f32[16,128]{1,0:T(8,128)S(1)}, u32[]{:S(2)}, u32[]{:S(2)}) collective-permute-start(f32[16,128]{1,0:T(8,128)S(1)} %down.1), channel_id=1, source_target_pairs={{0,3},{1,2},{2,1},{3,0},{4,7},{5,6},{6,5},{7,4},{8,11},{9,10},{10,... | collective-permute-start | bytes 24584 | tf_op jit(solution)/shard_map/ppermute | solution.py:563
  38.8 3.7 %collective-permute-start.4 = (f32[16,128]{1,0:T(8,128)S(1)}, f32[16,128]{1,0:T(8,128)S(1)}, u32[]{:S(2)}, u32[]{:S(2)}) collective-permute-start(f32[16,128]{1,0:T(8,128)S(1)} %down.1), channel_id=1, source_target_pairs={{0,2},{1,3},{2,0},{3,1},{4,6},{5,7},{6,4},{7,5},{8,10},{9,11},{10,... | collective-permute-start | bytes 24584 | tf_op jit(solution)/shard_map/ppermute | solution.py:563
  39.2 3.3 %collective-permute-start.3 = (f32[16,128]{1,0:T(8,128)S(1)}, f32[16,128]{1,0:T(8,128)S(1)}, u32[]{:S(2)}, u32[]{:S(2)}) collective-permute-start(f32[16,128]{1,0:T(8,128)S(1)} %down.1), channel_id=1, source_target_pairs={{0,1},{1,0},{2,3},{3,2},{4,5},{5,4},{6,7},{7,6},{8,9},{9,8},{10,11... | collective-permute-start | bytes 24584 | tf_op jit(solution)/shard_map/ppermute | solution.py:563
  42.4 5.5 %collective-permute-start.8 = (f32[16,128]{1,0:T(8,128)S(1)}, f32[16,128]{1,0:T(8,128)S(1)}, u32[]{:S(2)}, u32[]{:S(2)}) collective-permute-start(f32[16,128]{1,0:T(8,128)S(1)} %add_add_fusion.1), channel_id=1, source_target_pairs={{0,24},{4,28},{8,16},{12,20},{16,8},{20,12},{24,0},{28,4},{1,25},{... | collective-permute-start | bytes 24584 | tf_op jit(solution)/shard_map/ppermute | solution.py:563
  46.1 4.5 %collective-permute-start.7 = (f32[16,128]{1,0:T(8,128)S(1)}, f32[16,128]{1,0:T(8,128)S(1)}, u32[]{:S(2)}, u32[]{:S(2)}) collective-permute-start(f32[16,128]{1,0:T(8,128)S(1)} %add_add_fusion.1), channel_id=1, source_target_pairs={{0,16},{4,20},{8,24},{12,28},{16,0},{20,4},{24,8},{28,12},{1,17},{... | collective-permute-start | bytes 24584 | tf_op jit(solution)/shard_map/ppermute | solution.py:563
  46.1 4.5 %collective-permute-start.6 = (f32[16,128]{1,0:T(8,128)S(1)}, f32[16,128]{1,0:T(8,128)S(1)}, u32[]{:S(2)}, u32[]{:S(2)}) collective-permute-start(f32[16,128]{1,0:T(8,128)S(1)} %add_add_fusion.1), channel_id=1, source_target_pairs={{0,8},{4,12},{8,0},{12,4},{16,24},{20,28},{24,16},{28,20},{1,9},{5... | collective-permute-start | bytes 24584 | tf_op jit(solution)/shard_map/ppermute | solution.py:563
  50.7 3.7 %collective-permute-start.9 = (f32[16,128]{1,0:T(8,128)S(1)}, f32[16,128]{1,0:T(8,128)S(1)}, u32[]{:S(2)}, u32[]{:S(2)}) collective-permute-start(f32[16,128]{1,0:T(8,128)S(1)} %add_add_fusion.refs_0_), channel_id=1, source_target_pairs={{0,4},{4,0},{8,12},{12,8},{16,20},{20,16},{24,28},{28,24},{1,5},{5... | collective-permute-start | bytes 24584 | tf_op jit(solution)/shard_map/ppermute | solution.py:563

commit v8 on v7

--- a/solution.py
+++ b/solution.py
@@ -81,12 +81,22 @@
     return mxu(matrix, jnp.concatenate([high, low, high, low], axis=0))
 
 
-def double(ref, p, x):
+def doubled(x):
     mask = low_half()
     swapped = pltpu.roll(x, 64, 1)
-    for e, both in enumerate((jnp.where(mask, x, swapped), jnp.where(mask, swapped, x))):
+    return jnp.where(mask, x, swapped), jnp.where(mask, swapped, x)
+
+
+def double(ref, p, x):
+    for e, both in enumerate(doubled(x)):
         high, low = split(both)
         ref[2 * p + e] = jnp.concatenate([high, low], axis=1)
+
+
+def side_by_side(ref, p, x):
+    for e, both in enumerate(doubled(x)):
+        rest = both - both.astype(BF).astype(F32)
+        ref[2 * p + e] = jnp.where(low_half(), both, rest).astype(BF)
 
 
 def identity_twice():
@@ -200,7 +210,7 @@
     ex_ref, freq_ref, omega_ref, len_ref, cls_ref, sense_ref, single_ref, nonsyn_ref,
     top_ref, chain_ref, last_ref, power_ref, dup_ref, fixed_ref,
     message_ref, high_ref, low_ref, leaf_ref, scale_ref, inverse_ref,
-    first_ref, up_ref,
+    first_ref, up_ref, thin_ref,
 ):
     subtree = lax.axis_index("branch")
     mask = low_half()
@@ -249,7 +259,7 @@
 
     expand(jnp.where(low_half(), even, odd), dup_ref, store)
 
-    def squarings(step, carry):
+    def squarings(leaves, step, carry):
         width = 16
         held = [first_ref[pl.ds(step * width + j, 64, stride=STRIDE), :] for j in range(width)]
         zero = jnp.zeros((128, 128), BF)
@@ -276,12 +286,17 @@
                     )
         for j in range(width):
             p = step * width + j
-            last_ref[p] = held[j]
-            double(up_ref, p, inverse_root_col * (held[j] + twice) * root_row)
+            matrix = inverse_root_col * (held[j] + twice) * root_row
+            if leaves:
+                side_by_side(thin_ref, p, matrix)
+            else:
+                last_ref[p - 32] = held[j]
+                double(up_ref, p - 32, matrix)
         return carry
 
     inverse_root_col = 1.0 / root_col
-    lax.fori_loop(0, PAIRS // 16, squarings, 0)
+    lax.fori_loop(0, 2, functools.partial(squarings, True), 0)
+    lax.fori_loop(2, 4, functools.partial(squarings, False), 0)
 
     def finish(p, message):
         message_ref[p] = jnp.concatenate(message, axis=0)
@@ -296,13 +311,14 @@
 
     for p in range(32):
         both = [leaf_ref[p, 64 * e : 64 * e + 64, :] for e in range(2)]
-        nothing = jnp.zeros_like(both[0])
-        finish(p, [messages(up_ref[2 * p + e], both[e], nothing) for e in range(2)])
+        finish(p, [
+            mxu(thin_ref[2 * p + e], jnp.concatenate([both[e], both[e]], axis=0)) for e in range(2)
+        ])
 
     def inner(p):
         child = 2 * p - 64
         return [
-            messages(up_ref[2 * p + e], high_ref[child + e], low_ref[child + e]) for e in range(2)
+            messages(up_ref[child + e], high_ref[child + e], low_ref[child + e]) for e in range(2)
         ]
 
     for p in range(32, 48):
@@ -335,7 +351,7 @@
     def matrices(step, carry):
         for j in range(8):
             r = step * 8 + j
-            double(matrix_ref, r, root_col * (last_ref[32 + r] + twice) * inverse_root_row)
+            double(matrix_ref, r, root_col * (last_ref[r] + twice) * inverse_root_row)
         return carry
 
     lax.fori_loop(0, 4, matrices, 0)
@@ -539,11 +555,10 @@
     out_ref[...] = packed + jnp.where(line == 12 + subtree, length_row, 0.0)
 
 
-def last_kernel(total_sites, count, *refs):
+def last_kernel(total_sites, own_ref, got_ref, exch_ref, omega_ref, length_ref, log_ref):
     members = lax.axis_size("branch")
     subtree = lax.axis_index("branch")
-    exch_ref, omega_ref, length_ref, log_ref = refs[count:]
-    total = tree_sum([ref[...] for ref in refs[:count]])
+    total = jnp.where(subtree % 2 == 1, own_ref[...], got_ref[...])
     masks, picks = neighbours()
     table = jnp.zeros((64, 128), F32)
     for at_position, pick in zip(masks, picks):
@@ -572,13 +587,20 @@
     return parts[0]
 
 
-def axis_steps(axis):
-    size, start, steps = lax.axis_size(axis), 1, []
+def sum_stages(x, axes, size):
+    stages, start = [(1, 2)], 2
     while start < size:
-        radix = 2 if size // start in (2, 8) else 4
-        steps.append((axis, start, radix))
+        radix = min(4, size // start)
+        stages.append((start, radix))
         start *= radix
-    return steps[::-1]
+    for start, radix in stages:
+        x = tree_sum([x] + [
+            lax.ppermute(x, axes, [
+                (i, i ^ (step * start)) for i in range(size) if start == 1 or i % 2
+            ])
+            for step in range(1, radix)
+        ])
+    return x, lax.ppermute(x, axes, [(i, i - 1) for i in range(1, size, 2)])
 
 
 def body(
@@ -612,7 +634,7 @@
         out_shape=[
             shape((64, sites), F32),
             held((4, 2, PAIRS, 64, 128), BF),
-            held((PAIRS, 64, 128), F32),
+            held((PAIRS // 2, 64, 128), F32),
             held((CLASSES // 2, 4, 64, 128), F32),
             held((STRIDE * 64, 128), F32),
             held((7, 64, 128), F32),
@@ -627,7 +649,8 @@
         out_specs=[vmem] * 12,
         scratch_shapes=[
             pltpu.VMEM((STRIDE * 64, 128), F32),
-            pltpu.VMEM((2 * PAIRS, 64, 256), BF),
+            pltpu.VMEM((PAIRS, 64, 256), BF),
+            pltpu.VMEM((PAIRS, 64, 128), BF),
         ],
         compiler_params=limit,
         name="up",
@@ -670,12 +693,9 @@
         chain, turned, slope, powers, fixed,
         outside(weights.reshape(1, sites)), omega, single2, nonsyn2,
     )
-    steps = axis_steps("branch") + axis_steps("site")
-    for step in steps[:-1]:
-        part = tree_sum(partners(part, *step))
-    parts = partners(part, *steps[-1])
+    parts = sum_stages(part, ("site", "branch"), members * lax.axis_size("site"))
     exch, ratio, length, loglik = pl.pallas_call(
-        functools.partial(last_kernel, total_sites, len(parts)),
+        functools.partial(last_kernel, total_sites),
         out_shape=[shape((64, 64), F32), shape((1, CLASSES), F32), shape((1, EDGES), F32), shape((1, 1), F32)],
         in_specs=[vmem] * len(parts),
         out_specs=[vmem] * 4,

time: 55.4 us -> 66.6 us (1.20)
  waiting for transfers between devices: 10.8 us -> 24.7 us
  starting transfers between devices: 11.1 us -> 8.61 us
    ppermute x0 -> x8, waiting for transfers between devices: none -> 22.9 us  [the longest x1 21.9 us: sum_stages(): return (x, lax.ppermute(x, axes, [(i, i - 1) for i in range(1, size, 2)]))]
    ppermute x10 -> x3, waiting for transfers between devices: 10.8 us -> 1.76 us  [partners(): lax.ppermute(x, axis, [(i, i ^ step * start) for i in range(size)])]
    ppermute x10 -> x3, starting transfers between devices: 11.1 us -> 3.15 us  [partners(): lax.ppermute(x, axis, [(i, i ^ step * start) for i in range(size)])]
    ppermute x0 -> x8, starting transfers between devices: none -> 5.46 us  [the longest x7 4.16 us: sum_stages(): lax.ppermute(x, axes, [(i, i ^ step * start) for i in range(size) if star...]
  transfers between devices with their start and end apart: 10 -> 11, of which waited for: 6 -> 4; matrix products, arithmetic and copies ran while one was open for 0% -> 0% of each run, Pallas kernels for 4% -> 3%
where the time goes in v8:
time: 66.6 us; the launch traced here: 66.2 us
  Pallas kernels  32.1 us (48%)
  waiting for transfers between devices  24.7 us (37%)
  starting transfers between devices  8.61 us (13%)
  between operations  0.78 us (1%)
    ppermute x1, waiting for transfers between devices, sum_stages(): return (x, lax.ppermute(x, axes, [(i, i - 1) for i in range(1, size, 2)]))  21.9 us
    pallas_call x1, Pallas kernels, body(): pl.pallas_call(functools.partial(down_kernel, total_sites, members), out_...  16.4 us
    pallas_call x1, Pallas kernels, body(): pl.pallas_call(up_kernel, out_shape=[shape((64, sites), F32), held((4, 2,...  12.7 us
    ppermute x7, starting transfers between devices, sum_stages(): lax.ppermute(x, axes, [(i, i ^ step * start) for i in range(size) if star...  4.16 us
    ppermute x3, starting transfers between devices, partners(): lax.ppermute(x, axis, [(i, i ^ step * start) for i in range(size)])  3.15 us
    pallas_call x1, Pallas kernels, body(): pl.pallas_call(side_kernel, out_shape=[held((STRIDE * 64, 128), F32), hel...  2.2 us
    ppermute x3, waiting for transfers between devices, partners(): lax.ppermute(x, axis, [(i, i ^ step * start) for i in range(size)])  1.76 us
  transfers between devices with their start and end apart: 11, of which 4 were waited for; matrix products, arithmetic and copies ran while one was open for 0% of the time, Pallas kernels for 3%

profile of v8, /device:TPU:0, one launch (start us, length us, event | category | flops | bytes accessed | tf_op | source)
XLA Modules:
  0.0 66.2 jit_solution(13185128778505878947)
XLA Ops:
  0.6 12.7 %up.1 = (f32[64,256]{1,0:T(8,128)S(1)}, bf16[4,2,64,64,128]{4,3,2,1,0:T(8,128)(2,1)S(1)}, f32[32,64,128]{2,1,0:T(8,128)S(1)}, f32[4,4,64,128]{3,2,1,0:T(8,128)S(...) custom-call(s32[256,256]{1,0:T(8,128)} %states_ref.1, ...), custom_call_target="tpu_custom_call" | custom-call | tf_op jit(solution)/shard_map/up/pallas_call | solution.py:632
  13.3 0.5 collective-permute-start
  13.8 2.6 %collective-permute-start.1 = (f32[64,256]{1,0:T(8,128)S(1)}, f32[64,256]{1,0:T(8,128)S(1)}, u32[]{:S(2)}, u32[]{:S(2)}) collective-permute-start(f32[64,256]{1,0:T(8,128)S(1)} %get-tuple-element.23.refs_0_), channel_id=1, source_target_pairs={{0,2},{1,3},{2,0},{3,1},{4,6},{5,7},{6,4},{7,5},{8,10},{9,11},{10,... | collective-permute-start | bytes 196616 | tf_op jit(solution)/shard_map/ppermute | solution.py:578
  16.4 0.1 collective-permute-start.2
  16.4 2.2 %side.1 = (f32[4160,128]{1,0:T(8,128)S(1)}, bf16[64,64,256]{2,1,0:T(8,128)(2,1)S(1)}, f32[128,128]{1,0:T(8,128)S(1)}) custom-call(f32[4160,128]{1,0:T(8,128)S(1)} %get-tuple-element.24.dup_ref, f32[32,64,128]{2,1,0:T(8,128)S(1)} %get-tuple-element.25.last_ref, f32[1,127]{1,0:T(1,128)} %bitcast.8, s32[1,127]{1,0:T(1,128)} %bitcast.10, ...), custom_call_target="tpu_custom_call" | custom-call | tf_op jit(solution)/shard_map/side/pallas_call | solution.py:665
  18.7 0.0 collective-permute-done.refs_1_
  18.7 0.4 collective-permute-done.1.refs_2_
  19.1 1.4 %collective-permute-done.2.refs_3_ = f32[64,256]{1,0:T(8,128)S(1)} collective-permute-done((f32[64,256]{1,0:T(8,128)S(1)}, f32[64,256]{1,0:T(8,128)S(1)}, u32[]{:S(2)}, u32[]{:S(2)}) %collective-permute-start.2) | collective-permute-done | bytes 65568 | tf_op jit(solution)/shard_map/ppermute | solution.py:578
  20.4 16.4 %down.1 = f32[16,128]{1,0:T(8,128)S(1)} custom-call(f32[64,256]{1,0:T(8,128)S(1)} %get-tuple-element.23.refs_0_, f32[64,256]{1,0:T(8,128)S(1)} %collective-permute-done.refs_1_, f32[64,256]{1,0:T(8,128)S(1)} %collective-permute-done.1.refs_2_, f32[64,256]{1,0:T(8,128)S(1)} %collective-permute-done.2.refs_3_, ...), custom_call_target="tpu_custom_call" | custom-call | tf_op jit(solution)/shard_map/down/pallas_call | solution.py:677
  36.9 0.2 collective-permute-start.3
  37.1 1.0 %collective-permute-done.3 = f32[16,128]{1,0:T(8,128)S(1)} collective-permute-done((f32[16,128]{1,0:T(8,128)S(1)}, f32[16,128]{1,0:T(8,128)S(1)}, u32[]{:S(2)}, u32[]{:S(2)}) %collective-permute-start.3) | collective-permute-done | bytes 8224 | tf_op jit(solution)/shard_map/ppermute | solution.py:598
  38.1 0.7 collective-permute-start.4
  38.7 0.7 collective-permute-start.5
  39.4 0.7 collective-permute-start.6
  40.1 0.0 collective-permute-done.4
  40.1 0.0 collective-permute-done.5
  40.1 0.0 collective-permute-done.6
  40.1 0.7 collective-permute-start.7
  40.8 0.7 collective-permute-start.8
  41.5 0.7 collective-permute-start.9
  42.1 0.0 collective-permute-done.7
  42.1 0.0 collective-permute-done.8
  42.2 0.0 collective-permute-done.9
  42.2 1.3 %collective-permute-start.10 = (f32[16,128]{1,0:T(8,128)S(1)}, f32[16,128]{1,0:T(8,128)S(1)}, u32[]{:S(2)}, u32[]{:S(2)}) collective-permute-start(f32[16,128]{1,0:T(8,128)S(1)} %add_add_fusion.own_ref), channel_id=1, source_target_pairs={{1,0},{3,2},{5,4},{7,6},{9,8},{11,10},{13,12},{15,14},{17,16},{19,... | collective-permute-start | bytes 24584 | tf_op jit(solution)/shard_map/ppermute | solution.py:603
  43.5 21.9 %collective-permute-done.10.got_ref = f32[16,128]{1,0:T(8,128)S(1)} collective-permute-done((f32[16,128]{1,0:T(8,128)S(1)}, f32[16,128]{1,0:T(8,128)S(1)}, u32[]{:S(2)}, u32[]{:S(2)}) %collective-permute-start.10) | collective-permute-done | bytes 8224 | tf_op jit(solution)/shard_map/ppermute | solution.py:603
  65.4 0.9 %last.1 = (f32[64,64]{1,0:T(8,128)}, f32[1,8]{1,0:T(1,128)}, f32[1,127]{1,0:T(1,128)}, f32[1,1]{1,0:T(1,128)}) custom-call(f32[16,128]{1,0:T(8,128)S(1)} %add_add_fusion.own_ref, f32[16,128]{1,0:T(8,128)S(1)} %collective-permute-done.10.got_ref), custom_call_target="tpu_custom_call" | custom-call | tf_op jit(solution)/shard_map/last/pallas_call | solution.py:697
  (3 shorter events, 0.0 us)
Async XLA Ops:
  13.3 5.4 %collective-permute-start = (f32[64,256]{1,0:T(8,128)S(1)}, f32[64,256]{1,0:T(8,128)S(1)}, u32[]{:S(2)}, u32[]{:S(2)}) collective-permute-start(f32[64,256]{1,0:T(8,128)S(1)} %get-tuple-element.23.refs_0_), channel_id=1, source_target_pairs={{0,1},{1,0},{2,3},{3,2},{4,5},{5,4},{6,7},{7,6},{8,9},{9,8},{10,11... | collective-permute-start | bytes 196616 | tf_op jit(solution)/shard_map/ppermute | solution.py:578
  13.8 5.3 %collective-permute-start.1 = (f32[64,256]{1,0:T(8,128)S(1)}, f32[64,256]{1,0:T(8,128)S(1)}, u32[]{:S(2)}, u32[]{:S(2)}) collective-permute-start(f32[64,256]{1,0:T(8,128)S(1)} %get-tuple-element.23.refs_0_), channel_id=1, source_target_pairs={{0,2},{1,3},{2,0},{3,1},{4,6},{5,7},{6,4},{7,5},{8,10},{9,11},{10,... | collective-permute-start | bytes 196616 | tf_op jit(solution)/shard_map/ppermute | solution.py:578
  16.4 4.0 %collective-permute-start.2 = (f32[64,256]{1,0:T(8,128)S(1)}, f32[64,256]{1,0:T(8,128)S(1)}, u32[]{:S(2)}, u32[]{:S(2)}) collective-permute-start(f32[64,256]{1,0:T(8,128)S(1)} %get-tuple-element.23.refs_0_), channel_id=1, source_target_pairs={{0,3},{1,2},{2,1},{3,0},{4,7},{5,6},{6,5},{7,4},{8,11},{9,10},{10,... | collective-permute-start | bytes 196616 | tf_op jit(solution)/shard_map/ppermute | solution.py:578
  36.9 1.2 %collective-permute-start.3 = (f32[16,128]{1,0:T(8,128)S(1)}, f32[16,128]{1,0:T(8,128)S(1)}, u32[]{:S(2)}, u32[]{:S(2)}) collective-permute-start(f32[16,128]{1,0:T(8,128)S(1)} %down.1), channel_id=1, source_target_pairs={{0,1},{1,0},{2,3},{3,2},{4,5},{5,4},{6,7},{7,6},{8,9},{9,8},{10,11... | collective-permute-start | bytes 24584 | tf_op jit(solution)/shard_map/ppermute | solution.py:598
  38.1 2.0 %collective-permute-start.4 = (f32[16,128]{1,0:T(8,128)S(1)}, f32[16,128]{1,0:T(8,128)S(1)}, u32[]{:S(2)}, u32[]{:S(2)}) collective-permute-start(f32[16,128]{1,0:T(8,128)S(1)} %add.21), channel_id=1, source_target_pairs={{1,3},{3,1},{5,7},{7,5},{9,11},{11,9},{13,15},{15,13},{17,19},{19,... | collective-permute-start | bytes 24584 | tf_op jit(solution)/shard_map/ppermute | solution.py:598
  38.7 1.4 %collective-permute-start.5 = (f32[16,128]{1,0:T(8,128)S(1)}, f32[16,128]{1,0:T(8,128)S(1)}, u32[]{:S(2)}, u32[]{:S(2)}) collective-permute-start(f32[16,128]{1,0:T(8,128)S(1)} %add.21), channel_id=1, source_target_pairs={{1,5},{3,7},{5,1},{7,3},{9,13},{11,15},{13,9},{15,11},{17,21},{19,... | collective-permute-start | bytes 24584 | tf_op jit(solution)/shard_map/ppermute | solution.py:598
  39.4 0.7 %collective-permute-start.6 = (f32[16,128]{1,0:T(8,128)S(1)}, f32[16,128]{1,0:T(8,128)S(1)}, u32[]{:S(2)}, u32[]{:S(2)}) collective-permute-start(f32[16,128]{1,0:T(8,128)S(1)} %add.21), channel_id=1, source_target_pairs={{1,7},{3,5},{5,3},{7,1},{9,15},{11,13},{13,11},{15,9},{17,23},{19,... | collective-permute-start | bytes 24584 | tf_op jit(solution)/shard_map/ppermute | solution.py:598
  40.1 2.0 %collective-permute-start.7 = (f32[16,128]{1,0:T(8,128)S(1)}, f32[16,128]{1,0:T(8,128)S(1)}, u32[]{:S(2)}, u32[]{:S(2)}) collective-permute-start(f32[16,128]{1,0:T(8,128)S(1)} %add_add_fusion.1), channel_id=1, source_target_pairs={{1,9},{3,11},{5,13},{7,15},{9,1},{11,3},{13,5},{15,7},{17,25},{19,... | collective-permute-start | bytes 24584 | tf_op jit(solution)/shard_map/ppermute | solution.py:598
  40.8 1.4 %collective-permute-start.8 = (f32[16,128]{1,0:T(8,128)S(1)}, f32[16,128]{1,0:T(8,128)S(1)}, u32[]{:S(2)}, u32[]{:S(2)}) collective-permute-start(f32[16,128]{1,0:T(8,128)S(1)} %add_add_fusion.1), channel_id=1, source_target_pairs={{1,17},{3,19},{5,21},{7,23},{9,25},{11,27},{13,29},{15,31},{17,1},... | collective-permute-start | bytes 24584 | tf_op jit(solution)/shard_map/ppermute | solution.py:598
  41.5 0.7 %collective-permute-start.9 = (f32[16,128]{1,0:T(8,128)S(1)}, f32[16,128]{1,0:T(8,128)S(1)}, u32[]{:S(2)}, u32[]{:S(2)}) collective-permute-start(f32[16,128]{1,0:T(8,128)S(1)} %add_add_fusion.1), channel_id=1, source_target_pairs={{1,25},{3,27},{5,29},{7,31},{9,17},{11,19},{13,21},{15,23},{17,9},... | collective-permute-start | bytes 24584 | tf_op jit(solution)/shard_map/ppermute | solution.py:598
  42.2 23.2 %collective-permute-start.10 = (f32[16,128]{1,0:T(8,128)S(1)}, f32[16,128]{1,0:T(8,128)S(1)}, u32[]{:S(2)}, u32[]{:S(2)}) collective-permute-start(f32[16,128]{1,0:T(8,128)S(1)} %add_add_fusion.own_ref), channel_id=1, source_target_pairs={{1,0},{3,2},{5,4},{7,6},{9,8},{11,10},{13,12},{15,14},{17,16},{19,... | collective-permute-start | bytes 24584 | tf_op jit(solution)/shard_map/ppermute | solution.py:603

commit v9 on v8

--- a/solution.py
+++ b/solution.py
@@ -13,6 +13,7 @@
 CLASSES = 8
 ORDER = 8
 STRIDE = 65
+SPACED = 72
 BF = jnp.bfloat16
 F32 = jnp.float32
 
@@ -191,7 +192,7 @@
         [jnp.concatenate([high, high], axis=1), jnp.concatenate([low, low], axis=1)], axis=0
     )
     for i in range(0, 64, 2):
-        parts = [split(dup_ref[rows_of(i + t), :]) for t in range(2)]
+        parts = [split(dup_ref[SPACED * (i + t) : SPACED * (i + t) + 64, :]) for t in range(2)]
         right = jnp.concatenate([
             jnp.concatenate([spread(parts[0][h]), spread(parts[1][h])], axis=1) for h in range(2)
         ], axis=0)
@@ -247,21 +248,21 @@
             value = powers[pair][k]
             swapped = pltpu.roll(value, 64, 1)
             at = CLASSES * k + 2 * pair
-            dup_ref[pl.ds(at, 64, stride=STRIDE), :] = jnp.where(mask, value, swapped)
-            dup_ref[pl.ds(at + 1, 64, stride=STRIDE), :] = jnp.where(mask, swapped, value)
+            dup_ref[pl.ds(at, 64, stride=SPACED), :] = jnp.where(mask, value, swapped)
+            dup_ref[pl.ds(at + 1, 64, stride=SPACED), :] = jnp.where(mask, swapped, value)
             if k < 4:
                 power_ref[pair, k] = value
 
     even, odd = coefficients(len_ref, cls_ref, False)
 
     def store(i, value):
-        first_ref[rows_of(i), :] = value
+        first_ref[SPACED * i : SPACED * i + 64, :] = value
 
     expand(jnp.where(low_half(), even, odd), dup_ref, store)
 
     def squarings(leaves, step, carry):
         width = 16
-        held = [first_ref[pl.ds(step * width + j, 64, stride=STRIDE), :] for j in range(width)]
+        held = [first_ref[pl.ds(step * width + j, 64, stride=SPACED), :] for j in range(width)]
         zero = jnp.zeros((128, 128), BF)
         for level in range(4):
             for j in range(0, width, 2):
@@ -341,7 +342,7 @@
     even, odd = coefficients(len_ref, cls_ref, True)
 
     def store(i, value):
-        slope_ref[rows_of(i), :] = value
+        slope_ref[64 * i : 64 * i + 64, :] = value
 
     expand(jnp.where(low_half(), even, odd), dup_ref, store)
     even, odd = coefficients(len_ref, cls_ref, False)
@@ -469,7 +470,7 @@
         values = [back_ref[rows_of(i + t), :] for t in range(2)]
         both = mxu(left, four_right(jnp.concatenate(values, axis=1)))
         for t in range(2):
-            total = total + values[t] * slope_ref[rows_of(i + t), :]
+            total = total + values[t] * slope_ref[64 * (i + t) : 64 * (i + t) + 64, :]
             here = both[:, 128 * t : 128 * t + 128]
             bins_ref[rows_of(i + t), :] = jnp.where(mask, here[0:64], here[64:128])
     slopes = total * 0.0625
@@ -555,10 +556,11 @@
     out_ref[...] = packed + jnp.where(line == 12 + subtree, length_row, 0.0)
 
 
-def last_kernel(total_sites, own_ref, got_ref, exch_ref, omega_ref, length_ref, log_ref):
+def last_kernel(total_sites, count, *refs):
     members = lax.axis_size("branch")
     subtree = lax.axis_index("branch")
-    total = jnp.where(subtree % 2 == 1, own_ref[...], got_ref[...])
+    exch_ref, omega_ref, length_ref, log_ref = refs[count:]
+    total = tree_sum([ref[...] for ref in refs[:count]])
     masks, picks = neighbours()
     table = jnp.zeros((64, 128), F32)
     for at_position, pick in zip(masks, picks):
@@ -587,20 +589,23 @@
     return parts[0]
 
 
-def sum_stages(x, axes, size):
-    stages, start = [(1, 2)], 2
-    while start < size:
-        radix = min(4, size // start)
-        stages.append((start, radix))
+def sum_stages(x, members, sites):
+    stages, start = [], 1
+    while start < sites:
+        radix = 2 if sites // start in (2, 8) else 4
+        stages.append((members * start, radix, 1))
         start *= radix
-    for start, radix in stages:
-        x = tree_sum([x] + [
-            lax.ppermute(x, axes, [
-                (i, i ^ (step * start)) for i in range(size) if start == 1 or i % 2
+    stages.append((1, members, 0))
+    parts = [x]
+    for start, radix, flip in stages[::-1]:
+        x = tree_sum(parts)
+        parts = [x] + [
+            lax.ppermute(x, ("site", "branch"), [
+                (i, i ^ (step * start + flip)) for i in range(sites * members)
             ])
             for step in range(1, radix)
-        ])
-    return x, lax.ppermute(x, axes, [(i, i - 1) for i in range(1, size, 2)])
+        ]
+    return parts
 
 
 def body(
@@ -636,7 +641,7 @@
             held((4, 2, PAIRS, 64, 128), BF),
             held((PAIRS // 2, 64, 128), F32),
             held((CLASSES // 2, 4, 64, 128), F32),
-            held((STRIDE * 64, 128), F32),
+            held((SPACED * 64, 128), F32),
             held((7, 64, 128), F32),
             held((PAIRS, 128, sites), F32),
             held((64, 64, sites), BF),
@@ -648,7 +653,7 @@
         in_specs=[vmem, vmem, smem, vmem, vmem, smem] + [vmem] * 5,
         out_specs=[vmem] * 12,
         scratch_shapes=[
-            pltpu.VMEM((STRIDE * 64, 128), F32),
+            pltpu.VMEM((SPACED * 64, 128), F32),
             pltpu.VMEM((PAIRS, 64, 256), BF),
             pltpu.VMEM((PAIRS, 64, 128), BF),
         ],
@@ -665,7 +670,7 @@
     slope, matrix, turned = inside(pl.pallas_call(
         side_kernel,
         out_shape=[
-            held((STRIDE * 64, 128), F32),
+            held((PAIRS * 64, 128), F32),
             held((64, 64, 256), BF),
             held((128, 128), F32),
         ],
@@ -693,9 +698,9 @@
         chain, turned, slope, powers, fixed,
         outside(weights.reshape(1, sites)), omega, single2, nonsyn2,
     )
-    parts = sum_stages(part, ("site", "branch"), members * lax.axis_size("site"))
+    parts = sum_stages(part, members, lax.axis_size("site"))
     exch, ratio, length, loglik = pl.pallas_call(
-        functools.partial(last_kernel, total_sites),
+        functools.partial(last_kernel, total_sites, len(parts)),
         out_shape=[shape((64, 64), F32), shape((1, CLASSES), F32), shape((1, EDGES), F32), shape((1, 1), F32)],
         in_specs=[vmem] * len(parts),
         out_specs=[vmem] * 4,

time: 66.6 us -> 54.7 us (0.82)
  waiting for transfers between devices: 24.7 us -> 11.3 us
  starting transfers between devices: 8.61 us -> 10.2 us
    ppermute x8 -> x7, waiting for transfers between devices: 22.9 us -> 9.53 us  [sum_stages(): lax.ppermute(x, ('site', 'branch'), [(i, i ^ step * start + flip) for i i...]
    ppermute x8 -> x7, starting transfers between devices: 5.46 us -> 7.06 us  [sum_stages(): lax.ppermute(x, ('site', 'branch'), [(i, i ^ step * start + flip) for i i...]
  transfers between devices with their start and end apart: 11 -> 10, of which waited for: 4 -> 7; matrix products, arithmetic and copies ran while one was open for 0% -> 0% of each run, Pallas kernels for 3% -> 4%
where the time goes in v9:
time: 54.7 us; the launch traced here: 54.5 us
  Pallas kernels  32.3 us (59%)
  waiting for transfers between devices  11.3 us (21%)
  starting transfers between devices  10.2 us (19%)
  between operations  0.67 us (1%)
    pallas_call x1, Pallas kernels, body(): pl.pallas_call(functools.partial(down_kernel, total_sites, members), out_...  16.4 us
    pallas_call x1, Pallas kernels, body(): pl.pallas_call(up_kernel, out_shape=[shape((64, sites), F32), held((4, 2,...  12.8 us
    ppermute x7, waiting for transfers between devices, sum_stages(): lax.ppermute(x, ('site', 'branch'), [(i, i ^ step * start + flip) for i i...  9.53 us
    ppermute x7, starting transfers between devices, sum_stages(): lax.ppermute(x, ('site', 'branch'), [(i, i ^ step * start + flip) for i i...  7.06 us
    ppermute x3, starting transfers between devices, partners(): lax.ppermute(x, axis, [(i, i ^ step * start) for i in range(size)])  3.15 us
    pallas_call x1, Pallas kernels, body(): pl.pallas_call(side_kernel, out_shape=[held((PAIRS * 64, 128), F32), held...  2.2 us
    ppermute x3, waiting for transfers between devices, partners(): lax.ppermute(x, axis, [(i, i ^ step * start) for i in range(size)])  1.76 us
  transfers between devices with their start and end apart: 10, of which 7 were waited for; matrix products, arithmetic and copies ran while one was open for 0% of the time, Pallas kernels for 4%

profile of v9, /device:TPU:0, one launch (start us, length us, event | category | flops | bytes accessed | tf_op | source)
XLA Modules:
  0.0 54.5 jit_solution(16152854427890943883)
XLA Ops:
  0.6 12.8 %up.1 = (f32[64,256]{1,0:T(8,128)S(1)}, bf16[4,2,64,64,128]{4,3,2,1,0:T(8,128)(2,1)S(1)}, f32[32,64,128]{2,1,0:T(8,128)S(1)}, f32[4,4,64,128]{3,2,1,0:T(8,128)S(...) custom-call(s32[256,256]{1,0:T(8,128)} %states_ref.1, ...), custom_call_target="tpu_custom_call" | custom-call | tf_op jit(solution)/shard_map/up/pallas_call | solution.py:637
  13.5 0.5 collective-permute-start
  14.0 2.6 %collective-permute-start.1 = (f32[64,256]{1,0:T(8,128)S(1)}, f32[64,256]{1,0:T(8,128)S(1)}, u32[]{:S(2)}, u32[]{:S(2)}) collective-permute-start(f32[64,256]{1,0:T(8,128)S(1)} %get-tuple-element.23.refs_0_), channel_id=1, source_target_pairs={{0,2},{1,3},{2,0},{3,1},{4,6},{5,7},{6,4},{7,5},{8,10},{9,11},{10,... | collective-permute-start | bytes 196616 | tf_op jit(solution)/shard_map/ppermute | solution.py:580
  16.6 0.1 collective-permute-start.2
  16.6 2.2 %side.1 = (f32[4096,128]{1,0:T(8,128)S(1)}, bf16[64,64,256]{2,1,0:T(8,128)(2,1)S(1)}, f32[128,128]{1,0:T(8,128)S(1)}) custom-call(f32[4608,128]{1,0:T(8,128)S(1)} %get-tuple-element.24.dup_ref, f32[32,64,128]{2,1,0:T(8,128)S(1)} %get-tuple-element.25.last_ref, f32[1,127]{1,0:T(1,128)} %bitcast.8, s32[1,127]{1,0:T(1,128)} %bitcast.10, ...), custom_call_target="tpu_custom_call" | custom-call | tf_op jit(solution)/shard_map/side/pallas_call | solution.py:670
  18.8 0.0 collective-permute-done.refs_1_
  18.8 0.4 collective-permute-done.1.refs_2_
  19.3 1.4 %collective-permute-done.2.refs_3_ = f32[64,256]{1,0:T(8,128)S(1)} collective-permute-done((f32[64,256]{1,0:T(8,128)S(1)}, f32[64,256]{1,0:T(8,128)S(1)}, u32[]{:S(2)}, u32[]{:S(2)}) %collective-permute-start.2) | collective-permute-done | bytes 65568 | tf_op jit(solution)/shard_map/ppermute | solution.py:580
  20.6 16.4 %down.1 = f32[16,128]{1,0:T(8,128)S(1)} custom-call(f32[64,256]{1,0:T(8,128)S(1)} %get-tuple-element.23.refs_0_, f32[64,256]{1,0:T(8,128)S(1)} %collective-permute-done.refs_1_, f32[64,256]{1,0:T(8,128)S(1)} %collective-permute-done.1.refs_2_, f32[64,256]{1,0:T(8,128)S(1)} %collective-permute-done.2.refs_3_, ...), custom_call_target="tpu_custom_call" | custom-call | tf_op jit(solution)/shard_map/down/pallas_call | solution.py:682
  37.0 0.2 collective-permute-start.3
  37.2 1.4 %collective-permute-start.4 = (f32[16,128]{1,0:T(8,128)S(1)}, f32[16,128]{1,0:T(8,128)S(1)}, u32[]{:S(2)}, u32[]{:S(2)}) collective-permute-start(f32[16,128]{1,0:T(8,128)S(1)} %down.1), channel_id=1, source_target_pairs={{0,2},{1,3},{2,0},{3,1},{4,6},{5,7},{6,4},{7,5},{8,10},{9,11},{10,... | collective-permute-start | bytes 24584 | tf_op jit(solution)/shard_map/ppermute | solution.py:603
  38.7 0.3 collective-permute-start.5
  38.9 0.0 collective-permute-done.3
  38.9 2.0 %collective-permute-done.4 = f32[16,128]{1,0:T(8,128)S(1)} collective-permute-done((f32[16,128]{1,0:T(8,128)S(1)}, f32[16,128]{1,0:T(8,128)S(1)}, u32[]{:S(2)}, u32[]{:S(2)}) %collective-permute-start.4) | collective-permute-done | bytes 8224 | tf_op jit(solution)/shard_map/ppermute | solution.py:603
  40.9 0.9 %collective-permute-done.5 = f32[16,128]{1,0:T(8,128)S(1)} collective-permute-done((f32[16,128]{1,0:T(8,128)S(1)}, f32[16,128]{1,0:T(8,128)S(1)}, u32[]{:S(2)}, u32[]{:S(2)}) %collective-permute-start.5) | collective-permute-done | bytes 8224 | tf_op jit(solution)/shard_map/ppermute | solution.py:603
  41.8 1.3 %collective-permute-start.6 = (f32[16,128]{1,0:T(8,128)S(1)}, f32[16,128]{1,0:T(8,128)S(1)}, u32[]{:S(2)}, u32[]{:S(2)}) collective-permute-start(f32[16,128]{1,0:T(8,128)S(1)} %add_add_fusion.1), channel_id=1, source_target_pairs={{0,9},{1,8},{2,11},{3,10},{4,13},{5,12},{6,15},{7,14},{8,1},{9,0},... | collective-permute-start | bytes 24584 | tf_op jit(solution)/shard_map/ppermute | solution.py:603
  43.1 2.6 %collective-permute-start.7 = (f32[16,128]{1,0:T(8,128)S(1)}, f32[16,128]{1,0:T(8,128)S(1)}, u32[]{:S(2)}, u32[]{:S(2)}) collective-permute-start(f32[16,128]{1,0:T(8,128)S(1)} %add_add_fusion.1), channel_id=1, source_target_pairs={{0,17},{1,16},{2,19},{3,18},{4,21},{5,20},{6,23},{7,22},{8,25},{9,... | collective-permute-start | bytes 24584 | tf_op jit(solution)/shard_map/ppermute | solution.py:603
  45.7 0.0 collective-permute-start.8
  45.7 0.0 collective-permute-done.6
  45.7 1.4 %collective-permute-done.7 = f32[16,128]{1,0:T(8,128)S(1)} collective-permute-done((f32[16,128]{1,0:T(8,128)S(1)}, f32[16,128]{1,0:T(8,128)S(1)}, u32[]{:S(2)}, u32[]{:S(2)}) %collective-permute-start.7) | collective-permute-done | bytes 8224 | tf_op jit(solution)/shard_map/ppermute | solution.py:603
  47.1 3.5 %collective-permute-done.8 = f32[16,128]{1,0:T(8,128)S(1)} collective-permute-done((f32[16,128]{1,0:T(8,128)S(1)}, f32[16,128]{1,0:T(8,128)S(1)}, u32[]{:S(2)}, u32[]{:S(2)}) %collective-permute-start.8) | collective-permute-done | bytes 8224 | tf_op jit(solution)/shard_map/ppermute | solution.py:603
  50.6 1.2 %collective-permute-start.9 = (f32[16,128]{1,0:T(8,128)S(1)}, f32[16,128]{1,0:T(8,128)S(1)}, u32[]{:S(2)}, u32[]{:S(2)}) collective-permute-start(f32[16,128]{1,0:T(8,128)S(1)} %add_add_fusion.refs_0_), channel_id=1, source_target_pairs={{0,5},{1,4},{2,7},{3,6},{4,1},{5,0},{6,3},{7,2},{8,13},{9,12},{10,... | collective-permute-start | bytes 24584 | tf_op jit(solution)/shard_map/ppermute | solution.py:603
  51.8 1.8 %collective-permute-done.9.refs_1_ = f32[16,128]{1,0:T(8,128)S(1)} collective-permute-done((f32[16,128]{1,0:T(8,128)S(1)}, f32[16,128]{1,0:T(8,128)S(1)}, u32[]{:S(2)}, u32[]{:S(2)}) %collective-permute-start.9) | collective-permute-done | bytes 8224 | tf_op jit(solution)/shard_map/ppermute | solution.py:603
  53.6 0.8 %last.1 = (f32[64,64]{1,0:T(8,128)}, f32[1,8]{1,0:T(1,128)}, f32[1,127]{1,0:T(1,128)}, f32[1,1]{1,0:T(1,128)}) custom-call(f32[16,128]{1,0:T(8,128)S(1)} %add_add_fusion.refs_0_, f32[16,128]{1,0:T(8,128)S(1)} %collective-permute-done.9.refs_1_), custom_call_target="tpu_custom_call" | custom-call | tf_op jit(solution)/shard_map/last/pallas_call | solution.py:702
  (2 shorter events, 0.0 us)
Async XLA Ops:
  13.5 5.4 %collective-permute-start = (f32[64,256]{1,0:T(8,128)S(1)}, f32[64,256]{1,0:T(8,128)S(1)}, u32[]{:S(2)}, u32[]{:S(2)}) collective-permute-start(f32[64,256]{1,0:T(8,128)S(1)} %get-tuple-element.23.refs_0_), channel_id=1, source_target_pairs={{0,1},{1,0},{2,3},{3,2},{4,5},{5,4},{6,7},{7,6},{8,9},{9,8},{10,11... | collective-permute-start | bytes 196616 | tf_op jit(solution)/shard_map/ppermute | solution.py:580
  14.0 5.3 %collective-permute-start.1 = (f32[64,256]{1,0:T(8,128)S(1)}, f32[64,256]{1,0:T(8,128)S(1)}, u32[]{:S(2)}, u32[]{:S(2)}) collective-permute-start(f32[64,256]{1,0:T(8,128)S(1)} %get-tuple-element.23.refs_0_), channel_id=1, source_target_pairs={{0,2},{1,3},{2,0},{3,1},{4,6},{5,7},{6,4},{7,5},{8,10},{9,11},{10,... | collective-permute-start | bytes 196616 | tf_op jit(solution)/shard_map/ppermute | solution.py:580
  16.6 4.0 %collective-permute-start.2 = (f32[64,256]{1,0:T(8,128)S(1)}, f32[64,256]{1,0:T(8,128)S(1)}, u32[]{:S(2)}, u32[]{:S(2)}) collective-permute-start(f32[64,256]{1,0:T(8,128)S(1)} %get-tuple-element.23.refs_0_), channel_id=1, source_target_pairs={{0,3},{1,2},{2,1},{3,0},{4,7},{5,6},{6,5},{7,4},{8,11},{9,10},{10,... | collective-permute-start | bytes 196616 | tf_op jit(solution)/shard_map/ppermute | solution.py:580
  37.0 1.9 %collective-permute-start.3 = (f32[16,128]{1,0:T(8,128)S(1)}, f32[16,128]{1,0:T(8,128)S(1)}, u32[]{:S(2)}, u32[]{:S(2)}) collective-permute-start(f32[16,128]{1,0:T(8,128)S(1)} %down.1), channel_id=1, source_target_pairs={{0,1},{1,0},{2,3},{3,2},{4,5},{5,4},{6,7},{7,6},{8,9},{9,8},{10,11... | collective-permute-start | bytes 24584 | tf_op jit(solution)/shard_map/ppermute | solution.py:603
  37.2 3.7 %collective-permute-start.4 = (f32[16,128]{1,0:T(8,128)S(1)}, f32[16,128]{1,0:T(8,128)S(1)}, u32[]{:S(2)}, u32[]{:S(2)}) collective-permute-start(f32[16,128]{1,0:T(8,128)S(1)} %down.1), channel_id=1, source_target_pairs={{0,2},{1,3},{2,0},{3,1},{4,6},{5,7},{6,4},{7,5},{8,10},{9,11},{10,... | collective-permute-start | bytes 24584 | tf_op jit(solution)/shard_map/ppermute | solution.py:603
  38.7 3.1 %collective-permute-start.5 = (f32[16,128]{1,0:T(8,128)S(1)}, f32[16,128]{1,0:T(8,128)S(1)}, u32[]{:S(2)}, u32[]{:S(2)}) collective-permute-start(f32[16,128]{1,0:T(8,128)S(1)} %down.1), channel_id=1, source_target_pairs={{0,3},{1,2},{2,1},{3,0},{4,7},{5,6},{6,5},{7,4},{8,11},{9,10},{10,... | collective-permute-start | bytes 24584 | tf_op jit(solution)/shard_map/ppermute | solution.py:603
  41.8 3.9 %collective-permute-start.6 = (f32[16,128]{1,0:T(8,128)S(1)}, f32[16,128]{1,0:T(8,128)S(1)}, u32[]{:S(2)}, u32[]{:S(2)}) collective-permute-start(f32[16,128]{1,0:T(8,128)S(1)} %add_add_fusion.1), channel_id=1, source_target_pairs={{0,9},{1,8},{2,11},{3,10},{4,13},{5,12},{6,15},{7,14},{8,1},{9,0},... | collective-permute-start | bytes 24584 | tf_op jit(solution)/shard_map/ppermute | solution.py:603
  43.1 4.0 %collective-permute-start.7 = (f32[16,128]{1,0:T(8,128)S(1)}, f32[16,128]{1,0:T(8,128)S(1)}, u32[]{:S(2)}, u32[]{:S(2)}) collective-permute-start(f32[16,128]{1,0:T(8,128)S(1)} %add_add_fusion.1), channel_id=1, source_target_pairs={{0,17},{1,16},{2,19},{3,18},{4,21},{5,20},{6,23},{7,22},{8,25},{9,... | collective-permute-start | bytes 24584 | tf_op jit(solution)/shard_map/ppermute | solution.py:603
  45.7 4.9 %collective-permute-start.8 = (f32[16,128]{1,0:T(8,128)S(1)}, f32[16,128]{1,0:T(8,128)S(1)}, u32[]{:S(2)}, u32[]{:S(2)}) collective-permute-start(f32[16,128]{1,0:T(8,128)S(1)} %add_add_fusion.1), channel_id=1, source_target_pairs={{0,25},{1,24},{2,27},{3,26},{4,29},{5,28},{6,31},{7,30},{8,17},{9,... | collective-permute-start | bytes 24584 | tf_op jit(solution)/shard_map/ppermute | solution.py:603
  50.6 3.1 %collective-permute-start.9 = (f32[16,128]{1,0:T(8,128)S(1)}, f32[16,128]{1,0:T(8,128)S(1)}, u32[]{:S(2)}, u32[]{:S(2)}) collective-permute-start(f32[16,128]{1,0:T(8,128)S(1)} %add_add_fusion.refs_0_), channel_id=1, source_target_pairs={{0,5},{1,4},{2,7},{3,6},{4,1},{5,0},{6,3},{7,2},{8,13},{9,12},{10,... | collective-permute-start | bytes 24584 | tf_op jit(solution)/shard_map/ppermute | solution.py:603

commit v10 on v9

--- a/solution.py
+++ b/solution.py
@@ -13,7 +13,6 @@
 CLASSES = 8
 ORDER = 8
 STRIDE = 65
-SPACED = 72
 BF = jnp.bfloat16
 F32 = jnp.float32
 
@@ -80,6 +79,14 @@
 
 def messages(matrix, high, low):
     return mxu(matrix, jnp.concatenate([high, low, high, low], axis=0))
+
+
+def leaf_messages(thin_ref, leaf_ref, p):
+    found = []
+    for e in range(2):
+        vector = leaf_ref[p, 64 * e : 64 * e + 64, :]
+        found.append(mxu(thin_ref[2 * p + e], jnp.concatenate([vector, vector], axis=0)))
+    return found
 
 
 def doubled(x):
@@ -192,7 +199,7 @@
         [jnp.concatenate([high, high], axis=1), jnp.concatenate([low, low], axis=1)], axis=0
     )
     for i in range(0, 64, 2):
-        parts = [split(dup_ref[SPACED * (i + t) : SPACED * (i + t) + 64, :]) for t in range(2)]
+        parts = [split(dup_ref[rows_of(i + t), :]) for t in range(2)]
         right = jnp.concatenate([
             jnp.concatenate([spread(parts[0][h]), spread(parts[1][h])], axis=1) for h in range(2)
         ], axis=0)
@@ -210,8 +217,8 @@
     states_ref, gap_ref, order_ref,
     ex_ref, freq_ref, omega_ref, len_ref, cls_ref, sense_ref, single_ref, nonsyn_ref,
     top_ref, chain_ref, last_ref, power_ref, dup_ref, fixed_ref,
-    message_ref, high_ref, low_ref, leaf_ref, scale_ref, inverse_ref,
-    first_ref, up_ref, thin_ref,
+    message_ref, high_ref, low_ref, leaf_ref, scale_ref, inverse_ref, thin_ref,
+    first_ref, up_ref,
 ):
     subtree = lax.axis_index("branch")
     mask = low_half()
@@ -248,43 +255,31 @@
             value = powers[pair][k]
             swapped = pltpu.roll(value, 64, 1)
             at = CLASSES * k + 2 * pair
-            dup_ref[pl.ds(at, 64, stride=SPACED), :] = jnp.where(mask, value, swapped)
-            dup_ref[pl.ds(at + 1, 64, stride=SPACED), :] = jnp.where(mask, swapped, value)
+            dup_ref[pl.ds(at, 64, stride=STRIDE), :] = jnp.where(mask, value, swapped)
+            dup_ref[pl.ds(at + 1, 64, stride=STRIDE), :] = jnp.where(mask, swapped, value)
             if k < 4:
                 power_ref[pair, k] = value
 
     even, odd = coefficients(len_ref, cls_ref, False)
 
     def store(i, value):
-        first_ref[SPACED * i : SPACED * i + 64, :] = value
+        first_ref[rows_of(i), :] = value
 
     expand(jnp.where(low_half(), even, odd), dup_ref, store)
 
     def squarings(leaves, step, carry):
         width = 16
-        held = [first_ref[pl.ds(step * width + j, 64, stride=SPACED), :] for j in range(width)]
-        zero = jnp.zeros((128, 128), BF)
+        held = [first_ref[pl.ds(step * width + j, 64, stride=STRIDE), :] for j in range(width)]
         for level in range(4):
-            for j in range(0, width, 2):
-                highs, lows, products = [], [], []
-                for t in range(2):
-                    high, low = split(held[j + t])
-                    chain_ref[level, 0, step * width + j + t] = high
-                    chain_ref[level, 1, step * width + j + t] = low
-                    wide = spread(high)
-                    highs.append(high)
-                    lows.append(spread(low))
-                    products.append(mxu(
-                        jnp.concatenate([high, low], axis=1), jnp.concatenate([wide, wide], axis=0)
-                    ))
-                rest = mxu(jnp.concatenate(highs, axis=1), jnp.concatenate([
-                    jnp.concatenate([lows[0], zero], axis=1),
-                    jnp.concatenate([zero, lows[1]], axis=1),
-                ], axis=0))
-                for t in range(2):
-                    held[j + t] = (
-                        2.0 * held[j + t] + products[t] + rest[:, 128 * t : 128 * t + 128]
-                    )
+            for j in range(width):
+                high, low = split(held[j])
+                chain_ref[level, 0, step * width + j] = high
+                chain_ref[level, 1, step * width + j] = low
+                wide_high, wide_low = spread(high), spread(low)
+                held[j] = 2.0 * held[j] + mxu(
+                    jnp.concatenate([high, high, low], axis=1),
+                    jnp.concatenate([wide_high, wide_low, wide_high], axis=0),
+                )
         for j in range(width):
             p = step * width + j
             matrix = inverse_root_col * (held[j] + twice) * root_row
@@ -300,7 +295,8 @@
     lax.fori_loop(2, 4, functools.partial(squarings, False), 0)
 
     def finish(p, message):
-        message_ref[p] = jnp.concatenate(message, axis=0)
+        if p >= 32:
+            message_ref[p - 32] = jnp.concatenate(message, axis=0)
         raw = message[0] * message[1]
         scaling = jnp.sum(raw, axis=0, keepdims=True)
         inverse = 1.0 / scaling
@@ -311,10 +307,7 @@
         low_ref[p] = low
 
     for p in range(32):
-        both = [leaf_ref[p, 64 * e : 64 * e + 64, :] for e in range(2)]
-        finish(p, [
-            mxu(thin_ref[2 * p + e], jnp.concatenate([both[e], both[e]], axis=0)) for e in range(2)
-        ])
+        finish(p, leaf_messages(thin_ref, leaf_ref, p))
 
     def inner(p):
         child = 2 * p - 64
@@ -331,12 +324,12 @@
     scale_ref[63:64, :] = jnp.ones((1, sites), F32)
     inverse_ref[63:64, :] = jnp.ones((1, sites), F32)
     top = inner(63)
-    message_ref[63] = jnp.concatenate(top, axis=0)
     top_ref[...] = top[0]
 
 
 def side_kernel(
-    dup_ref, last_ref, len_ref, cls_ref, fixed_ref, slope_ref, matrix_ref, turned_ref,
+    dup_ref, last_ref, len_ref, cls_ref, fixed_ref, thin_ref, leaf_ref,
+    slope_ref, matrix_ref, turned_ref, given_ref,
 ):
     twice = identity_twice()
     even, odd = coefficients(len_ref, cls_ref, True)
@@ -356,12 +349,14 @@
         return carry
 
     lax.fori_loop(0, 4, matrices, 0)
+    for p in range(32):
+        given_ref[p] = jnp.concatenate(leaf_messages(thin_ref, leaf_ref, p), axis=0)
 
 
 def down_kernel(total_sites, members, *refs):
     tops = refs[:members]
     (
-        matrix_ref, message_ref, high_ref, low_ref, leaf_ref, scale_ref, inverse_ref,
+        matrix_ref, given_ref, message_ref, high_ref, low_ref, leaf_ref, scale_ref, inverse_ref,
         chain_ref, turned_ref, slope_ref, power_ref, fixed_ref,
         weights_ref, omega_ref, single_ref, nonsyn_ref,
         out_ref,
@@ -412,7 +407,7 @@
     def children(down, e, p):
         vector = down[e]
         inverse = inverse_ref[pl.ds(p, 1), :]
-        message = message_ref[p]
+        message = message_ref[p - 32] if p >= 32 else given_ref[p]
         pair = jnp.concatenate(
             [vector * message[64:128] * inverse, vector * message[0:64] * inverse], axis=0
         )
@@ -641,21 +636,21 @@
             held((4, 2, PAIRS, 64, 128), BF),
             held((PAIRS // 2, 64, 128), F32),
             held((CLASSES // 2, 4, 64, 128), F32),
-            held((SPACED * 64, 128), F32),
+            held((STRIDE * 64, 128), F32),
             held((7, 64, 128), F32),
-            held((PAIRS, 128, sites), F32),
+            held((PAIRS // 2, 128, sites), F32),
             held((64, 64, sites), BF),
             held((64, 64, sites), BF),
             held((32, 128, sites), BF),
             held((64, sites), F32),
             held((64, sites), F32),
+            held((PAIRS, 64, 128), BF),
         ],
         in_specs=[vmem, vmem, smem, vmem, vmem, smem] + [vmem] * 5,
-        out_specs=[vmem] * 12,
+        out_specs=[vmem] * 13,
         scratch_shapes=[
-            pltpu.VMEM((SPACED * 64, 128), F32),
+            pltpu.VMEM((STRIDE * 64, 128), F32),
             pltpu.VMEM((PAIRS, 64, 256), BF),
-            pltpu.VMEM((PAIRS, 64, 128), BF),
         ],
         compiler_params=limit,
         name="up",
@@ -664,25 +659,26 @@
         table, freq, omega, span, owner, sense2, single2, nonsyn2,
     )
     (
-        chain, last, powers, dup, fixed, message, high, low, leaf, scale, inverse,
+        chain, last, powers, dup, fixed, message, high, low, leaf, scale, inverse, thin,
     ) = inside(kept)
     tops = partners(top, "branch", 1, members)
-    slope, matrix, turned = inside(pl.pallas_call(
+    slope, matrix, turned, given = inside(pl.pallas_call(
         side_kernel,
         out_shape=[
             held((PAIRS * 64, 128), F32),
             held((64, 64, 256), BF),
             held((128, 128), F32),
+            held((PAIRS // 2, 128, sites), F32),
         ],
-        in_specs=[vmem] * 5,
-        out_specs=[vmem] * 3,
+        in_specs=[vmem] * 7,
+        out_specs=[vmem] * 4,
         compiler_params=limit,
         name="side",
-    )(dup, last, span, owner, fixed))
+    )(dup, last, span, owner, fixed, thin, leaf))
     part = pl.pallas_call(
         functools.partial(down_kernel, total_sites, members),
         out_shape=shape((16, 128), F32),
-        in_specs=[vmem] * (13 + members) + [smem, vmem, vmem],
+        in_specs=[vmem] * (14 + members) + [smem, vmem, vmem],
         out_specs=vmem,
         scratch_shapes=[
             pltpu.VMEM((32, 128, sites), BF),
@@ -694,7 +690,7 @@
         compiler_params=limit,
         name="down",
     )(
-        *tops, matrix, message, high, low, leaf, scale, inverse,
+        *tops, matrix, given, message, high, low, leaf, scale, inverse,
         chain, turned, slope, powers, fixed,
         outside(weights.reshape(1, sites)), omega, single2, nonsyn2,
     )

time: 54.7 us -> 53.8 us (0.984)
  waiting for transfers between devices: 11.3 us -> 10.5 us
    pallas_call x1, Pallas kernels: 12.8 us -> 11.9 us  [body(): pl.pallas_call(up_kernel, out_shape=[shape((64, sites), F32), held((4, 2,...]
    ppermute x3, waiting for transfers between devices: 1.76 us -> 0.95 us  [partners(): lax.ppermute(x, axis, [(i, i ^ step * start) for i in range(size)])]
    pallas_call x1, Pallas kernels: 2.2 us -> 3.01 us  [body(): pl.pallas_call(side_kernel, out_shape=[held((PAIRS * 64, 128), F32), held...]
  transfers between devices with their start and end apart: 10 -> 10, of which waited for: 7 -> 6; matrix products, arithmetic and copies ran while one was open for 0% -> 0% of each run, Pallas kernels for 4% -> 6%
where the time goes in v10:
time: 53.8 us; the launch traced here: 53.5 us
  Pallas kernels  32.2 us (60%)
  waiting for transfers between devices  10.5 us (20%)
  starting transfers between devices  10.2 us (19%)
  between operations  0.67 us (1%)
    pallas_call x1, Pallas kernels, body(): pl.pallas_call(functools.partial(down_kernel, total_sites, members), out_...  16.4 us
    pallas_call x1, Pallas kernels, body(): pl.pallas_call(up_kernel, out_shape=[shape((64, sites), F32), held((4, 2,...  11.9 us
    ppermute x7, waiting for transfers between devices, sum_stages(): lax.ppermute(x, ('site', 'branch'), [(i, i ^ step * start + flip) for i i...  9.55 us
    ppermute x7, starting transfers between devices, sum_stages(): lax.ppermute(x, ('site', 'branch'), [(i, i ^ step * start + flip) for i i...  7.05 us
    ppermute x3, starting transfers between devices, partners(): lax.ppermute(x, axis, [(i, i ^ step * start) for i in range(size)])  3.15 us
    pallas_call x1, Pallas kernels, body(): pl.pallas_call(side_kernel, out_shape=[held((PAIRS * 64, 128), F32), held...  3.01 us
  transfers between devices with their start and end apart: 10, of which 6 were waited for; matrix products, arithmetic and copies ran while one was open for 0% of the time, Pallas kernels for 6%

profile of v10, /device:TPU:0, one launch (start us, length us, event | category | flops | bytes accessed | tf_op | source)
XLA Modules:
  0.0 53.5 jit_solution(8383343288987489496)
XLA Ops:
  0.6 11.9 %up.1 = (f32[64,256]{1,0:T(8,128)S(1)}, bf16[4,2,64,64,128]{4,3,2,1,0:T(8,128)(2,1)S(1)}, f32[32,64,128]{2,1,0:T(8,128)S(1)}, f32[4,4,64,128]{3,2,1,0:T(8,128)S(...) custom-call(s32[256,256]{1,0:T(8,128)} %states_ref.1, ...), custom_call_target="tpu_custom_call" | custom-call | tf_op jit(solution)/shard_map/up/pallas_call | solution.py:632
  12.5 0.5 collective-permute-start
  13.0 2.6 %collective-permute-start.1 = (f32[64,256]{1,0:T(8,128)S(1)}, f32[64,256]{1,0:T(8,128)S(1)}, u32[]{:S(2)}, u32[]{:S(2)}) collective-permute-start(f32[64,256]{1,0:T(8,128)S(1)} %get-tuple-element.25.refs_0_), channel_id=1, source_target_pairs={{0,2},{1,3},{2,0},{3,1},{4,6},{5,7},{6,4},{7,5},{8,10},{9,11},{10,... | collective-permute-start | bytes 196616 | tf_op jit(solution)/shard_map/ppermute | solution.py:575
  15.6 0.1 collective-permute-start.2
  15.7 3.0 %side.1 = (f32[4096,128]{1,0:T(8,128)S(1)}, bf16[64,64,256]{2,1,0:T(8,128)(2,1)S(1)}, f32[128,128]{1,0:T(8,128)S(1)}, f32[32,128,256]{2,1,0:T(8,128)S(1)}) custom-call(f32[4160,128]{1,0:T(8,128)S(1)} %get-tuple-element.26.dup_ref, f32[32,64,128]{2,1,0:T(8,128)S(1)} %get-tuple-element.27.last_ref, f32[1,127]{1,0:T(1,128)} %bitcast.8, s32[1,127]{1,0:T(1,128)} %bitcast.10, ...), custom_call_target="tpu_custom_call" | custom-call | tf_op jit(solution)/shard_map/side/pallas_call | solution.py:665
  18.7 0.0 collective-permute-done.refs_1_
  18.7 0.0 collective-permute-done.1.refs_2_
  18.7 0.9 %collective-permute-done.2.refs_3_ = f32[64,256]{1,0:T(8,128)S(1)} collective-permute-done((f32[64,256]{1,0:T(8,128)S(1)}, f32[64,256]{1,0:T(8,128)S(1)}, u32[]{:S(2)}, u32[]{:S(2)}) %collective-permute-start.2) | collective-permute-done | bytes 65568 | tf_op jit(solution)/shard_map/ppermute | solution.py:575
  19.7 16.4 %down.1 = f32[16,128]{1,0:T(8,128)S(1)} custom-call(f32[64,256]{1,0:T(8,128)S(1)} %get-tuple-element.25.refs_0_, f32[64,256]{1,0:T(8,128)S(1)} %collective-permute-done.refs_1_, f32[64,256]{1,0:T(8,128)S(1)} %collective-permute-done.1.refs_2_, f32[64,256]{1,0:T(8,128)S(1)} %collective-permute-done.2.refs_3_, ...), custom_call_target="tpu_custom_call" | custom-call | tf_op jit(solution)/shard_map/down/pallas_call | solution.py:678
  36.1 0.2 collective-permute-start.3
  36.3 1.4 %collective-permute-start.4 = (f32[16,128]{1,0:T(8,128)S(1)}, f32[16,128]{1,0:T(8,128)S(1)}, u32[]{:S(2)}, u32[]{:S(2)}) collective-permute-start(f32[16,128]{1,0:T(8,128)S(1)} %down.1), channel_id=1, source_target_pairs={{0,2},{1,3},{2,0},{3,1},{4,6},{5,7},{6,4},{7,5},{8,10},{9,11},{10,... | collective-permute-start | bytes 24584 | tf_op jit(solution)/shard_map/ppermute | solution.py:598
  37.7 0.2 collective-permute-start.5
  38.0 0.0 collective-permute-done.3
  38.0 2.0 %collective-permute-done.4 = f32[16,128]{1,0:T(8,128)S(1)} collective-permute-done((f32[16,128]{1,0:T(8,128)S(1)}, f32[16,128]{1,0:T(8,128)S(1)}, u32[]{:S(2)}, u32[]{:S(2)}) %collective-permute-start.4) | collective-permute-done | bytes 8224 | tf_op jit(solution)/shard_map/ppermute | solution.py:598
  40.0 0.9 %collective-permute-done.5 = f32[16,128]{1,0:T(8,128)S(1)} collective-permute-done((f32[16,128]{1,0:T(8,128)S(1)}, f32[16,128]{1,0:T(8,128)S(1)}, u32[]{:S(2)}, u32[]{:S(2)}) %collective-permute-start.5) | collective-permute-done | bytes 8224 | tf_op jit(solution)/shard_map/ppermute | solution.py:598
  40.8 1.3 %collective-permute-start.6 = (f32[16,128]{1,0:T(8,128)S(1)}, f32[16,128]{1,0:T(8,128)S(1)}, u32[]{:S(2)}, u32[]{:S(2)}) collective-permute-start(f32[16,128]{1,0:T(8,128)S(1)} %add_add_fusion.1), channel_id=1, source_target_pairs={{0,9},{1,8},{2,11},{3,10},{4,13},{5,12},{6,15},{7,14},{8,1},{9,0},... | collective-permute-start | bytes 24584 | tf_op jit(solution)/shard_map/ppermute | solution.py:598
  42.1 2.6 %collective-permute-start.7 = (f32[16,128]{1,0:T(8,128)S(1)}, f32[16,128]{1,0:T(8,128)S(1)}, u32[]{:S(2)}, u32[]{:S(2)}) collective-permute-start(f32[16,128]{1,0:T(8,128)S(1)} %add_add_fusion.1), channel_id=1, source_target_pairs={{0,17},{1,16},{2,19},{3,18},{4,21},{5,20},{6,23},{7,22},{8,25},{9,... | collective-permute-start | bytes 24584 | tf_op jit(solution)/shard_map/ppermute | solution.py:598
  44.8 0.0 collective-permute-start.8
  44.8 0.0 collective-permute-done.6
  44.8 1.4 %collective-permute-done.7 = f32[16,128]{1,0:T(8,128)S(1)} collective-permute-done((f32[16,128]{1,0:T(8,128)S(1)}, f32[16,128]{1,0:T(8,128)S(1)}, u32[]{:S(2)}, u32[]{:S(2)}) %collective-permute-start.7) | collective-permute-done | bytes 8224 | tf_op jit(solution)/shard_map/ppermute | solution.py:598
  46.1 3.5 %collective-permute-done.8 = f32[16,128]{1,0:T(8,128)S(1)} collective-permute-done((f32[16,128]{1,0:T(8,128)S(1)}, f32[16,128]{1,0:T(8,128)S(1)}, u32[]{:S(2)}, u32[]{:S(2)}) %collective-permute-start.8) | collective-permute-done | bytes 8224 | tf_op jit(solution)/shard_map/ppermute | solution.py:598
  49.6 1.2 %collective-permute-start.9 = (f32[16,128]{1,0:T(8,128)S(1)}, f32[16,128]{1,0:T(8,128)S(1)}, u32[]{:S(2)}, u32[]{:S(2)}) collective-permute-start(f32[16,128]{1,0:T(8,128)S(1)} %add_add_fusion.refs_0_), channel_id=1, source_target_pairs={{0,5},{1,4},{2,7},{3,6},{4,1},{5,0},{6,3},{7,2},{8,13},{9,12},{10,... | collective-permute-start | bytes 24584 | tf_op jit(solution)/shard_map/ppermute | solution.py:598
  50.9 1.8 %collective-permute-done.9.refs_1_ = f32[16,128]{1,0:T(8,128)S(1)} collective-permute-done((f32[16,128]{1,0:T(8,128)S(1)}, f32[16,128]{1,0:T(8,128)S(1)}, u32[]{:S(2)}, u32[]{:S(2)}) %collective-permute-start.9) | collective-permute-done | bytes 8224 | tf_op jit(solution)/shard_map/ppermute | solution.py:598
  52.7 0.8 %last.1 = (f32[64,64]{1,0:T(8,128)}, f32[1,8]{1,0:T(1,128)}, f32[1,127]{1,0:T(1,128)}, f32[1,1]{1,0:T(1,128)}) custom-call(f32[16,128]{1,0:T(8,128)S(1)} %add_add_fusion.refs_0_, f32[16,128]{1,0:T(8,128)S(1)} %collective-permute-done.9.refs_1_), custom_call_target="tpu_custom_call" | custom-call | tf_op jit(solution)/shard_map/last/pallas_call | solution.py:698
  (2 shorter events, 0.0 us)
Async XLA Ops:
  12.5 6.2 %collective-permute-start = (f32[64,256]{1,0:T(8,128)S(1)}, f32[64,256]{1,0:T(8,128)S(1)}, u32[]{:S(2)}, u32[]{:S(2)}) collective-permute-start(f32[64,256]{1,0:T(8,128)S(1)} %get-tuple-element.25.refs_0_), channel_id=1, source_target_pairs={{0,1},{1,0},{2,3},{3,2},{4,5},{5,4},{6,7},{7,6},{8,9},{9,8},{10,11... | collective-permute-start | bytes 196616 | tf_op jit(solution)/shard_map/ppermute | solution.py:575
  13.0 5.7 %collective-permute-start.1 = (f32[64,256]{1,0:T(8,128)S(1)}, f32[64,256]{1,0:T(8,128)S(1)}, u32[]{:S(2)}, u32[]{:S(2)}) collective-permute-start(f32[64,256]{1,0:T(8,128)S(1)} %get-tuple-element.25.refs_0_), channel_id=1, source_target_pairs={{0,2},{1,3},{2,0},{3,1},{4,6},{5,7},{6,4},{7,5},{8,10},{9,11},{10,... | collective-permute-start | bytes 196616 | tf_op jit(solution)/shard_map/ppermute | solution.py:575
  15.6 4.0 %collective-permute-start.2 = (f32[64,256]{1,0:T(8,128)S(1)}, f32[64,256]{1,0:T(8,128)S(1)}, u32[]{:S(2)}, u32[]{:S(2)}) collective-permute-start(f32[64,256]{1,0:T(8,128)S(1)} %get-tuple-element.25.refs_0_), channel_id=1, source_target_pairs={{0,3},{1,2},{2,1},{3,0},{4,7},{5,6},{6,5},{7,4},{8,11},{9,10},{10,... | collective-permute-start | bytes 196616 | tf_op jit(solution)/shard_map/ppermute | solution.py:575
  36.1 1.9 %collective-permute-start.3 = (f32[16,128]{1,0:T(8,128)S(1)}, f32[16,128]{1,0:T(8,128)S(1)}, u32[]{:S(2)}, u32[]{:S(2)}) collective-permute-start(f32[16,128]{1,0:T(8,128)S(1)} %down.1), channel_id=1, source_target_pairs={{0,1},{1,0},{2,3},{3,2},{4,5},{5,4},{6,7},{7,6},{8,9},{9,8},{10,11... | collective-permute-start | bytes 24584 | tf_op jit(solution)/shard_map/ppermute | solution.py:598
  36.3 3.7 %collective-permute-start.4 = (f32[16,128]{1,0:T(8,128)S(1)}, f32[16,128]{1,0:T(8,128)S(1)}, u32[]{:S(2)}, u32[]{:S(2)}) collective-permute-start(f32[16,128]{1,0:T(8,128)S(1)} %down.1), channel_id=1, source_target_pairs={{0,2},{1,3},{2,0},{3,1},{4,6},{5,7},{6,4},{7,5},{8,10},{9,11},{10,... | collective-permute-start | bytes 24584 | tf_op jit(solution)/shard_map/ppermute | solution.py:598
  37.7 3.1 %collective-permute-start.5 = (f32[16,128]{1,0:T(8,128)S(1)}, f32[16,128]{1,0:T(8,128)S(1)}, u32[]{:S(2)}, u32[]{:S(2)}) collective-permute-start(f32[16,128]{1,0:T(8,128)S(1)} %down.1), channel_id=1, source_target_pairs={{0,3},{1,2},{2,1},{3,0},{4,7},{5,6},{6,5},{7,4},{8,11},{9,10},{10,... | collective-permute-start | bytes 24584 | tf_op jit(solution)/shard_map/ppermute | solution.py:598
  40.8 3.9 %collective-permute-start.6 = (f32[16,128]{1,0:T(8,128)S(1)}, f32[16,128]{1,0:T(8,128)S(1)}, u32[]{:S(2)}, u32[]{:S(2)}) collective-permute-start(f32[16,128]{1,0:T(8,128)S(1)} %add_add_fusion.1), channel_id=1, source_target_pairs={{0,9},{1,8},{2,11},{3,10},{4,13},{5,12},{6,15},{7,14},{8,1},{9,0},... | collective-permute-start | bytes 24584 | tf_op jit(solution)/shard_map/ppermute | solution.py:598
  42.1 4.0 %collective-permute-start.7 = (f32[16,128]{1,0:T(8,128)S(1)}, f32[16,128]{1,0:T(8,128)S(1)}, u32[]{:S(2)}, u32[]{:S(2)}) collective-permute-start(f32[16,128]{1,0:T(8,128)S(1)} %add_add_fusion.1), channel_id=1, source_target_pairs={{0,17},{1,16},{2,19},{3,18},{4,21},{5,20},{6,23},{7,22},{8,25},{9,... | collective-permute-start | bytes 24584 | tf_op jit(solution)/shard_map/ppermute | solution.py:598
  44.8 4.9 %collective-permute-start.8 = (f32[16,128]{1,0:T(8,128)S(1)}, f32[16,128]{1,0:T(8,128)S(1)}, u32[]{:S(2)}, u32[]{:S(2)}) collective-permute-start(f32[16,128]{1,0:T(8,128)S(1)} %add_add_fusion.1), channel_id=1, source_target_pairs={{0,25},{1,24},{2,27},{3,26},{4,29},{5,28},{6,31},{7,30},{8,17},{9,... | collective-permute-start | bytes 24584 | tf_op jit(solution)/shard_map/ppermute | solution.py:598
  49.6 3.1 %collective-permute-start.9 = (f32[16,128]{1,0:T(8,128)S(1)}, f32[16,128]{1,0:T(8,128)S(1)}, u32[]{:S(2)}, u32[]{:S(2)}) collective-permute-start(f32[16,128]{1,0:T(8,128)S(1)} %add_add_fusion.refs_0_), channel_id=1, source_target_pairs={{0,5},{1,4},{2,7},{3,6},{4,1},{5,0},{6,3},{7,2},{8,13},{9,12},{10,... | collective-permute-start | bytes 24584 | tf_op jit(solution)/shard_map/ppermute | solution.py:598

commit v11 on v10

--- a/solution.py
+++ b/solution.py
@@ -328,8 +328,9 @@
 
 
 def side_kernel(
-    dup_ref, last_ref, len_ref, cls_ref, fixed_ref, thin_ref, leaf_ref,
-    slope_ref, matrix_ref, turned_ref, given_ref,
+    dup_ref, last_ref, len_ref, cls_ref, fixed_ref, thin_ref, leaf_ref, omega_ref, single_ref,
+    nonsyn_ref,
+    slope_ref, matrix_ref, turned_ref, given_ref, class_ref,
 ):
     twice = identity_twice()
     even, odd = coefficients(len_ref, cls_ref, True)
@@ -349,6 +350,14 @@
         return carry
 
     lax.fori_loop(0, 4, matrices, 0)
+    pi_row, pi_col, table, single = fixed_ref[0], fixed_ref[1], fixed_ref[6], single_ref[...]
+    for pair in range(CLASSES // 2):
+        factor, off, rows, mean = class_pair(
+            table, nonsyn_ref[...], omega_ref, pair, twice, pi_row, pi_col
+        )
+        class_ref[pair, 0] = (off - twice * rows) / mean
+        class_ref[pair, 1] = pi_row / mean
+        class_ref[pair, 2] = factor * single
     for p in range(32):
         given_ref[p] = jnp.concatenate(leaf_messages(thin_ref, leaf_ref, p), axis=0)
 
@@ -358,7 +367,7 @@
     (
         matrix_ref, given_ref, message_ref, high_ref, low_ref, leaf_ref, scale_ref, inverse_ref,
         chain_ref, turned_ref, slope_ref, power_ref, fixed_ref,
-        weights_ref, omega_ref, single_ref, nonsyn_ref,
+        class_ref, weights_ref, nonsyn_ref,
         out_ref,
         a_high_ref, a_low_ref, count_ref, back_ref, bins_ref,
     ) = refs[members:]
@@ -440,17 +449,12 @@
             for j in range(16):
                 high, low = split(held[j])
                 e_high, e_low = chain_ref[level, 0, step * 16 + j], chain_ref[level, 1, step * 16 + j]
-                left = jnp.concatenate([
-                    jnp.concatenate([high, e_high], axis=1),
-                    jnp.concatenate([low, e_low], axis=1),
-                ], axis=0)
-                right = jnp.concatenate([
-                    jnp.concatenate([spread(e_high), spread(e_low)], axis=1),
-                    jnp.concatenate([spread(high), spread(low)], axis=1),
-                ], axis=0)
-                four = mxu(left, right)
-                held[j] = 2.0 * held[j] + (
-                    four[0:64, 0:128] + four[0:64, 128:256] + four[64:128, 0:128]
+                wide_high, wide_e_high = spread(high), spread(e_high)
+                held[j] = 2.0 * held[j] + mxu(
+                    jnp.concatenate([high, e_high, high, e_high, low, e_low], axis=1),
+                    jnp.concatenate([
+                        wide_e_high, wide_high, spread(e_low), spread(low), wide_e_high, wide_high
+                    ], axis=0),
                 )
         for j in range(16):
             back_ref[pl.ds(step * 16 + j, 64, stride=STRIDE), :] = held[j]
@@ -470,7 +474,8 @@
             bins_ref[rows_of(i + t), :] = jnp.where(mask, here[0:64], here[64:128])
     slopes = total * 0.0625
 
-    table, nonsyn = fixed_ref[6], nonsyn_ref[...]
+    ratio_table = fixed_ref[6] * nonsyn_ref[...]
+    half = lax.broadcasted_iota(jnp.int32, (1, 128), 1) < 64
     row = lax.broadcasted_iota(jnp.int32, (64, 128), 0)
     lane = lax.broadcasted_iota(jnp.int32, (64, 128), 1)
     table_grad = jnp.zeros((64, 128), F32)
@@ -494,27 +499,20 @@
         g2 = g2 + pair_products((g4, a2), (a2, g4), (g3, a1))
         g1 = g1 + pair_products((a2, g3))
         g1 = g1 + pair_products((g2, a1), (a1, g2))
-        factor, off, rows, mean = class_pair(
-            table, nonsyn, omega_ref, pair, twice, pi_row, pi_col
-        )
+        rate, pi_mean, factor = [class_ref[pair, at] for at in range(3)]
         d_rate = root_col * g1 * inverse_root_row
-        rate = (off - twice * rows) / mean
-        weighted = d_rate * rate
+        weighted = jnp.sum(d_rate * rate, axis=0, keepdims=True)
+        total0 = jnp.sum(jnp.where(half, weighted, 0.0), axis=1, keepdims=True)
+        total1 = jnp.sum(jnp.where(half, 0.0, weighted), axis=1, keepdims=True)
         diagonal = d_rate * twice
-        total0 = jnp.sum(jnp.where(mask, weighted, 0.0), axis=1, keepdims=True)
-        total1 = jnp.sum(jnp.where(mask, 0.0, weighted), axis=1, keepdims=True)
-        total0 = jnp.sum(total0, axis=0, keepdims=True)
-        total1 = jnp.sum(total1, axis=0, keepdims=True)
         diag0 = jnp.sum(jnp.where(mask, diagonal, 0.0), axis=1, keepdims=True)
         diag1 = jnp.sum(jnp.where(mask, 0.0, diagonal), axis=1, keepdims=True)
-        row_grad = jnp.where(mask, diag0 + pi_col * total0, diag1 + pi_col * total1)
-        flux_grad = (d_rate - row_grad) * pi_row / mean
-        table_grad = table_grad + flux_grad * factor * single_ref[...]
-        ratio = flux_grad * table * nonsyn
-        ratio0 = jnp.sum(jnp.where(mask, ratio, 0.0), axis=1, keepdims=True)
-        ratio1 = jnp.sum(jnp.where(mask, 0.0, ratio), axis=1, keepdims=True)
-        ratio0 = jnp.sum(ratio0, axis=0, keepdims=True)
-        ratio1 = jnp.sum(ratio1, axis=0, keepdims=True)
+        row_grad = jnp.where(mask, diag0, diag1) + pi_col * jnp.where(half, total0, total1)
+        flux_grad = (d_rate - row_grad) * pi_mean
+        table_grad = table_grad + flux_grad * factor
+        ratio = jnp.sum(flux_grad * ratio_table, axis=0, keepdims=True)
+        ratio0 = jnp.sum(jnp.where(half, ratio, 0.0), axis=1, keepdims=True)
+        ratio1 = jnp.sum(jnp.where(half, 0.0, ratio), axis=1, keepdims=True)
         omega_row = jnp.where(lane_row == 2 * pair, ratio0, omega_row)
         omega_row = jnp.where(lane_row == 2 * pair + 1, ratio1, omega_row)
     table_grad = table_grad + pltpu.roll(table_grad, 64, 1)
@@ -662,23 +660,24 @@
         chain, last, powers, dup, fixed, message, high, low, leaf, scale, inverse, thin,
     ) = inside(kept)
     tops = partners(top, "branch", 1, members)
-    slope, matrix, turned, given = inside(pl.pallas_call(
+    slope, matrix, turned, given, table_of = inside(pl.pallas_call(
         side_kernel,
         out_shape=[
             held((PAIRS * 64, 128), F32),
             held((64, 64, 256), BF),
             held((128, 128), F32),
             held((PAIRS // 2, 128, sites), F32),
+            held((CLASSES // 2, 3, 64, 128), F32),
         ],
-        in_specs=[vmem] * 7,
-        out_specs=[vmem] * 4,
+        in_specs=[vmem] * 7 + [smem, vmem, vmem],
+        out_specs=[vmem] * 5,
         compiler_params=limit,
         name="side",
-    )(dup, last, span, owner, fixed, thin, leaf))
+    )(dup, last, span, owner, fixed, thin, leaf, omega, single2, nonsyn2))
     part = pl.pallas_call(
         functools.partial(down_kernel, total_sites, members),
         out_shape=shape((16, 128), F32),
-        in_specs=[vmem] * (14 + members) + [smem, vmem, vmem],
+        in_specs=[vmem] * (16 + members),
         out_specs=vmem,
         scratch_shapes=[
             pltpu.VMEM((32, 128, sites), BF),
@@ -692,7 +691,7 @@
     )(
         *tops, matrix, given, message, high, low, leaf, scale, inverse,
         chain, turned, slope, powers, fixed,
-        outside(weights.reshape(1, sites)), omega, single2, nonsyn2,
+        table_of, outside(weights.reshape(1, sites)), nonsyn2,
     )
     parts = sum_stages(part, members, lax.axis_size("site"))
     exch, ratio, length, loglik = pl.pallas_call(

time: 53.8 us -> 54.9 us (1.020)
  Pallas kernels: 32.2 us -> 33.4 us
    pallas_call x1, Pallas kernels: 16.4 us -> 17.5 us  [body(): pl.pallas_call(functools.partial(down_kernel, total_sites, members), out_...]
where the time goes in v11:
time: 54.9 us; the launch traced here: 54.6 us
  Pallas kernels  33.4 us (61%)
  waiting for transfers between devices  10.3 us (19%)
  starting transfers between devices  10.2 us (19%)
  between operations  0.67 us (1%)
    pallas_call x1, Pallas kernels, body(): pl.pallas_call(functools.partial(down_kernel, total_sites, members), out_...  17.5 us
    pallas_call x1, Pallas kernels, body(): pl.pallas_call(up_kernel, out_shape=[shape((64, sites), F32), held((4, 2,...  11.9 us
    ppermute x7, waiting for transfers between devices, sum_stages(): lax.ppermute(x, ('site', 'branch'), [(i, i ^ step * start + flip) for i i...  9.55 us
    ppermute x7, starting transfers between devices, sum_stages(): lax.ppermute(x, ('site', 'branch'), [(i, i ^ step * start + flip) for i i...  7.08 us
    pallas_call x1, Pallas kernels, body(): pl.pallas_call(side_kernel, out_shape=[held((PAIRS * 64, 128), F32), held...  3.16 us
    ppermute x3, starting transfers between devices, partners(): lax.ppermute(x, axis, [(i, i ^ step * start) for i in range(size)])  3.15 us
  transfers between devices with their start and end apart: 10, of which 6 were waited for; matrix products, arithmetic and copies ran while one was open for 0% of the time, Pallas kernels for 6%

profile of v11, /device:TPU:0, one launch (start us, length us, event | category | flops | bytes accessed | tf_op | source)
XLA Modules:
  0.0 54.6 jit_solution(14336423414278029537)
XLA Ops:
  0.6 11.9 %up.1 = (f32[64,256]{1,0:T(8,128)S(1)}, bf16[4,2,64,64,128]{4,3,2,1,0:T(8,128)(2,1)S(1)}, f32[32,64,128]{2,1,0:T(8,128)S(1)}, f32[4,4,64,128]{3,2,1,0:T(8,128)S(...) custom-call(s32[256,256]{1,0:T(8,128)} %states_ref.1, ...), custom_call_target="tpu_custom_call" | custom-call | tf_op jit(solution)/shard_map/up/pallas_call | solution.py:630
  12.5 0.5 collective-permute-start
  13.0 2.6 %collective-permute-start.1 = (f32[64,256]{1,0:T(8,128)S(1)}, f32[64,256]{1,0:T(8,128)S(1)}, u32[]{:S(2)}, u32[]{:S(2)}) collective-permute-start(f32[64,256]{1,0:T(8,128)S(1)} %get-tuple-element.26.refs_0_), channel_id=1, source_target_pairs={{0,2},{1,3},{2,0},{3,1},{4,6},{5,7},{6,4},{7,5},{8,10},{9,11},{10,... | collective-permute-start | bytes 196616 | tf_op jit(solution)/shard_map/ppermute | solution.py:573
  15.6 0.1 collective-permute-start.2
  15.7 3.2 %side.1 = (f32[4096,128]{1,0:T(8,128)S(1)}, bf16[64,64,256]{2,1,0:T(8,128)(2,1)S(1)}, f32[128,128]{1,0:T(8,128)S(1)}, f32[32,128,256]{2,1,0:T(8,128)S(1)}, f32[4,3,64,128]{3,2,1,0:T(8,128)S(1)}) custom-call(f32[4160,128]{1,0:T(8,128)S(1)} %get-tuple-element.27.dup_ref, f32[32,64,128]{2,1,0:T(8,128)S(1)} %get-tuple-element.28.last_ref, f32[1,127]{1,0:T(1,128)} %bitcast.8, ...), custom_call_target="tpu_custom_call" | custom-call | tf_op jit(solution)/shard_map/side/pallas_call | solution.py:663
  18.8 0.0 collective-permute-done.refs_1_
  18.9 0.0 collective-permute-done.1.refs_2_
  18.9 0.8 %collective-permute-done.2.refs_3_ = f32[64,256]{1,0:T(8,128)S(1)} collective-permute-done((f32[64,256]{1,0:T(8,128)S(1)}, f32[64,256]{1,0:T(8,128)S(1)}, u32[]{:S(2)}, u32[]{:S(2)}) %collective-permute-start.2) | collective-permute-done | bytes 65568 | tf_op jit(solution)/shard_map/ppermute | solution.py:573
  19.7 17.5 %down.1 = f32[16,128]{1,0:T(8,128)S(1)} custom-call(f32[64,256]{1,0:T(8,128)S(1)} %get-tuple-element.26.refs_0_, f32[64,256]{1,0:T(8,128)S(1)} %collective-permute-done.refs_1_, f32[64,256]{1,0:T(8,128)S(1)} %collective-permute-done.1.refs_2_, f32[64,256]{1,0:T(8,128)S(1)} %collective-permute-done.2.refs_3_, ...), custom_call_target="tpu_custom_call" | custom-call | tf_op jit(solution)/shard_map/down/pallas_call | solution.py:677
  37.1 0.2 collective-permute-start.3
  37.4 1.4 %collective-permute-start.4 = (f32[16,128]{1,0:T(8,128)S(1)}, f32[16,128]{1,0:T(8,128)S(1)}, u32[]{:S(2)}, u32[]{:S(2)}) collective-permute-start(f32[16,128]{1,0:T(8,128)S(1)} %down.1), channel_id=1, source_target_pairs={{0,2},{1,3},{2,0},{3,1},{4,6},{5,7},{6,4},{7,5},{8,10},{9,11},{10,... | collective-permute-start | bytes 24584 | tf_op jit(solution)/shard_map/ppermute | solution.py:596
  38.8 0.2 collective-permute-start.5
  39.0 0.0 collective-permute-done.3
  39.0 2.0 %collective-permute-done.4 = f32[16,128]{1,0:T(8,128)S(1)} collective-permute-done((f32[16,128]{1,0:T(8,128)S(1)}, f32[16,128]{1,0:T(8,128)S(1)}, u32[]{:S(2)}, u32[]{:S(2)}) %collective-permute-start.4) | collective-permute-done | bytes 8224 | tf_op jit(solution)/shard_map/ppermute | solution.py:596
  41.0 0.9 %collective-permute-done.5 = f32[16,128]{1,0:T(8,128)S(1)} collective-permute-done((f32[16,128]{1,0:T(8,128)S(1)}, f32[16,128]{1,0:T(8,128)S(1)}, u32[]{:S(2)}, u32[]{:S(2)}) %collective-permute-start.5) | collective-permute-done | bytes 8224 | tf_op jit(solution)/shard_map/ppermute | solution.py:596
  41.9 1.3 %collective-permute-start.6 = (f32[16,128]{1,0:T(8,128)S(1)}, f32[16,128]{1,0:T(8,128)S(1)}, u32[]{:S(2)}, u32[]{:S(2)}) collective-permute-start(f32[16,128]{1,0:T(8,128)S(1)} %add_add_fusion.1), channel_id=1, source_target_pairs={{0,9},{1,8},{2,11},{3,10},{4,13},{5,12},{6,15},{7,14},{8,1},{9,0},... | collective-permute-start | bytes 24584 | tf_op jit(solution)/shard_map/ppermute | solution.py:596
  43.2 2.6 %collective-permute-start.7 = (f32[16,128]{1,0:T(8,128)S(1)}, f32[16,128]{1,0:T(8,128)S(1)}, u32[]{:S(2)}, u32[]{:S(2)}) collective-permute-start(f32[16,128]{1,0:T(8,128)S(1)} %add_add_fusion.1), channel_id=1, source_target_pairs={{0,17},{1,16},{2,19},{3,18},{4,21},{5,20},{6,23},{7,22},{8,25},{9,... | collective-permute-start | bytes 24584 | tf_op jit(solution)/shard_map/ppermute | solution.py:596
  45.8 0.0 collective-permute-start.8
  45.8 0.0 collective-permute-done.6
  45.8 1.4 %collective-permute-done.7 = f32[16,128]{1,0:T(8,128)S(1)} collective-permute-done((f32[16,128]{1,0:T(8,128)S(1)}, f32[16,128]{1,0:T(8,128)S(1)}, u32[]{:S(2)}, u32[]{:S(2)}) %collective-permute-start.7) | collective-permute-done | bytes 8224 | tf_op jit(solution)/shard_map/ppermute | solution.py:596
  47.2 3.5 %collective-permute-done.8 = f32[16,128]{1,0:T(8,128)S(1)} collective-permute-done((f32[16,128]{1,0:T(8,128)S(1)}, f32[16,128]{1,0:T(8,128)S(1)}, u32[]{:S(2)}, u32[]{:S(2)}) %collective-permute-start.8) | collective-permute-done | bytes 8224 | tf_op jit(solution)/shard_map/ppermute | solution.py:596
  50.7 1.2 %collective-permute-start.9 = (f32[16,128]{1,0:T(8,128)S(1)}, f32[16,128]{1,0:T(8,128)S(1)}, u32[]{:S(2)}, u32[]{:S(2)}) collective-permute-start(f32[16,128]{1,0:T(8,128)S(1)} %add_add_fusion.refs_0_), channel_id=1, source_target_pairs={{0,5},{1,4},{2,7},{3,6},{4,1},{5,0},{6,3},{7,2},{8,13},{9,12},{10,... | collective-permute-start | bytes 24584 | tf_op jit(solution)/shard_map/ppermute | solution.py:596
  51.9 1.8 %collective-permute-done.9.refs_1_ = f32[16,128]{1,0:T(8,128)S(1)} collective-permute-done((f32[16,128]{1,0:T(8,128)S(1)}, f32[16,128]{1,0:T(8,128)S(1)}, u32[]{:S(2)}, u32[]{:S(2)}) %collective-permute-start.9) | collective-permute-done | bytes 8224 | tf_op jit(solution)/shard_map/ppermute | solution.py:596
  53.8 0.8 %last.1 = (f32[64,64]{1,0:T(8,128)}, f32[1,8]{1,0:T(1,128)}, f32[1,127]{1,0:T(1,128)}, f32[1,1]{1,0:T(1,128)}) custom-call(f32[16,128]{1,0:T(8,128)S(1)} %add_add_fusion.refs_0_, f32[16,128]{1,0:T(8,128)S(1)} %collective-permute-done.9.refs_1_), custom_call_target="tpu_custom_call" | custom-call | tf_op jit(solution)/shard_map/last/pallas_call | solution.py:697
  (2 shorter events, 0.0 us)
Async XLA Ops:
  12.5 6.3 %collective-permute-start = (f32[64,256]{1,0:T(8,128)S(1)}, f32[64,256]{1,0:T(8,128)S(1)}, u32[]{:S(2)}, u32[]{:S(2)}) collective-permute-start(f32[64,256]{1,0:T(8,128)S(1)} %get-tuple-element.26.refs_0_), channel_id=1, source_target_pairs={{0,1},{1,0},{2,3},{3,2},{4,5},{5,4},{6,7},{7,6},{8,9},{9,8},{10,11... | collective-permute-start | bytes 196616 | tf_op jit(solution)/shard_map/ppermute | solution.py:573
  13.0 5.8 %collective-permute-start.1 = (f32[64,256]{1,0:T(8,128)S(1)}, f32[64,256]{1,0:T(8,128)S(1)}, u32[]{:S(2)}, u32[]{:S(2)}) collective-permute-start(f32[64,256]{1,0:T(8,128)S(1)} %get-tuple-element.26.refs_0_), channel_id=1, source_target_pairs={{0,2},{1,3},{2,0},{3,1},{4,6},{5,7},{6,4},{7,5},{8,10},{9,11},{10,... | collective-permute-start | bytes 196616 | tf_op jit(solution)/shard_map/ppermute | solution.py:573
  15.6 4.0 %collective-permute-start.2 = (f32[64,256]{1,0:T(8,128)S(1)}, f32[64,256]{1,0:T(8,128)S(1)}, u32[]{:S(2)}, u32[]{:S(2)}) collective-permute-start(f32[64,256]{1,0:T(8,128)S(1)} %get-tuple-element.26.refs_0_), channel_id=1, source_target_pairs={{0,3},{1,2},{2,1},{3,0},{4,7},{5,6},{6,5},{7,4},{8,11},{9,10},{10,... | collective-permute-start | bytes 196616 | tf_op jit(solution)/shard_map/ppermute | solution.py:573
  37.1 1.9 %collective-permute-start.3 = (f32[16,128]{1,0:T(8,128)S(1)}, f32[16,128]{1,0:T(8,128)S(1)}, u32[]{:S(2)}, u32[]{:S(2)}) collective-permute-start(f32[16,128]{1,0:T(8,128)S(1)} %down.1), channel_id=1, source_target_pairs={{0,1},{1,0},{2,3},{3,2},{4,5},{5,4},{6,7},{7,6},{8,9},{9,8},{10,11... | collective-permute-start | bytes 24584 | tf_op jit(solution)/shard_map/ppermute | solution.py:596
  37.4 3.7 %collective-permute-start.4 = (f32[16,128]{1,0:T(8,128)S(1)}, f32[16,128]{1,0:T(8,128)S(1)}, u32[]{:S(2)}, u32[]{:S(2)}) collective-permute-start(f32[16,128]{1,0:T(8,128)S(1)} %down.1), channel_id=1, source_target_pairs={{0,2},{1,3},{2,0},{3,1},{4,6},{5,7},{6,4},{7,5},{8,10},{9,11},{10,... | collective-permute-start | bytes 24584 | tf_op jit(solution)/shard_map/ppermute | solution.py:596
  38.8 3.1 %collective-permute-start.5 = (f32[16,128]{1,0:T(8,128)S(1)}, f32[16,128]{1,0:T(8,128)S(1)}, u32[]{:S(2)}, u32[]{:S(2)}) collective-permute-start(f32[16,128]{1,0:T(8,128)S(1)} %down.1), channel_id=1, source_target_pairs={{0,3},{1,2},{2,1},{3,0},{4,7},{5,6},{6,5},{7,4},{8,11},{9,10},{10,... | collective-permute-start | bytes 24584 | tf_op jit(solution)/shard_map/ppermute | solution.py:596
  41.9 3.9 %collective-permute-start.6 = (f32[16,128]{1,0:T(8,128)S(1)}, f32[16,128]{1,0:T(8,128)S(1)}, u32[]{:S(2)}, u32[]{:S(2)}) collective-permute-start(f32[16,128]{1,0:T(8,128)S(1)} %add_add_fusion.1), channel_id=1, source_target_pairs={{0,9},{1,8},{2,11},{3,10},{4,13},{5,12},{6,15},{7,14},{8,1},{9,0},... | collective-permute-start | bytes 24584 | tf_op jit(solution)/shard_map/ppermute | solution.py:596
  43.2 4.0 %collective-permute-start.7 = (f32[16,128]{1,0:T(8,128)S(1)}, f32[16,128]{1,0:T(8,128)S(1)}, u32[]{:S(2)}, u32[]{:S(2)}) collective-permute-start(f32[16,128]{1,0:T(8,128)S(1)} %add_add_fusion.1), channel_id=1, source_target_pairs={{0,17},{1,16},{2,19},{3,18},{4,21},{5,20},{6,23},{7,22},{8,25},{9,... | collective-permute-start | bytes 24584 | tf_op jit(solution)/shard_map/ppermute | solution.py:596
  45.8 4.9 %collective-permute-start.8 = (f32[16,128]{1,0:T(8,128)S(1)}, f32[16,128]{1,0:T(8,128)S(1)}, u32[]{:S(2)}, u32[]{:S(2)}) collective-permute-start(f32[16,128]{1,0:T(8,128)S(1)} %add_add_fusion.1), channel_id=1, source_target_pairs={{0,25},{1,24},{2,27},{3,26},{4,29},{5,28},{6,31},{7,30},{8,17},{9,... | collective-permute-start | bytes 24584 | tf_op jit(solution)/shard_map/ppermute | solution.py:596
  50.7 3.1 %collective-permute-start.9 = (f32[16,128]{1,0:T(8,128)S(1)}, f32[16,128]{1,0:T(8,128)S(1)}, u32[]{:S(2)}, u32[]{:S(2)}) collective-permute-start(f32[16,128]{1,0:T(8,128)S(1)} %add_add_fusion.refs_0_), channel_id=1, source_target_pairs={{0,5},{1,4},{2,7},{3,6},{4,1},{5,0},{6,3},{7,2},{8,13},{9,12},{10,... | collective-permute-start | bytes 24584 | tf_op jit(solution)/shard_map/ppermute | solution.py:596

commit v12 on v11

--- a/solution.py
+++ b/solution.py
@@ -403,9 +403,10 @@
         child = 2 * r - 64
         u_high = jnp.concatenate([high_ref[child], high_ref[child + 1]], axis=0)
         u_low = jnp.concatenate([low_ref[child], low_ref[child + 1]], axis=0)
-        first = mxu_nt(jnp.concatenate([a_high, a_low], axis=0), u_high)
-        second = mxu_nt(a_high, u_low)
-        store_counts(r, first[0:128] + first[128:256] + second)
+        four = mxu_nt(
+            jnp.concatenate([a_high, a_low], axis=0), jnp.concatenate([u_high, u_low], axis=0)
+        )
+        store_counts(r, four[0:128, 0:128] + four[0:128, 128:256] + four[128:256, 0:128])
         return [
             messages(
                 matrix_ref[2 * (r - 32) + e], a_high[64 * e : 64 * e + 64], a_low[64 * e : 64 * e + 64]
@@ -449,12 +450,17 @@
             for j in range(16):
                 high, low = split(held[j])
                 e_high, e_low = chain_ref[level, 0, step * 16 + j], chain_ref[level, 1, step * 16 + j]
-                wide_high, wide_e_high = spread(high), spread(e_high)
-                held[j] = 2.0 * held[j] + mxu(
-                    jnp.concatenate([high, e_high, high, e_high, low, e_low], axis=1),
-                    jnp.concatenate([
-                        wide_e_high, wide_high, spread(e_low), spread(low), wide_e_high, wide_high
-                    ], axis=0),
+                left = jnp.concatenate([
+                    jnp.concatenate([high, e_high], axis=1),
+                    jnp.concatenate([low, e_low], axis=1),
+                ], axis=0)
+                right = jnp.concatenate([
+                    jnp.concatenate([spread(e_high), spread(e_low)], axis=1),
+                    jnp.concatenate([spread(high), spread(low)], axis=1),
+                ], axis=0)
+                four = mxu(left, right)
+                held[j] = 2.0 * held[j] + (
+                    four[0:64, 0:128] + four[0:64, 128:256] + four[64:128, 0:128]
                 )
         for j in range(16):
             back_ref[pl.ds(step * 16 + j, 64, stride=STRIDE), :] = held[j]

time: 54.9 us -> 53.5 us (0.974)
  Pallas kernels: 33.4 us -> 31.9 us
    pallas_call x1, Pallas kernels: 17.5 us -> 16 us  [body(): pl.pallas_call(functools.partial(down_kernel, total_sites, members), out_...]
where the time goes in v12:
time: 53.5 us; the launch traced here: 53.2 us
  Pallas kernels  31.9 us (60%)
  waiting for transfers between devices  10.3 us (19%)
  starting transfers between devices  10.2 us (19%)
  between operations  0.67 us (1%)
    pallas_call x1, Pallas kernels, body(): pl.pallas_call(functools.partial(down_kernel, total_sites, members), out_...  16 us
    pallas_call x1, Pallas kernels, body(): pl.pallas_call(up_kernel, out_shape=[shape((64, sites), F32), held((4, 2,...  11.9 us
    ppermute x7, waiting for transfers between devices, sum_stages(): lax.ppermute(x, ('site', 'branch'), [(i, i ^ step * start + flip) for i i...  9.55 us
    ppermute x7, starting transfers between devices, sum_stages(): lax.ppermute(x, ('site', 'branch'), [(i, i ^ step * start + flip) for i i...  7.07 us
    pallas_call x1, Pallas kernels, body(): pl.pallas_call(side_kernel, out_shape=[held((PAIRS * 64, 128), F32), held...  3.16 us
    ppermute x3, starting transfers between devices, partners(): lax.ppermute(x, axis, [(i, i ^ step * start) for i in range(size)])  3.15 us
  transfers between devices with their start and end apart: 10, of which 6 were waited for; matrix products, arithmetic and copies ran while one was open for 0% of the time, Pallas kernels for 6%

profile of v12, /device:TPU:0, one launch (start us, length us, event | category | flops | bytes accessed | tf_op | source)
XLA Modules:
  0.0 53.2 jit_solution(4306309772326112565)
XLA Ops:
  0.6 11.9 %up.1 = (f32[64,256]{1,0:T(8,128)S(1)}, bf16[4,2,64,64,128]{4,3,2,1,0:T(8,128)(2,1)S(1)}, f32[32,64,128]{2,1,0:T(8,128)S(1)}, f32[4,4,64,128]{3,2,1,0:T(8,128)S(...) custom-call(s32[256,256]{1,0:T(8,128)} %states_ref.1, ...), custom_call_target="tpu_custom_call" | custom-call | tf_op jit(solution)/shard_map/up/pallas_call | solution.py:636
  12.5 0.5 collective-permute-start
  13.0 2.6 %collective-permute-start.1 = (f32[64,256]{1,0:T(8,128)S(1)}, f32[64,256]{1,0:T(8,128)S(1)}, u32[]{:S(2)}, u32[]{:S(2)}) collective-permute-start(f32[64,256]{1,0:T(8,128)S(1)} %get-tuple-element.26.refs_0_), channel_id=1, source_target_pairs={{0,2},{1,3},{2,0},{3,1},{4,6},{5,7},{6,4},{7,5},{8,10},{9,11},{10,... | collective-permute-start | bytes 196616 | tf_op jit(solution)/shard_map/ppermute | solution.py:579
  15.6 0.1 collective-permute-start.2
  15.7 3.2 %side.1 = (f32[4096,128]{1,0:T(8,128)S(1)}, bf16[64,64,256]{2,1,0:T(8,128)(2,1)S(1)}, f32[128,128]{1,0:T(8,128)S(1)}, f32[32,128,256]{2,1,0:T(8,128)S(1)}, f32[4,3,64,128]{3,2,1,0:T(8,128)S(1)}) custom-call(f32[4160,128]{1,0:T(8,128)S(1)} %get-tuple-element.27.dup_ref, f32[32,64,128]{2,1,0:T(8,128)S(1)} %get-tuple-element.28.last_ref, f32[1,127]{1,0:T(1,128)} %bitcast.8, ...), custom_call_target="tpu_custom_call" | custom-call | tf_op jit(solution)/shard_map/side/pallas_call | solution.py:669
  18.8 0.0 collective-permute-done.refs_1_
  18.9 0.0 collective-permute-done.1.refs_2_
  18.9 0.8 %collective-permute-done.2.refs_3_ = f32[64,256]{1,0:T(8,128)S(1)} collective-permute-done((f32[64,256]{1,0:T(8,128)S(1)}, f32[64,256]{1,0:T(8,128)S(1)}, u32[]{:S(2)}, u32[]{:S(2)}) %collective-permute-start.2) | collective-permute-done | bytes 65568 | tf_op jit(solution)/shard_map/ppermute | solution.py:579
  19.7 16.0 %down.1 = f32[16,128]{1,0:T(8,128)S(1)} custom-call(f32[64,256]{1,0:T(8,128)S(1)} %get-tuple-element.26.refs_0_, f32[64,256]{1,0:T(8,128)S(1)} %collective-permute-done.refs_1_, f32[64,256]{1,0:T(8,128)S(1)} %collective-permute-done.1.refs_2_, f32[64,256]{1,0:T(8,128)S(1)} %collective-permute-done.2.refs_3_, ...), custom_call_target="tpu_custom_call" | custom-call | tf_op jit(solution)/shard_map/down/pallas_call | solution.py:683
  35.7 0.2 collective-permute-start.3
  35.9 1.5 %collective-permute-start.4 = (f32[16,128]{1,0:T(8,128)S(1)}, f32[16,128]{1,0:T(8,128)S(1)}, u32[]{:S(2)}, u32[]{:S(2)}) collective-permute-start(f32[16,128]{1,0:T(8,128)S(1)} %down.1), channel_id=1, source_target_pairs={{0,2},{1,3},{2,0},{3,1},{4,6},{5,7},{6,4},{7,5},{8,10},{9,11},{10,... | collective-permute-start | bytes 24584 | tf_op jit(solution)/shard_map/ppermute | solution.py:602
  37.4 0.2 collective-permute-start.5
  37.6 0.0 collective-permute-done.3
  37.6 2.0 %collective-permute-done.4 = f32[16,128]{1,0:T(8,128)S(1)} collective-permute-done((f32[16,128]{1,0:T(8,128)S(1)}, f32[16,128]{1,0:T(8,128)S(1)}, u32[]{:S(2)}, u32[]{:S(2)}) %collective-permute-start.4) | collective-permute-done | bytes 8224 | tf_op jit(solution)/shard_map/ppermute | solution.py:602
  39.6 0.9 %collective-permute-done.5 = f32[16,128]{1,0:T(8,128)S(1)} collective-permute-done((f32[16,128]{1,0:T(8,128)S(1)}, f32[16,128]{1,0:T(8,128)S(1)}, u32[]{:S(2)}, u32[]{:S(2)}) %collective-permute-start.5) | collective-permute-done | bytes 8224 | tf_op jit(solution)/shard_map/ppermute | solution.py:602
  40.5 1.3 %collective-permute-start.6 = (f32[16,128]{1,0:T(8,128)S(1)}, f32[16,128]{1,0:T(8,128)S(1)}, u32[]{:S(2)}, u32[]{:S(2)}) collective-permute-start(f32[16,128]{1,0:T(8,128)S(1)} %add_add_fusion.1), channel_id=1, source_target_pairs={{0,9},{1,8},{2,11},{3,10},{4,13},{5,12},{6,15},{7,14},{8,1},{9,0},... | collective-permute-start | bytes 24584 | tf_op jit(solution)/shard_map/ppermute | solution.py:602
  41.8 2.6 %collective-permute-start.7 = (f32[16,128]{1,0:T(8,128)S(1)}, f32[16,128]{1,0:T(8,128)S(1)}, u32[]{:S(2)}, u32[]{:S(2)}) collective-permute-start(f32[16,128]{1,0:T(8,128)S(1)} %add_add_fusion.1), channel_id=1, source_target_pairs={{0,17},{1,16},{2,19},{3,18},{4,21},{5,20},{6,23},{7,22},{8,25},{9,... | collective-permute-start | bytes 24584 | tf_op jit(solution)/shard_map/ppermute | solution.py:602
  44.4 0.0 collective-permute-start.8
  44.4 0.0 collective-permute-done.6
  44.4 1.4 %collective-permute-done.7 = f32[16,128]{1,0:T(8,128)S(1)} collective-permute-done((f32[16,128]{1,0:T(8,128)S(1)}, f32[16,128]{1,0:T(8,128)S(1)}, u32[]{:S(2)}, u32[]{:S(2)}) %collective-permute-start.7) | collective-permute-done | bytes 8224 | tf_op jit(solution)/shard_map/ppermute | solution.py:602
  45.8 3.5 %collective-permute-done.8 = f32[16,128]{1,0:T(8,128)S(1)} collective-permute-done((f32[16,128]{1,0:T(8,128)S(1)}, f32[16,128]{1,0:T(8,128)S(1)}, u32[]{:S(2)}, u32[]{:S(2)}) %collective-permute-start.8) | collective-permute-done | bytes 8224 | tf_op jit(solution)/shard_map/ppermute | solution.py:602
  49.3 1.2 %collective-permute-start.9 = (f32[16,128]{1,0:T(8,128)S(1)}, f32[16,128]{1,0:T(8,128)S(1)}, u32[]{:S(2)}, u32[]{:S(2)}) collective-permute-start(f32[16,128]{1,0:T(8,128)S(1)} %add_add_fusion.refs_0_), channel_id=1, source_target_pairs={{0,5},{1,4},{2,7},{3,6},{4,1},{5,0},{6,3},{7,2},{8,13},{9,12},{10,... | collective-permute-start | bytes 24584 | tf_op jit(solution)/shard_map/ppermute | solution.py:602
  50.5 1.8 %collective-permute-done.9.refs_1_ = f32[16,128]{1,0:T(8,128)S(1)} collective-permute-done((f32[16,128]{1,0:T(8,128)S(1)}, f32[16,128]{1,0:T(8,128)S(1)}, u32[]{:S(2)}, u32[]{:S(2)}) %collective-permute-start.9) | collective-permute-done | bytes 8224 | tf_op jit(solution)/shard_map/ppermute | solution.py:602
  52.3 0.8 %last.1 = (f32[64,64]{1,0:T(8,128)}, f32[1,8]{1,0:T(1,128)}, f32[1,127]{1,0:T(1,128)}, f32[1,1]{1,0:T(1,128)}) custom-call(f32[16,128]{1,0:T(8,128)S(1)} %add_add_fusion.refs_0_, f32[16,128]{1,0:T(8,128)S(1)} %collective-permute-done.9.refs_1_), custom_call_target="tpu_custom_call" | custom-call | tf_op jit(solution)/shard_map/last/pallas_call | solution.py:703
  (2 shorter events, 0.0 us)
Async XLA Ops:
  12.5 6.3 %collective-permute-start = (f32[64,256]{1,0:T(8,128)S(1)}, f32[64,256]{1,0:T(8,128)S(1)}, u32[]{:S(2)}, u32[]{:S(2)}) collective-permute-start(f32[64,256]{1,0:T(8,128)S(1)} %get-tuple-element.26.refs_0_), channel_id=1, source_target_pairs={{0,1},{1,0},{2,3},{3,2},{4,5},{5,4},{6,7},{7,6},{8,9},{9,8},{10,11... | collective-permute-start | bytes 196616 | tf_op jit(solution)/shard_map/ppermute | solution.py:579
  13.0 5.8 %collective-permute-start.1 = (f32[64,256]{1,0:T(8,128)S(1)}, f32[64,256]{1,0:T(8,128)S(1)}, u32[]{:S(2)}, u32[]{:S(2)}) collective-permute-start(f32[64,256]{1,0:T(8,128)S(1)} %get-tuple-element.26.refs_0_), channel_id=1, source_target_pairs={{0,2},{1,3},{2,0},{3,1},{4,6},{5,7},{6,4},{7,5},{8,10},{9,11},{10,... | collective-permute-start | bytes 196616 | tf_op jit(solution)/shard_map/ppermute | solution.py:579
  15.6 4.0 %collective-permute-start.2 = (f32[64,256]{1,0:T(8,128)S(1)}, f32[64,256]{1,0:T(8,128)S(1)}, u32[]{:S(2)}, u32[]{:S(2)}) collective-permute-start(f32[64,256]{1,0:T(8,128)S(1)} %get-tuple-element.26.refs_0_), channel_id=1, source_target_pairs={{0,3},{1,2},{2,1},{3,0},{4,7},{5,6},{6,5},{7,4},{8,11},{9,10},{10,... | collective-permute-start | bytes 196616 | tf_op jit(solution)/shard_map/ppermute | solution.py:579
  35.7 1.9 %collective-permute-start.3 = (f32[16,128]{1,0:T(8,128)S(1)}, f32[16,128]{1,0:T(8,128)S(1)}, u32[]{:S(2)}, u32[]{:S(2)}) collective-permute-start(f32[16,128]{1,0:T(8,128)S(1)} %down.1), channel_id=1, source_target_pairs={{0,1},{1,0},{2,3},{3,2},{4,5},{5,4},{6,7},{7,6},{8,9},{9,8},{10,11... | collective-permute-start | bytes 24584 | tf_op jit(solution)/shard_map/ppermute | solution.py:602
  35.9 3.7 %collective-permute-start.4 = (f32[16,128]{1,0:T(8,128)S(1)}, f32[16,128]{1,0:T(8,128)S(1)}, u32[]{:S(2)}, u32[]{:S(2)}) collective-permute-start(f32[16,128]{1,0:T(8,128)S(1)} %down.1), channel_id=1, source_target_pairs={{0,2},{1,3},{2,0},{3,1},{4,6},{5,7},{6,4},{7,5},{8,10},{9,11},{10,... | collective-permute-start | bytes 24584 | tf_op jit(solution)/shard_map/ppermute | solution.py:602
  37.4 3.1 %collective-permute-start.5 = (f32[16,128]{1,0:T(8,128)S(1)}, f32[16,128]{1,0:T(8,128)S(1)}, u32[]{:S(2)}, u32[]{:S(2)}) collective-permute-start(f32[16,128]{1,0:T(8,128)S(1)} %down.1), channel_id=1, source_target_pairs={{0,3},{1,2},{2,1},{3,0},{4,7},{5,6},{6,5},{7,4},{8,11},{9,10},{10,... | collective-permute-start | bytes 24584 | tf_op jit(solution)/shard_map/ppermute | solution.py:602
  40.5 3.9 %collective-permute-start.6 = (f32[16,128]{1,0:T(8,128)S(1)}, f32[16,128]{1,0:T(8,128)S(1)}, u32[]{:S(2)}, u32[]{:S(2)}) collective-permute-start(f32[16,128]{1,0:T(8,128)S(1)} %add_add_fusion.1), channel_id=1, source_target_pairs={{0,9},{1,8},{2,11},{3,10},{4,13},{5,12},{6,15},{7,14},{8,1},{9,0},... | collective-permute-start | bytes 24584 | tf_op jit(solution)/shard_map/ppermute | solution.py:602
  41.8 4.0 %collective-permute-start.7 = (f32[16,128]{1,0:T(8,128)S(1)}, f32[16,128]{1,0:T(8,128)S(1)}, u32[]{:S(2)}, u32[]{:S(2)}) collective-permute-start(f32[16,128]{1,0:T(8,128)S(1)} %add_add_fusion.1), channel_id=1, source_target_pairs={{0,17},{1,16},{2,19},{3,18},{4,21},{5,20},{6,23},{7,22},{8,25},{9,... | collective-permute-start | bytes 24584 | tf_op jit(solution)/shard_map/ppermute | solution.py:602
  44.4 4.9 %collective-permute-start.8 = (f32[16,128]{1,0:T(8,128)S(1)}, f32[16,128]{1,0:T(8,128)S(1)}, u32[]{:S(2)}, u32[]{:S(2)}) collective-permute-start(f32[16,128]{1,0:T(8,128)S(1)} %add_add_fusion.1), channel_id=1, source_target_pairs={{0,25},{1,24},{2,27},{3,26},{4,29},{5,28},{6,31},{7,30},{8,17},{9,... | collective-permute-start | bytes 24584 | tf_op jit(solution)/shard_map/ppermute | solution.py:602
  49.3 3.1 %collective-permute-start.9 = (f32[16,128]{1,0:T(8,128)S(1)}, f32[16,128]{1,0:T(8,128)S(1)}, u32[]{:S(2)}, u32[]{:S(2)}) collective-permute-start(f32[16,128]{1,0:T(8,128)S(1)} %add_add_fusion.refs_0_), channel_id=1, source_target_pairs={{0,5},{1,4},{2,7},{3,6},{4,1},{5,0},{6,3},{7,2},{8,13},{9,12},{10,... | collective-permute-start | bytes 24584 | tf_op jit(solution)/shard_map/ppermute | solution.py:602

commit v13 on v12

--- a/solution.py
+++ b/solution.py
@@ -267,7 +267,8 @@
 
     expand(jnp.where(low_half(), even, odd), dup_ref, store)
 
-    def squarings(leaves, step, carry):
+    def squarings(step):
+        leaves = step < 2
         width = 16
         held = [first_ref[pl.ds(step * width + j, 64, stride=STRIDE), :] for j in range(width)]
         for level in range(4):
@@ -288,11 +289,10 @@
             else:
                 last_ref[p - 32] = held[j]
                 double(up_ref, p - 32, matrix)
-        return carry
 
     inverse_root_col = 1.0 / root_col
-    lax.fori_loop(0, 2, functools.partial(squarings, True), 0)
-    lax.fori_loop(2, 4, functools.partial(squarings, False), 0)
+    squarings(0)
+    squarings(1)
 
     def finish(p, message):
         if p >= 32:
@@ -306,8 +306,12 @@
         high_ref[p] = high
         low_ref[p] = low
 
-    for p in range(32):
+    for p in range(16):
         finish(p, leaf_messages(thin_ref, leaf_ref, p))
+    squarings(2)
+    for p in range(16, 32):
+        finish(p, leaf_messages(thin_ref, leaf_ref, p))
+    squarings(3)
 
     def inner(p):
         child = 2 * p - 64
@@ -433,18 +437,7 @@
             a_high_ref[p - 32] = high
             a_low_ref[p - 32] = low
 
-    for r in range(63, 47, -1):
-        inner(r)
-
-    for r in range(47, 31, -1):
-        down = descend(r)
-        for e in range(2):
-            p = 2 * r + e - 64
-            high, low = children(down, e, p)
-            square = mxu_nt(jnp.concatenate([high, low], axis=0), leaf_ref[p])
-            store_counts(p, square[0:128] + square[128:256])
-
-    def adjoint(step, carry):
+    def adjoint(step):
         held = [count_ref[step * 16 + j] for j in range(16)]
         for level in range(3, -1, -1):
             for j in range(16):
@@ -464,9 +457,24 @@
                 )
         for j in range(16):
             back_ref[pl.ds(step * 16 + j, 64, stride=STRIDE), :] = held[j]
-        return carry
-
-    lax.fori_loop(0, PAIRS // 16, adjoint, 0)
+
+    def outer(r):
+        down = descend(r)
+        for e in range(2):
+            p = 2 * r + e - 64
+            high, low = children(down, e, p)
+            square = mxu_nt(jnp.concatenate([high, low], axis=0), leaf_ref[p])
+            store_counts(p, square[0:128] + square[128:256])
+
+    for r in range(63, 47, -1):
+        inner(r)
+    for r in range(47, 39, -1):
+        outer(r)
+    adjoint(3)
+    for r in range(39, 31, -1):
+        outer(r)
+    for step in (1, 2, 0):
+        adjoint(step)
 
     left = four_left(turned_ref[...])
 

time: 53.5 us -> 52.6 us (0.983)
  Pallas kernels: 31.9 us -> 31.3 us
where the time goes in v13:
time: 52.6 us; the launch traced here: 52.4 us
  Pallas kernels  31.3 us (60%)
  starting transfers between devices  10.2 us (19%)
  waiting for transfers between devices  10.2 us (19%)
  between operations  0.67 us (1%)
    pallas_call x1, Pallas kernels, body(): pl.pallas_call(functools.partial(down_kernel, total_sites, members), out_...  15.5 us
    pallas_call x1, Pallas kernels, body(): pl.pallas_call(up_kernel, out_shape=[shape((64, sites), F32), held((4, 2,...  11.6 us
    ppermute x7, waiting for transfers between devices, sum_stages(): lax.ppermute(x, ('site', 'branch'), [(i, i ^ step * start + flip) for i i...  9.54 us
    ppermute x7, starting transfers between devices, sum_stages(): lax.ppermute(x, ('site', 'branch'), [(i, i ^ step * start + flip) for i i...  7.04 us
    pallas_call x1, Pallas kernels, body(): pl.pallas_call(side_kernel, out_shape=[held((PAIRS * 64, 128), F32), held...  3.34 us
    ppermute x3, starting transfers between devices, partners(): lax.ppermute(x, axis, [(i, i ^ step * start) for i in range(size)])  3.15 us
  transfers between devices with their start and end apart: 10, of which 6 were waited for; matrix products, arithmetic and copies ran while one was open for 0% of the time, Pallas kernels for 6%

profile of v13, /device:TPU:0, one launch (start us, length us, event | category | flops | bytes accessed | tf_op | source)
XLA Modules:
  0.0 52.4 jit_solution(13215058508871180694)
XLA Ops:
  0.6 11.6 %up.1 = (f32[64,256]{1,0:T(8,128)S(1)}, bf16[4,2,64,64,128]{4,3,2,1,0:T(8,128)(2,1)S(1)}, f32[32,64,128]{2,1,0:T(8,128)S(1)}, f32[4,4,64,128]{3,2,1,0:T(8,128)S(...) custom-call(s32[256,256]{1,0:T(8,128)} %states_ref.1, ...), custom_call_target="tpu_custom_call" | custom-call | tf_op jit(solution)/shard_map/up/pallas_call | solution.py:644
  12.2 0.5 collective-permute-start
  12.8 2.6 %collective-permute-start.1 = (f32[64,256]{1,0:T(8,128)S(1)}, f32[64,256]{1,0:T(8,128)S(1)}, u32[]{:S(2)}, u32[]{:S(2)}) collective-permute-start(f32[64,256]{1,0:T(8,128)S(1)} %get-tuple-element.26.refs_0_), channel_id=1, source_target_pairs={{0,2},{1,3},{2,0},{3,1},{4,6},{5,7},{6,4},{7,5},{8,10},{9,11},{10,... | collective-permute-start | bytes 196616 | tf_op jit(solution)/shard_map/ppermute | solution.py:587
  15.3 0.1 collective-permute-start.2
  15.4 3.3 %side.1 = (f32[4096,128]{1,0:T(8,128)S(1)}, bf16[64,64,256]{2,1,0:T(8,128)(2,1)S(1)}, f32[128,128]{1,0:T(8,128)S(1)}, f32[32,128,256]{2,1,0:T(8,128)S(1)}, f32[4,3,64,128]{3,2,1,0:T(8,128)S(1)}) custom-call(f32[4160,128]{1,0:T(8,128)S(1)} %get-tuple-element.27.dup_ref, f32[32,64,128]{2,1,0:T(8,128)S(1)} %get-tuple-element.28.last_ref, f32[1,127]{1,0:T(1,128)} %bitcast.8, ...), custom_call_target="tpu_custom_call" | custom-call | tf_op jit(solution)/shard_map/side/pallas_call | solution.py:677
  18.7 0.0 collective-permute-done.refs_1_
  18.7 0.0 collective-permute-done.1.refs_2_
  18.8 0.6 %collective-permute-done.2.refs_3_ = f32[64,256]{1,0:T(8,128)S(1)} collective-permute-done((f32[64,256]{1,0:T(8,128)S(1)}, f32[64,256]{1,0:T(8,128)S(1)}, u32[]{:S(2)}, u32[]{:S(2)}) %collective-permute-start.2) | collective-permute-done | bytes 65568 | tf_op jit(solution)/shard_map/ppermute | solution.py:587
  19.4 15.5 %down.1 = f32[16,128]{1,0:T(8,128)S(1)} custom-call(f32[64,256]{1,0:T(8,128)S(1)} %get-tuple-element.26.refs_0_, f32[64,256]{1,0:T(8,128)S(1)} %collective-permute-done.refs_1_, f32[64,256]{1,0:T(8,128)S(1)} %collective-permute-done.1.refs_2_, f32[64,256]{1,0:T(8,128)S(1)} %collective-permute-done.2.refs_3_, ...), custom_call_target="tpu_custom_call" | custom-call | tf_op jit(solution)/shard_map/down/pallas_call | solution.py:691
  34.9 0.2 collective-permute-start.3
  35.1 1.4 %collective-permute-start.4 = (f32[16,128]{1,0:T(8,128)S(1)}, f32[16,128]{1,0:T(8,128)S(1)}, u32[]{:S(2)}, u32[]{:S(2)}) collective-permute-start(f32[16,128]{1,0:T(8,128)S(1)} %down.1), channel_id=1, source_target_pairs={{0,2},{1,3},{2,0},{3,1},{4,6},{5,7},{6,4},{7,5},{8,10},{9,11},{10,... | collective-permute-start | bytes 24584 | tf_op jit(solution)/shard_map/ppermute | solution.py:610
  36.5 0.2 collective-permute-start.5
  36.8 0.0 collective-permute-done.3
  36.8 2.0 %collective-permute-done.4 = f32[16,128]{1,0:T(8,128)S(1)} collective-permute-done((f32[16,128]{1,0:T(8,128)S(1)}, f32[16,128]{1,0:T(8,128)S(1)}, u32[]{:S(2)}, u32[]{:S(2)}) %collective-permute-start.4) | collective-permute-done | bytes 8224 | tf_op jit(solution)/shard_map/ppermute | solution.py:610
  38.8 0.9 %collective-permute-done.5 = f32[16,128]{1,0:T(8,128)S(1)} collective-permute-done((f32[16,128]{1,0:T(8,128)S(1)}, f32[16,128]{1,0:T(8,128)S(1)}, u32[]{:S(2)}, u32[]{:S(2)}) %collective-permute-start.5) | collective-permute-done | bytes 8224 | tf_op jit(solution)/shard_map/ppermute | solution.py:610
  39.6 1.3 %collective-permute-start.6 = (f32[16,128]{1,0:T(8,128)S(1)}, f32[16,128]{1,0:T(8,128)S(1)}, u32[]{:S(2)}, u32[]{:S(2)}) collective-permute-start(f32[16,128]{1,0:T(8,128)S(1)} %add_add_fusion.1), channel_id=1, source_target_pairs={{0,9},{1,8},{2,11},{3,10},{4,13},{5,12},{6,15},{7,14},{8,1},{9,0},... | collective-permute-start | bytes 24584 | tf_op jit(solution)/shard_map/ppermute | solution.py:610
  40.9 2.6 %collective-permute-start.7 = (f32[16,128]{1,0:T(8,128)S(1)}, f32[16,128]{1,0:T(8,128)S(1)}, u32[]{:S(2)}, u32[]{:S(2)}) collective-permute-start(f32[16,128]{1,0:T(8,128)S(1)} %add_add_fusion.1), channel_id=1, source_target_pairs={{0,17},{1,16},{2,19},{3,18},{4,21},{5,20},{6,23},{7,22},{8,25},{9,... | collective-permute-start | bytes 24584 | tf_op jit(solution)/shard_map/ppermute | solution.py:610
  43.6 0.0 collective-permute-start.8
  43.6 0.0 collective-permute-done.6
  43.6 1.4 %collective-permute-done.7 = f32[16,128]{1,0:T(8,128)S(1)} collective-permute-done((f32[16,128]{1,0:T(8,128)S(1)}, f32[16,128]{1,0:T(8,128)S(1)}, u32[]{:S(2)}, u32[]{:S(2)}) %collective-permute-start.7) | collective-permute-done | bytes 8224 | tf_op jit(solution)/shard_map/ppermute | solution.py:610
  44.9 3.5 %collective-permute-done.8 = f32[16,128]{1,0:T(8,128)S(1)} collective-permute-done((f32[16,128]{1,0:T(8,128)S(1)}, f32[16,128]{1,0:T(8,128)S(1)}, u32[]{:S(2)}, u32[]{:S(2)}) %collective-permute-start.8) | collective-permute-done | bytes 8224 | tf_op jit(solution)/shard_map/ppermute | solution.py:610
  48.4 1.2 %collective-permute-start.9 = (f32[16,128]{1,0:T(8,128)S(1)}, f32[16,128]{1,0:T(8,128)S(1)}, u32[]{:S(2)}, u32[]{:S(2)}) collective-permute-start(f32[16,128]{1,0:T(8,128)S(1)} %add_add_fusion.refs_0_), channel_id=1, source_target_pairs={{0,5},{1,4},{2,7},{3,6},{4,1},{5,0},{6,3},{7,2},{8,13},{9,12},{10,... | collective-permute-start | bytes 24584 | tf_op jit(solution)/shard_map/ppermute | solution.py:610
  49.7 1.8 %collective-permute-done.9.refs_1_ = f32[16,128]{1,0:T(8,128)S(1)} collective-permute-done((f32[16,128]{1,0:T(8,128)S(1)}, f32[16,128]{1,0:T(8,128)S(1)}, u32[]{:S(2)}, u32[]{:S(2)}) %collective-permute-start.9) | collective-permute-done | bytes 8224 | tf_op jit(solution)/shard_map/ppermute | solution.py:610
  51.5 0.8 %last.1 = (f32[64,64]{1,0:T(8,128)}, f32[1,8]{1,0:T(1,128)}, f32[1,127]{1,0:T(1,128)}, f32[1,1]{1,0:T(1,128)}) custom-call(f32[16,128]{1,0:T(8,128)S(1)} %add_add_fusion.refs_0_, f32[16,128]{1,0:T(8,128)S(1)} %collective-permute-done.9.refs_1_), custom_call_target="tpu_custom_call" | custom-call | tf_op jit(solution)/shard_map/last/pallas_call | solution.py:711
  (2 shorter events, 0.0 us)
Async XLA Ops:
  12.2 6.5 %collective-permute-start = (f32[64,256]{1,0:T(8,128)S(1)}, f32[64,256]{1,0:T(8,128)S(1)}, u32[]{:S(2)}, u32[]{:S(2)}) collective-permute-start(f32[64,256]{1,0:T(8,128)S(1)} %get-tuple-element.26.refs_0_), channel_id=1, source_target_pairs={{0,1},{1,0},{2,3},{3,2},{4,5},{5,4},{6,7},{7,6},{8,9},{9,8},{10,11... | collective-permute-start | bytes 196616 | tf_op jit(solution)/shard_map/ppermute | solution.py:587
  12.8 6.0 %collective-permute-start.1 = (f32[64,256]{1,0:T(8,128)S(1)}, f32[64,256]{1,0:T(8,128)S(1)}, u32[]{:S(2)}, u32[]{:S(2)}) collective-permute-start(f32[64,256]{1,0:T(8,128)S(1)} %get-tuple-element.26.refs_0_), channel_id=1, source_target_pairs={{0,2},{1,3},{2,0},{3,1},{4,6},{5,7},{6,4},{7,5},{8,10},{9,11},{10,... | collective-permute-start | bytes 196616 | tf_op jit(solution)/shard_map/ppermute | solution.py:587
  15.3 4.0 %collective-permute-start.2 = (f32[64,256]{1,0:T(8,128)S(1)}, f32[64,256]{1,0:T(8,128)S(1)}, u32[]{:S(2)}, u32[]{:S(2)}) collective-permute-start(f32[64,256]{1,0:T(8,128)S(1)} %get-tuple-element.26.refs_0_), channel_id=1, source_target_pairs={{0,3},{1,2},{2,1},{3,0},{4,7},{5,6},{6,5},{7,4},{8,11},{9,10},{10,... | collective-permute-start | bytes 196616 | tf_op jit(solution)/shard_map/ppermute | solution.py:587
  34.9 1.9 %collective-permute-start.3 = (f32[16,128]{1,0:T(8,128)S(1)}, f32[16,128]{1,0:T(8,128)S(1)}, u32[]{:S(2)}, u32[]{:S(2)}) collective-permute-start(f32[16,128]{1,0:T(8,128)S(1)} %down.1), channel_id=1, source_target_pairs={{0,1},{1,0},{2,3},{3,2},{4,5},{5,4},{6,7},{7,6},{8,9},{9,8},{10,11... | collective-permute-start | bytes 24584 | tf_op jit(solution)/shard_map/ppermute | solution.py:610
  35.1 3.7 %collective-permute-start.4 = (f32[16,128]{1,0:T(8,128)S(1)}, f32[16,128]{1,0:T(8,128)S(1)}, u32[]{:S(2)}, u32[]{:S(2)}) collective-permute-start(f32[16,128]{1,0:T(8,128)S(1)} %down.1), channel_id=1, source_target_pairs={{0,2},{1,3},{2,0},{3,1},{4,6},{5,7},{6,4},{7,5},{8,10},{9,11},{10,... | collective-permute-start | bytes 24584 | tf_op jit(solution)/shard_map/ppermute | solution.py:610
  36.5 3.1 %collective-permute-start.5 = (f32[16,128]{1,0:T(8,128)S(1)}, f32[16,128]{1,0:T(8,128)S(1)}, u32[]{:S(2)}, u32[]{:S(2)}) collective-permute-start(f32[16,128]{1,0:T(8,128)S(1)} %down.1), channel_id=1, source_target_pairs={{0,3},{1,2},{2,1},{3,0},{4,7},{5,6},{6,5},{7,4},{8,11},{9,10},{10,... | collective-permute-start | bytes 24584 | tf_op jit(solution)/shard_map/ppermute | solution.py:610
  39.6 3.9 %collective-permute-start.6 = (f32[16,128]{1,0:T(8,128)S(1)}, f32[16,128]{1,0:T(8,128)S(1)}, u32[]{:S(2)}, u32[]{:S(2)}) collective-permute-start(f32[16,128]{1,0:T(8,128)S(1)} %add_add_fusion.1), channel_id=1, source_target_pairs={{0,9},{1,8},{2,11},{3,10},{4,13},{5,12},{6,15},{7,14},{8,1},{9,0},... | collective-permute-start | bytes 24584 | tf_op jit(solution)/shard_map/ppermute | solution.py:610
  40.9 4.0 %collective-permute-start.7 = (f32[16,128]{1,0:T(8,128)S(1)}, f32[16,128]{1,0:T(8,128)S(1)}, u32[]{:S(2)}, u32[]{:S(2)}) collective-permute-start(f32[16,128]{1,0:T(8,128)S(1)} %add_add_fusion.1), channel_id=1, source_target_pairs={{0,17},{1,16},{2,19},{3,18},{4,21},{5,20},{6,23},{7,22},{8,25},{9,... | collective-permute-start | bytes 24584 | tf_op jit(solution)/shard_map/ppermute | solution.py:610
  43.6 4.9 %collective-permute-start.8 = (f32[16,128]{1,0:T(8,128)S(1)}, f32[16,128]{1,0:T(8,128)S(1)}, u32[]{:S(2)}, u32[]{:S(2)}) collective-permute-start(f32[16,128]{1,0:T(8,128)S(1)} %add_add_fusion.1), channel_id=1, source_target_pairs={{0,25},{1,24},{2,27},{3,26},{4,29},{5,28},{6,31},{7,30},{8,17},{9,... | collective-permute-start | bytes 24584 | tf_op jit(solution)/shard_map/ppermute | solution.py:610
  48.4 3.1 %collective-permute-start.9 = (f32[16,128]{1,0:T(8,128)S(1)}, f32[16,128]{1,0:T(8,128)S(1)}, u32[]{:S(2)}, u32[]{:S(2)}) collective-permute-start(f32[16,128]{1,0:T(8,128)S(1)} %add_add_fusion.refs_0_), channel_id=1, source_target_pairs={{0,5},{1,4},{2,7},{3,6},{4,1},{5,0},{6,3},{7,2},{8,13},{9,12},{10,... | collective-permute-start | bytes 24584 | tf_op jit(solution)/shard_map/ppermute | solution.py:610

commit v14 on v13

--- a/solution.py
+++ b/solution.py
@@ -437,12 +437,12 @@
             a_high_ref[p - 32] = high
             a_low_ref[p - 32] = low
 
-    def adjoint(step):
-        held = [count_ref[step * 16 + j] for j in range(16)]
+    def adjoint(first, width):
+        held = [count_ref[first + j] for j in range(width)]
         for level in range(3, -1, -1):
-            for j in range(16):
+            for j in range(width):
                 high, low = split(held[j])
-                e_high, e_low = chain_ref[level, 0, step * 16 + j], chain_ref[level, 1, step * 16 + j]
+                e_high, e_low = chain_ref[level, 0, first + j], chain_ref[level, 1, first + j]
                 left = jnp.concatenate([
                     jnp.concatenate([high, e_high], axis=1),
                     jnp.concatenate([low, e_low], axis=1),
@@ -455,8 +455,8 @@
                 held[j] = 2.0 * held[j] + (
                     four[0:64, 0:128] + four[0:64, 128:256] + four[64:128, 0:128]
                 )
-        for j in range(16):
-            back_ref[pl.ds(step * 16 + j, 64, stride=STRIDE), :] = held[j]
+        for j in range(width):
+            back_ref[pl.ds(first + j, 64, stride=STRIDE), :] = held[j]
 
     def outer(r):
         down = descend(r)
@@ -468,13 +468,13 @@
 
     for r in range(63, 47, -1):
         inner(r)
-    for r in range(47, 39, -1):
-        outer(r)
-    adjoint(3)
-    for r in range(39, 31, -1):
-        outer(r)
-    for step in (1, 2, 0):
-        adjoint(step)
+    adjoint(56, 8)
+    for block, first in enumerate((48, 24, 40, 16)):
+        for r in range(47 - 4 * block, 43 - 4 * block, -1):
+            outer(r)
+        adjoint(first, 8)
+    adjoint(0, 16)
+    adjoint(32, 8)
 
     left = four_left(turned_ref[...])
 

time: 52.6 us -> 52.6 us (level)
  no operation moved by 1% of the time
where the time goes in v14:
time: 52.6 us; the launch traced here: 52.3 us
  Pallas kernels  31.3 us (60%)
  starting transfers between devices  10.2 us (19%)
  waiting for transfers between devices  10.2 us (19%)
  between operations  0.67 us (1%)
    pallas_call x1, Pallas kernels, body(): pl.pallas_call(functools.partial(down_kernel, total_sites, members), out_...  15.5 us
    pallas_call x1, Pallas kernels, body(): pl.pallas_call(up_kernel, out_shape=[shape((64, sites), F32), held((4, 2,...  11.6 us
    ppermute x7, waiting for transfers between devices, sum_stages(): lax.ppermute(x, ('site', 'branch'), [(i, i ^ step * start + flip) for i i...  9.54 us
    ppermute x7, starting transfers between devices, sum_stages(): lax.ppermute(x, ('site', 'branch'), [(i, i ^ step * start + flip) for i i...  7.04 us
    pallas_call x1, Pallas kernels, body(): pl.pallas_call(side_kernel, out_shape=[held((PAIRS * 64, 128), F32), held...  3.34 us
    ppermute x3, starting transfers between devices, partners(): lax.ppermute(x, axis, [(i, i ^ step * start) for i in range(size)])  3.15 us
  transfers between devices with their start and end apart: 10, of which 6 were waited for; matrix products, arithmetic and copies ran while one was open for 0% of the time, Pallas kernels for 6%

profile of v14, /device:TPU:0, one launch (start us, length us, event | category | flops | bytes accessed | tf_op | source)
XLA Modules:
  0.0 52.3 jit_solution(16511907235678138002)
XLA Ops:
  0.6 11.6 %up.1 = (f32[64,256]{1,0:T(8,128)S(1)}, bf16[4,2,64,64,128]{4,3,2,1,0:T(8,128)(2,1)S(1)}, f32[32,64,128]{2,1,0:T(8,128)S(1)}, f32[4,4,64,128]{3,2,1,0:T(8,128)S(...) custom-call(s32[256,256]{1,0:T(8,128)} %states_ref.1, ...), custom_call_target="tpu_custom_call" | custom-call | tf_op jit(solution)/shard_map/up/pallas_call | solution.py:644
  12.2 0.5 collective-permute-start
  12.8 2.6 %collective-permute-start.1 = (f32[64,256]{1,0:T(8,128)S(1)}, f32[64,256]{1,0:T(8,128)S(1)}, u32[]{:S(2)}, u32[]{:S(2)}) collective-permute-start(f32[64,256]{1,0:T(8,128)S(1)} %get-tuple-element.26.refs_0_), channel_id=1, source_target_pairs={{0,2},{1,3},{2,0},{3,1},{4,6},{5,7},{6,4},{7,5},{8,10},{9,11},{10,... | collective-permute-start | bytes 196616 | tf_op jit(solution)/shard_map/ppermute | solution.py:587
  15.3 0.1 collective-permute-start.2
  15.4 3.3 %side.1 = (f32[4096,128]{1,0:T(8,128)S(1)}, bf16[64,64,256]{2,1,0:T(8,128)(2,1)S(1)}, f32[128,128]{1,0:T(8,128)S(1)}, f32[32,128,256]{2,1,0:T(8,128)S(1)}, f32[4,3,64,128]{3,2,1,0:T(8,128)S(1)}) custom-call(f32[4160,128]{1,0:T(8,128)S(1)} %get-tuple-element.27.dup_ref, f32[32,64,128]{2,1,0:T(8,128)S(1)} %get-tuple-element.28.last_ref, f32[1,127]{1,0:T(1,128)} %bitcast.8, ...), custom_call_target="tpu_custom_call" | custom-call | tf_op jit(solution)/shard_map/side/pallas_call | solution.py:677
  18.7 0.0 collective-permute-done.refs_1_
  18.7 0.0 collective-permute-done.1.refs_2_
  18.8 0.6 %collective-permute-done.2.refs_3_ = f32[64,256]{1,0:T(8,128)S(1)} collective-permute-done((f32[64,256]{1,0:T(8,128)S(1)}, f32[64,256]{1,0:T(8,128)S(1)}, u32[]{:S(2)}, u32[]{:S(2)}) %collective-permute-start.2) | collective-permute-done | bytes 65568 | tf_op jit(solution)/shard_map/ppermute | solution.py:587
  19.4 15.5 %down.1 = f32[16,128]{1,0:T(8,128)S(1)} custom-call(f32[64,256]{1,0:T(8,128)S(1)} %get-tuple-element.26.refs_0_, f32[64,256]{1,0:T(8,128)S(1)} %collective-permute-done.refs_1_, f32[64,256]{1,0:T(8,128)S(1)} %collective-permute-done.1.refs_2_, f32[64,256]{1,0:T(8,128)S(1)} %collective-permute-done.2.refs_3_, ...), custom_call_target="tpu_custom_call" | custom-call | tf_op jit(solution)/shard_map/down/pallas_call | solution.py:691
  34.9 0.2 collective-permute-start.3
  35.1 1.5 %collective-permute-start.4 = (f32[16,128]{1,0:T(8,128)S(1)}, f32[16,128]{1,0:T(8,128)S(1)}, u32[]{:S(2)}, u32[]{:S(2)}) collective-permute-start(f32[16,128]{1,0:T(8,128)S(1)} %down.1), channel_id=1, source_target_pairs={{0,2},{1,3},{2,0},{3,1},{4,6},{5,7},{6,4},{7,5},{8,10},{9,11},{10,... | collective-permute-start | bytes 24584 | tf_op jit(solution)/shard_map/ppermute | solution.py:610
  36.5 0.2 collective-permute-start.5
  36.8 0.0 collective-permute-done.3
  36.8 2.0 %collective-permute-done.4 = f32[16,128]{1,0:T(8,128)S(1)} collective-permute-done((f32[16,128]{1,0:T(8,128)S(1)}, f32[16,128]{1,0:T(8,128)S(1)}, u32[]{:S(2)}, u32[]{:S(2)}) %collective-permute-start.4) | collective-permute-done | bytes 8224 | tf_op jit(solution)/shard_map/ppermute | solution.py:610
  38.7 0.9 %collective-permute-done.5 = f32[16,128]{1,0:T(8,128)S(1)} collective-permute-done((f32[16,128]{1,0:T(8,128)S(1)}, f32[16,128]{1,0:T(8,128)S(1)}, u32[]{:S(2)}, u32[]{:S(2)}) %collective-permute-start.5) | collective-permute-done | bytes 8224 | tf_op jit(solution)/shard_map/ppermute | solution.py:610
  39.6 1.3 %collective-permute-start.6 = (f32[16,128]{1,0:T(8,128)S(1)}, f32[16,128]{1,0:T(8,128)S(1)}, u32[]{:S(2)}, u32[]{:S(2)}) collective-permute-start(f32[16,128]{1,0:T(8,128)S(1)} %add_add_fusion.1), channel_id=1, source_target_pairs={{0,9},{1,8},{2,11},{3,10},{4,13},{5,12},{6,15},{7,14},{8,1},{9,0},... | collective-permute-start | bytes 24584 | tf_op jit(solution)/shard_map/ppermute | solution.py:610
  40.9 2.6 %collective-permute-start.7 = (f32[16,128]{1,0:T(8,128)S(1)}, f32[16,128]{1,0:T(8,128)S(1)}, u32[]{:S(2)}, u32[]{:S(2)}) collective-permute-start(f32[16,128]{1,0:T(8,128)S(1)} %add_add_fusion.1), channel_id=1, source_target_pairs={{0,17},{1,16},{2,19},{3,18},{4,21},{5,20},{6,23},{7,22},{8,25},{9,... | collective-permute-start | bytes 24584 | tf_op jit(solution)/shard_map/ppermute | solution.py:610
  43.5 0.0 collective-permute-start.8
  43.5 0.0 collective-permute-done.6
  43.5 1.4 %collective-permute-done.7 = f32[16,128]{1,0:T(8,128)S(1)} collective-permute-done((f32[16,128]{1,0:T(8,128)S(1)}, f32[16,128]{1,0:T(8,128)S(1)}, u32[]{:S(2)}, u32[]{:S(2)}) %collective-permute-start.7) | collective-permute-done | bytes 8224 | tf_op jit(solution)/shard_map/ppermute | solution.py:610
  44.9 3.5 %collective-permute-done.8 = f32[16,128]{1,0:T(8,128)S(1)} collective-permute-done((f32[16,128]{1,0:T(8,128)S(1)}, f32[16,128]{1,0:T(8,128)S(1)}, u32[]{:S(2)}, u32[]{:S(2)}) %collective-permute-start.8) | collective-permute-done | bytes 8224 | tf_op jit(solution)/shard_map/ppermute | solution.py:610
  48.4 1.2 %collective-permute-start.9 = (f32[16,128]{1,0:T(8,128)S(1)}, f32[16,128]{1,0:T(8,128)S(1)}, u32[]{:S(2)}, u32[]{:S(2)}) collective-permute-start(f32[16,128]{1,0:T(8,128)S(1)} %add_add_fusion.refs_0_), channel_id=1, source_target_pairs={{0,5},{1,4},{2,7},{3,6},{4,1},{5,0},{6,3},{7,2},{8,13},{9,12},{10,... | collective-permute-start | bytes 24584 | tf_op jit(solution)/shard_map/ppermute | solution.py:610
  49.7 1.8 %collective-permute-done.9.refs_1_ = f32[16,128]{1,0:T(8,128)S(1)} collective-permute-done((f32[16,128]{1,0:T(8,128)S(1)}, f32[16,128]{1,0:T(8,128)S(1)}, u32[]{:S(2)}, u32[]{:S(2)}) %collective-permute-start.9) | collective-permute-done | bytes 8224 | tf_op jit(solution)/shard_map/ppermute | solution.py:610
  51.5 0.8 %last.1 = (f32[64,64]{1,0:T(8,128)}, f32[1,8]{1,0:T(1,128)}, f32[1,127]{1,0:T(1,128)}, f32[1,1]{1,0:T(1,128)}) custom-call(f32[16,128]{1,0:T(8,128)S(1)} %add_add_fusion.refs_0_, f32[16,128]{1,0:T(8,128)S(1)} %collective-permute-done.9.refs_1_), custom_call_target="tpu_custom_call" | custom-call | tf_op jit(solution)/shard_map/last/pallas_call | solution.py:711
  (2 shorter events, 0.0 us)
Async XLA Ops:
  12.2 6.5 %collective-permute-start = (f32[64,256]{1,0:T(8,128)S(1)}, f32[64,256]{1,0:T(8,128)S(1)}, u32[]{:S(2)}, u32[]{:S(2)}) collective-permute-start(f32[64,256]{1,0:T(8,128)S(1)} %get-tuple-element.26.refs_0_), channel_id=1, source_target_pairs={{0,1},{1,0},{2,3},{3,2},{4,5},{5,4},{6,7},{7,6},{8,9},{9,8},{10,11... | collective-permute-start | bytes 196616 | tf_op jit(solution)/shard_map/ppermute | solution.py:587
  12.8 6.0 %collective-permute-start.1 = (f32[64,256]{1,0:T(8,128)S(1)}, f32[64,256]{1,0:T(8,128)S(1)}, u32[]{:S(2)}, u32[]{:S(2)}) collective-permute-start(f32[64,256]{1,0:T(8,128)S(1)} %get-tuple-element.26.refs_0_), channel_id=1, source_target_pairs={{0,2},{1,3},{2,0},{3,1},{4,6},{5,7},{6,4},{7,5},{8,10},{9,11},{10,... | collective-permute-start | bytes 196616 | tf_op jit(solution)/shard_map/ppermute | solution.py:587
  15.3 4.0 %collective-permute-start.2 = (f32[64,256]{1,0:T(8,128)S(1)}, f32[64,256]{1,0:T(8,128)S(1)}, u32[]{:S(2)}, u32[]{:S(2)}) collective-permute-start(f32[64,256]{1,0:T(8,128)S(1)} %get-tuple-element.26.refs_0_), channel_id=1, source_target_pairs={{0,3},{1,2},{2,1},{3,0},{4,7},{5,6},{6,5},{7,4},{8,11},{9,10},{10,... | collective-permute-start | bytes 196616 | tf_op jit(solution)/shard_map/ppermute | solution.py:587
  34.9 1.9 %collective-permute-start.3 = (f32[16,128]{1,0:T(8,128)S(1)}, f32[16,128]{1,0:T(8,128)S(1)}, u32[]{:S(2)}, u32[]{:S(2)}) collective-permute-start(f32[16,128]{1,0:T(8,128)S(1)} %down.1), channel_id=1, source_target_pairs={{0,1},{1,0},{2,3},{3,2},{4,5},{5,4},{6,7},{7,6},{8,9},{9,8},{10,11... | collective-permute-start | bytes 24584 | tf_op jit(solution)/shard_map/ppermute | solution.py:610
  35.1 3.7 %collective-permute-start.4 = (f32[16,128]{1,0:T(8,128)S(1)}, f32[16,128]{1,0:T(8,128)S(1)}, u32[]{:S(2)}, u32[]{:S(2)}) collective-permute-start(f32[16,128]{1,0:T(8,128)S(1)} %down.1), channel_id=1, source_target_pairs={{0,2},{1,3},{2,0},{3,1},{4,6},{5,7},{6,4},{7,5},{8,10},{9,11},{10,... | collective-permute-start | bytes 24584 | tf_op jit(solution)/shard_map/ppermute | solution.py:610
  36.5 3.1 %collective-permute-start.5 = (f32[16,128]{1,0:T(8,128)S(1)}, f32[16,128]{1,0:T(8,128)S(1)}, u32[]{:S(2)}, u32[]{:S(2)}) collective-permute-start(f32[16,128]{1,0:T(8,128)S(1)} %down.1), channel_id=1, source_target_pairs={{0,3},{1,2},{2,1},{3,0},{4,7},{5,6},{6,5},{7,4},{8,11},{9,10},{10,... | collective-permute-start | bytes 24584 | tf_op jit(solution)/shard_map/ppermute | solution.py:610
  39.6 3.9 %collective-permute-start.6 = (f32[16,128]{1,0:T(8,128)S(1)}, f32[16,128]{1,0:T(8,128)S(1)}, u32[]{:S(2)}, u32[]{:S(2)}) collective-permute-start(f32[16,128]{1,0:T(8,128)S(1)} %add_add_fusion.1), channel_id=1, source_target_pairs={{0,9},{1,8},{2,11},{3,10},{4,13},{5,12},{6,15},{7,14},{8,1},{9,0},... | collective-permute-start | bytes 24584 | tf_op jit(solution)/shard_map/ppermute | solution.py:610
  40.9 4.0 %collective-permute-start.7 = (f32[16,128]{1,0:T(8,128)S(1)}, f32[16,128]{1,0:T(8,128)S(1)}, u32[]{:S(2)}, u32[]{:S(2)}) collective-permute-start(f32[16,128]{1,0:T(8,128)S(1)} %add_add_fusion.1), channel_id=1, source_target_pairs={{0,17},{1,16},{2,19},{3,18},{4,21},{5,20},{6,23},{7,22},{8,25},{9,... | collective-permute-start | bytes 24584 | tf_op jit(solution)/shard_map/ppermute | solution.py:610
  43.5 4.9 %collective-permute-start.8 = (f32[16,128]{1,0:T(8,128)S(1)}, f32[16,128]{1,0:T(8,128)S(1)}, u32[]{:S(2)}, u32[]{:S(2)}) collective-permute-start(f32[16,128]{1,0:T(8,128)S(1)} %add_add_fusion.1), channel_id=1, source_target_pairs={{0,25},{1,24},{2,27},{3,26},{4,29},{5,28},{6,31},{7,30},{8,17},{9,... | collective-permute-start | bytes 24584 | tf_op jit(solution)/shard_map/ppermute | solution.py:610
  48.4 3.1 %collective-permute-start.9 = (f32[16,128]{1,0:T(8,128)S(1)}, f32[16,128]{1,0:T(8,128)S(1)}, u32[]{:S(2)}, u32[]{:S(2)}) collective-permute-start(f32[16,128]{1,0:T(8,128)S(1)} %add_add_fusion.refs_0_), channel_id=1, source_target_pairs={{0,5},{1,4},{2,7},{3,6},{4,1},{5,0},{6,3},{7,2},{8,13},{9,12},{10,... | collective-permute-start | bytes 24584 | tf_op jit(solution)/shard_map/ppermute | solution.py:610
